TPU v7x, 32 devices: a whole 2x2x4 slice. The times are simulated.
32 devices in a mesh: groups: 2 (over x), seq: 16 (over z, y, core).
Axes of the slice: x: 2, y: 2, z: 4, core: 2. Of those that a mesh axis runs over, the one named last changes fastest.
Arguments:
- audio_qkv: bfloat16 [2048, 3, 16, 128], P(('groups', 'seq')), parts along dimension 0, may hold values from -8 to 8
- video_q: bfloat16 [16384, 16, 128], P(('groups', 'seq')), parts along dimension 0, may hold values from -8 to 8
- pairs: int32 [128, 4], P(('groups', 'seq')), parts along dimension 0, may hold values from 0 to 31, as said below
- counts: int32 [128], P(('groups', 'seq')), parts along dimension 0, may hold values from 1 to 4
Outputs:
- audio_attn: bfloat16 [2048, 16, 128], P(('groups', 'seq')), parts along dimension 0
- video_cross: bfloat16 [16384, 16, 128], P(('groups', 'seq')), parts along dimension 0
There are 2 independent parts, one for each index of `groups`. A program takes and returns all parts, laid end to end along the dimension named above; each array names one. Nothing has to cross between parts.
Inputs may be any that keep to these rules, and one draw needn't show every extreme that they name: `pairs`: entry 0 of row b is c = (b * 32) // 64; every entry is c plus an offset within -2 .. 2, clipped to the audio blocks; the offsets of entries 1 .. 3 of a row are distinct and nonzero.
All inputs are finite; a program needn't handle non-finite values.
Results may differ from a plain program's by a relative error of at most 0.0034.
Values may be sent and summed in bfloat16 or wider, within the bound.
No kernel may reach another device: no remote copies, remote signals or barrier semaphores. Data moves between devices by JAX's collectives and lax.ppermute only.
A program may use at most 64 MiB of HBM per device.

v0:
```python
import jax
import jax.numpy as jnp
from jax import lax
from jax.sharding import PartitionSpec as P

ABLK = 32
VBLK = 128


def with_halo(cells, sides, width):
    for axis, dim in sides:
        count = lax.axis_size(axis)
        ends = count - 1
        head = lax.slice_in_dim(cells, 0, width, axis=dim)
        tail = lax.slice_in_dim(cells, cells.shape[dim] - width, cells.shape[dim], axis=dim)
        cells = jnp.concatenate(
            [
                lax.ppermute(tail, axis, [(i, (i + 1) % count) for i in range(ends)]),
                cells,
                lax.ppermute(head, axis, [((i + 1) % count, i) for i in range(ends)]),
            ],
            axis=dim,
        )
    return cells


def block_count(total, most):
    count = max(1, total // most)
    while total % count:
        count += 1
    return count


def attend(queries, key_rows, value_rows, score_scale):
    query_total, head_size = queries.shape
    key_total = key_rows.shape[0]
    query_blocks = block_count(query_total, 512)
    key_blocks = block_count(key_total, 2048)
    key_tiles = key_rows.reshape(key_blocks, -1, head_size)
    value_tiles = value_rows.reshape(key_blocks, -1, head_size)

    def one_block(query_block):
        block_rows = query_block.shape[0]

        def advance(state, tile_pair):
            row_top, row_total, summed = state
            scores = (
                jnp.einsum(
                    "qd,kd->qk", query_block, tile_pair[0], preferred_element_type=jnp.float32
                )
                * score_scale
            )
            new_top = jnp.maximum(row_top, jnp.max(scores, axis=1))
            rescale = jnp.exp(row_top - new_top)
            weights = jnp.exp(scores - new_top[:, None])
            row_total = row_total * rescale + jnp.sum(weights, axis=1)
            summed = summed * rescale[:, None] + jnp.dot(
                weights.astype(jnp.bfloat16), tile_pair[1], preferred_element_type=jnp.float32
            )
            return ((new_top, row_total, summed), None)

        start_state = (
            jnp.full((block_rows,), -1e30, jnp.float32),
            jnp.zeros((block_rows,), jnp.float32),
            jnp.zeros((block_rows, head_size), jnp.float32),
        )
        finished, unused = lax.scan(advance, start_state, (key_tiles, value_tiles))
        return finished[2] / finished[1][:, None]

    gathered_out = lax.map(one_block, queries.reshape(query_blocks, -1, head_size))
    return gathered_out.reshape(query_total, head_size)


def local(audio_qkv, video_q, pairs, counts):
    devices = lax.axis_size("seq")
    own_index = lax.axis_index("seq")
    audio_rows, head_count, head_size = (audio_qkv.shape[0], audio_qkv.shape[2], audio_qkv.shape[3])
    band_count = devices // head_count
    band_rows = audio_rows // band_count
    score_scale = head_size ** (-0.5)
    arranged = (
        audio_qkv.reshape(band_count, band_rows, 3, head_count, head_size)
        .transpose(3, 0, 1, 2, 4)
        .reshape(devices, band_rows, 3, head_size)
    )
    queries = arranged[:, :, 0]
    spread_kv = jnp.broadcast_to(
        audio_qkv[:, 1:].transpose(2, 0, 1, 3)[:, None],
        (head_count, band_count, audio_rows, 2, head_size),
    ).reshape(devices, audio_rows, 2, head_size)
    query_rows, key_rows = (
        lax.all_to_all(queries, "seq", split_axis=0, concat_axis=1, tiled=True),
        lax.all_to_all(spread_kv, "seq", split_axis=0, concat_axis=1, tiled=True),
    )
    query_rows = query_rows[0]
    key_rows = key_rows[0]
    head_out = attend(query_rows, key_rows[:, 0], key_rows[:, 1], score_scale).astype(jnp.bfloat16)
    returned = lax.all_to_all(head_out[None], "seq", split_axis=1, concat_axis=0, tiled=True)
    audio_attn = (
        returned.reshape(head_count, band_count, band_rows, head_size)
        .transpose(1, 2, 0, 3)
        .reshape(audio_rows, head_count, head_size)
    )
    slot_count = pairs.shape[1]
    extended = with_halo(audio_qkv[:, 1:], (("seq", 0),), audio_rows)
    video_rows = video_q.shape[0]
    video_blocks = video_rows // VBLK
    starts = pairs * ABLK - own_index * audio_rows + audio_rows

    def take_block(start_row):
        return lax.dynamic_slice_in_dim(extended, start_row, ABLK, 0)

    taken = jax.vmap(jax.vmap(take_block))(starts)
    cross_keys = taken[:, :, :, 0].reshape(video_blocks, slot_count * ABLK, head_count, head_size)
    cross_values = taken[:, :, :, 1].reshape(video_blocks, slot_count * ABLK, head_count, head_size)
    video_tiles = video_q.reshape(video_blocks, VBLK, head_count, head_size)
    scores = (
        jnp.einsum("mqhd,mkhd->mhqk", video_tiles, cross_keys, preferred_element_type=jnp.float32)
        * score_scale
    )
    slot_live = (jnp.arange(slot_count * ABLK) // ABLK)[None, :] < counts[:, None]
    scores = jnp.where(slot_live[:, None, None, :], scores, -1e30)
    row_top = jnp.max(scores, axis=3)
    weights = jnp.exp(scores - row_top[..., None])
    row_total = jnp.sum(weights, axis=3)
    summed = jnp.einsum(
        "mhqk,mkhd->mqhd",
        weights.astype(jnp.bfloat16),
        cross_values,
        preferred_element_type=jnp.float32,
    )
    video_cross = (
        (summed / row_total.transpose(0, 2, 1)[..., None])
        .reshape(video_rows, head_count, head_size)
        .astype(jnp.bfloat16)
    )
    return (audio_attn, video_cross)


def solution(mesh):
    in_specs = (
        P(("groups", "seq"), None, None, None),
        P(("groups", "seq"), None, None),
        P(("groups", "seq"), None),
        P(("groups", "seq")),
    )
    out_specs = (P(("groups", "seq"), None, None), P(("groups", "seq"), None, None))
    return jax.shard_map(local, mesh=mesh, in_specs=in_specs, out_specs=out_specs, check_vma=False)
```

profile of v0, /device:TPU:0, one launch (start us, length us, event | category | flops | bytes accessed | tf_op | source)
XLA Modules:
  0.0 77.6 jit_solution(11424782735116689404)
XLA Ops:
  0.6 0.0 copy-start
  0.6 0.0 copy-start.1
  0.7 2.1 %fusion.32 = (bf16[64,2,16,128]{3,2,1,0:T(8,128)(2,1)}, bf16[16,64,2,128]{3,0,2,1:T(8,128)(2,1)S(1)}) fusion(bf16[64,3,16,128]{3,2,1,0:T(8,128)(2,1)} %param.6), kind=kLoop, calls=%fused_computation.52 | loop fusion | bytes 1572864 | tf_op jit(solution)/shard_map/slice | solution.py:88
  2.8 0.0 copy-start.2
  2.8 1.4 %collective-permute-start.1 = (bf16[64,2,16,128]{3,2,1,0:T(8,128)(2,1)}, bf16[64,2,16,128]{3,2,1,0:T(8,128)(2,1)}, u32[]{:S(2)}, u32[]{:S(2)}) collective-permute-start(bf16[64,2,16,128]{3,2,1,0:T(8,128)(2,1)} %get-tuple-element.73), channel_id=1, source_target_pairs={{1,0},{2,1},{3,2},{4,3},{5,4},{6,5},{7,6},{8,7},{9,8},{10,9},{11,1... | collective-permute-start | bytes 1572872 | tf_op jit(solution)/shard_map/ppermute | solution.py:20
  4.2 3.9 %collective-permute-start = (bf16[64,2,16,128]{3,2,1,0:T(8,128)(2,1)}, bf16[64,2,16,128]{3,2,1,0:T(8,128)(2,1)}, u32[]{:S(2)}, u32[]{:S(2)}) collective-permute-start(bf16[64,2,16,128]{3,2,1,0:T(8,128)(2,1)} %get-tuple-element.73), channel_id=1, source_target_pairs={{0,1},{1,2},{2,3},{3,4},{4,5},{5,6},{6,7},{7,8},{8,9},{9,10},{10,1... | collective-permute-start | bytes 1572872 | tf_op jit(solution)/shard_map/ppermute | solution.py:18
  8.1 0.0 copy-start.3
  8.1 1.3 %copy.29 = bf16[16,64,2,128]{3,2,1,0:T(2,128)(2,1)} copy(bf16[16,64,2,128]{3,0,2,1:T(8,128)(2,1)S(1)} %get-tuple-element.74) | data formatting | bytes 1048576 | tf_op jit(solution)/shard_map/transpose | solution.py:88
  9.4 7.4 %all-to-all-start.1 = ((bf16[16,64,2,128]{3,2,1,0:T(2,128)(2,1)}), bf16[16,64,2,128]{3,2,1,0:T(2,128)(2,1)S(1)}, u32[]{:S(2)}, u32[]{:S(2)}) async-start(bf16[16,64,2,128]{3,2,1,0:T(2,128)(2,1)} %copy.29), calls=%async_computation.1 | async-start | bytes 1048576 | tf_op jit(solution)/shard_map/all_to_all | solution.py:93
  16.7 0.0 copy-done.1
  16.8 1.1 %copy.48 = bf16[64,3,16,128]{3,0,2,1:T(8,128)(2,1)} copy(bf16[64,3,16,128]{3,2,1,0:T(8,128)(2,1)S(1)} %copy-done.1) | data formatting | bytes 1572864 | tf_op args[0]
  17.8 0.0 copy-done.2
  17.9 1.7 %slice_bitcast_fusion.2 = bf16[16,64,128]{2,1,0:T(8,128)(2,1)} fusion(bf16[16,64,3,128]{3,1,0,2:T(8,128)(2,1)} %bitcast.83), kind=kLoop, calls=%fused_computation.39 | loop fusion | bytes 524288 | tf_op jit(solution)/shard_map/squeeze | solution.py:86
  19.5 0.0 copy-done.3
  19.5 0.1 broadcast_compare_fusion
  19.6 0.1 reshape.101
  19.7 0.0 collective-permute-done.1
  19.7 0.0 collective-permute-done
  19.7 2.7 %pad_maximum_fusion = bf16[192,2,16,128]{3,2,1,0:T(8,128)(2,1)} fusion(bf16[64,2,16,128]{3,2,1,0:T(8,128)(2,1)} %collective-permute-done.1, bf16[64,2,16,128]{3,2,1,0:T(8,128)(2,1)} %get-tuple-element.73, bf16[64,2,16,128]{3,2,1,0:T(8,128)(2,1)} %collective-permute-done), kind=kLoop, calls=%fused_computation.35 | loop fusion | flops 1572864 | bytes 3145728 | tf_op jit(solution)/shard_map/concatenate | solution.py:16
  22.4 4.4 %gather_fusion = bf16[16,32,2,16,128]{4,3,2,1,0:T(8,128)(2,1)} fusion(bf16[192,2,16,128]{3,2,1,0:T(8,128)(2,1)} %pad_maximum_fusion, s32[16]{0:T(128)S(1)} %reshape.101), kind=kCustom, calls=%fused_computation | custom fusion | bytes 8388864 | tf_op jit(solution)/shard_map/vmap(vmap())/gather | solution.py:111
  26.8 3.0 %fusion.31 = (bf16[4,4,32,1,16,128]{5,4,3,2,1,0:T(8,128)(2,1)S(1)}, bf16[4,4,32,1,16,128]{5,4,3,2,1,0:T(8,128)(2,1)S(1)}) fusion(bf16[4,4,32,2,16,128]{5,4,3,2,1,0:T(8,128)(2,1)} %bitcast.75), kind=kLoop, calls=%fused_computation.51 | loop fusion | bytes 8388608 | tf_op jit(solution)/shard_map/slice | solution.py:114
  29.8 0.5 copy.41
  30.4 1.9 %copy.40 = bf16[4,4,32,1,16,128]{5,2,1,4,0,3:T(8,128)(2,1)} copy(bf16[4,4,32,1,16,128]{5,4,3,2,1,0:T(8,128)(2,1)S(1)} %get-tuple-element.72) | data formatting | bytes 4194304
  32.2 0.0 copy-done
  32.2 3.5 %bitcast_reduce_fusion = (f32[4,16,128]{2,1,0:T(8,128)S(1)}, f32[4,16,128,128]{3,2,1,0:T(8,128)}) fusion(pred[4,128]{1,0:T(4,128)(4,1)S(1)} %broadcast_compare_fusion, bf16[4,128,16,128]{3,1,2,0:T(8,128)(2,1)S(1)} %bitcast.80, bf16[4,128,16,128]{3,2,1,0:T(8,128)(2,1)S(1)} %bitcast.74), kind=kOutput, calls=%fused_computation.24 | convolution fusion | flops 271572992 | bytes 8421888 | tf_op jit(solution)/shard_map/mqhd,mkhd->mhqk/dot_general | solution.py:118
  35.7 0.0 all-to-all-done.1
  35.7 9.7 %all-to-all-start = ((bf16[16,64,128]{2,1,0:T(8,128)(2,1)}), bf16[16,64,128]{2,1,0:T(8,128)(2,1)S(1)}, u32[]{:S(2)}, u32[]{:S(2)}) async-start(bf16[16,64,128]{2,1,0:T(8,128)(2,1)} %slice_bitcast_fusion.2), calls=%async_computation | async-start | bytes 524288 | tf_op jit(solution)/shard_map/all_to_all | solution.py:92
  45.5 3.5 %fusion.18 = f32[4,16,128]{2,1,0:T(8,128)S(1)} fusion(f32[4,16,128,128]{3,2,1,0:T(8,128)} %get-tuple-element.78, f32[4,16,128]{2,1,0:T(8,128)S(1)} %get-tuple-element.77, pred[4,128]{1,0:T(4,128)(4,1)S(1)} %broadcast_compare_fusion), kind=kLoop, calls=%fused_computation.27 | loop fusion | flops 4186112 | bytes 4260352 | tf_op jit(solution)/shard_map/reduce_sum | solution.py:125
  49.0 0.1 copy.30
  49.1 6.4 %all-to-all-done = bf16[16,64,128]{2,1,0:T(8,128)(2,1)S(1)} async-done(((bf16[16,64,128]{2,1,0:T(8,128)(2,1)}), bf16[16,64,128]{2,1,0:T(8,128)(2,1)S(1)}, u32[]{:S(2)}, u32[]{:S(2)}) %all-to-all-start) | async-done | bytes 262176 | tf_op jit(solution)/shard_map/all_to_all | solution.py:92
  55.5 3.4 %while.12 = (s32[]{:T(128)}, bf16[2,512,128]{2,1,0:T(8,128)(2,1)S(1)}, bf16[2,512,128]{2,1,0:T(8,128)(2,1)S(1)}, bf16[1,1024,128]{2,1,0:T(8,128)(2,1)S(1)}, bf16[1,1024,128]{2,1,0:T(8,128)(2,1)S(1)}, /*index=5*/s32[]{:T(128)}) while((s32[]{:T(128)}, bf16[2,512,128]{2,1,0:T(8,128)(2,1)S(1)}, bf16[2,512,128]{2,1,0:T(8,128)(2,1)S(1)}, ...), condition=%wide.region_3.0_spmd, body=%wide.region_0.3_spmd.sunk | while | flops 272762368 | bytes 7233621 | solution.py:70
  55.5 0.5 multiply_reduce_fusion.2
  56.1 0.5 fusion.41
  56.6 0.6 fusion.42
  57.2 0.5 multiply_reduce_fusion.2
  57.8 0.5 fusion.41
  58.3 0.6 fusion.42
  58.9 0.4 copy.49
  59.3 0.5 broadcast.177
  59.9 2.2 %reduce = bf16[1024,128]{1,0:T(8,128)(2,1)S(1)} reduce(bf16[1024,1,128]{2,1,0:T(2,128)(2,1)S(1)} %bitcast.82, bf16[]{:T(256)} %broadcast.177), dimensions={1}, to_apply=%bitcast.65.reduce_sub_computation | reduce | bytes 524290
  62.1 0.8 reshape.113
  62.8 3.7 %all-to-all-start.2 = ((bf16[16,2,4096]{2,1,0:T(2,128)(2,1)}), bf16[16,2,4096]{2,1,0:T(2,128)(2,1)S(1)}, u32[]{:S(2)}, u32[]{:S(2)}) async-start(bf16[16,2,4096]{2,1,0:T(2,128)(2,1)} %reshape.113), calls=%async_computation.2 | async-start | bytes 524288 | tf_op jit(solution)/shard_map/all_to_all | solution.py:98
  66.6 5.0 %fusion.16 = bf16[4,128,16,128]{3,1,2,0:T(8,128)(2,1)S(1)} fusion(bf16[4,128,16,128]{3,1,2,0:T(8,128)(2,1)} %bitcast.78, f32[4,16,128,128]{3,2,1,0:T(8,128)} %get-tuple-element.78, f32[4,128,16]{1,2,0:T(8,128)S(1)} %bitcast.86, f32[4,16,128]{2,1,0:T(8,128)S(1)} %get-tuple-element.77, pred[4,128]{1,0:T(4,128)(4,1)S(1)} %broadcast_compare_fusion), kind=kOutput, calls=%fused_computation.22 | convolution fusion | flops 274726912 | bytes 8454656 | tf_op jit(solution)/shard_map/mhqk,mkhd->mqhd/dot_general | solution.py:126
  71.6 2.7 %copy.36 = bf16[4,128,16,128]{3,2,1,0:T(8,128)(2,1)} copy(bf16[4,128,16,128]{3,1,2,0:T(8,128)(2,1)S(1)} %fusion.16) | data formatting | bytes 4194304 | tf_op jit(solution)/shard_map/convert_element_type | solution.py:135
  74.3 2.1 %all-to-all-done.2 = bf16[16,2,4096]{2,1,0:T(2,128)(2,1)S(1)} async-done(((bf16[16,2,4096]{2,1,0:T(2,128)(2,1)}), bf16[16,2,4096]{2,1,0:T(2,128)(2,1)S(1)}, u32[]{:S(2)}, u32[]{:S(2)}) %all-to-all-start.2) | async-done | bytes 262176 | tf_op jit(solution)/shard_map/all_to_all | solution.py:98
  76.4 0.3 reshape.114
  76.7 0.9 %copy.37 = bf16[64,16,128]{2,1,0:T(8,128)(2,1)} copy(bf16[64,16,128]{2,0,1:T(8,128)(2,1)S(1)} %bitcast.84) | data formatting | bytes 524288
  (9 shorter events, 0.1 us)
Async XLA Ops:
  0.6 31.6 %copy-start = (bf16[512,16,128]{2,1,0:T(8,128)(2,1)S(1)}, bf16[512,16,128]{2,1,0:T(8,128)(2,1)}, u32[]{:S(2)}) copy-start(bf16[512,16,128]{2,1,0:T(8,128)(2,1)} %param.7) | copy-start | bytes 6291460
  0.6 16.1 %copy-start.1 = (bf16[64,3,16,128]{3,2,1,0:T(8,128)(2,1)S(1)}, bf16[64,3,16,128]{3,2,1,0:T(8,128)(2,1)}, u32[]{:S(2)}) copy-start(bf16[64,3,16,128]{3,2,1,0:T(8,128)(2,1)} %param.6) | copy-start | bytes 2359300
  2.8 15.0 %copy-start.2 = (s32[4,4]{1,0:T(4,128)S(1)}, s32[4,4]{1,0:T(4,128)}, u32[]{:S(2)}) copy-start(s32[4,4]{1,0:T(4,128)} %param.8) | copy-start | bytes 196
  2.8 16.9 %collective-permute-start.1 = (bf16[64,2,16,128]{3,2,1,0:T(8,128)(2,1)}, bf16[64,2,16,128]{3,2,1,0:T(8,128)(2,1)}, u32[]{:S(2)}, u32[]{:S(2)}) collective-permute-start(bf16[64,2,16,128]{3,2,1,0:T(8,128)(2,1)} %get-tuple-element.73), channel_id=1, source_target_pairs={{1,0},{2,1},{3,2},{4,3},{5,4},{6,5},{7,6},{8,7},{9,8},{10,9},{11,1... | collective-permute-start | bytes 1572872 | tf_op jit(solution)/shard_map/ppermute | solution.py:20
  4.2 15.5 %collective-permute-start = (bf16[64,2,16,128]{3,2,1,0:T(8,128)(2,1)}, bf16[64,2,16,128]{3,2,1,0:T(8,128)(2,1)}, u32[]{:S(2)}, u32[]{:S(2)}) collective-permute-start(bf16[64,2,16,128]{3,2,1,0:T(8,128)(2,1)} %get-tuple-element.73), channel_id=1, source_target_pairs={{0,1},{1,2},{2,3},{3,4},{4,5},{5,6},{6,7},{7,8},{8,9},{9,10},{10,1... | collective-permute-start | bytes 1572872 | tf_op jit(solution)/shard_map/ppermute | solution.py:18
  8.1 11.5 %copy-start.3 = (s32[4]{0:T(128)S(1)}, s32[4]{0:T(128)}, u32[]{:S(2)}) copy-start(s32[4]{0:T(128)} %param.9) | copy-start | bytes 52
  9.4 26.4 %all-to-all-start.1 = ((bf16[16,64,2,128]{3,2,1,0:T(2,128)(2,1)}), bf16[16,64,2,128]{3,2,1,0:T(2,128)(2,1)S(1)}, u32[]{:S(2)}, u32[]{:S(2)}) async-start(bf16[16,64,2,128]{3,2,1,0:T(2,128)(2,1)} %copy.29), calls=%async_computation.1 | async-start | bytes 1048576 | tf_op jit(solution)/shard_map/all_to_all | solution.py:93
  35.7 19.8 %all-to-all-start = ((bf16[16,64,128]{2,1,0:T(8,128)(2,1)}), bf16[16,64,128]{2,1,0:T(8,128)(2,1)S(1)}, u32[]{:S(2)}, u32[]{:S(2)}) async-start(bf16[16,64,128]{2,1,0:T(8,128)(2,1)} %slice_bitcast_fusion.2), calls=%async_computation | async-start | bytes 524288 | tf_op jit(solution)/shard_map/all_to_all | solution.py:92
  62.8 13.5 %all-to-all-start.2 = ((bf16[16,2,4096]{2,1,0:T(2,128)(2,1)}), bf16[16,2,4096]{2,1,0:T(2,128)(2,1)S(1)}, u32[]{:S(2)}, u32[]{:S(2)}) async-start(bf16[16,2,4096]{2,1,0:T(2,128)(2,1)} %reshape.113), calls=%async_computation.2 | async-start | bytes 524288 | tf_op jit(solution)/shard_map/all_to_all | solution.py:98
where the time goes:
time: 78.2 us; the launch traced here: 77.6 us
  starting transfers between devices  26.1 us (33%)
  local copies, waits for them, and re-layouts  21.8 us (28%)
  matrix products  10.8 us (14%)
  other arithmetic  9.53 us (12%)
  waiting for transfers between devices  8.53 us (11%)
  between operations  0.8 us (1%)
    all_to_all x1, starting transfers between devices, local(): lax.all_to_all(queries, 'seq', split_axis=0, concat_axis=1, tiled=True)  9.74 us
    all_to_all x1, starting transfers between devices, local(): lax.all_to_all(spread_kv, 'seq', split_axis=0, concat_axis=1, tiled=True)  7.37 us
    all_to_all x1, waiting for transfers between devices, local(): lax.all_to_all(queries, 'seq', split_axis=0, concat_axis=1, tiled=True)  6.42 us
    unnamed x16, local copies, waits for them, and re-layouts  5.97 us
    dot_general x1, matrix products, local(): jnp.einsum('mhqk,mkhd->mqhd', weights.astype(jnp.bfloat16), cross_values,...  5.04 us
    gather x1, local copies, waits for them, and re-layouts, take_block(): return lax.dynamic_slice_in_dim(extended, start_row, ABLK, 0)  4.43 us
    ppermute x1, starting transfers between devices, with_halo(): lax.ppermute(tail, axis, [(i, (i + 1) % count) for i in range(ends)])  3.85 us
    all_to_all x1, starting transfers between devices, local(): lax.all_to_all(head_out[None], 'seq', split_axis=1, concat_axis=0, tiled=...  3.71 us
  transfers between devices with their start and end apart: 5, of which 2 were waited for; matrix products, arithmetic and copies ran while one was open for 41% of the time, Pallas kernels for 0%

commit v1 on v0

v1 whole, which is shorter than its diff:
```python
import functools

import jax
import jax.numpy as jnp
from jax import lax
from jax.experimental import pallas as pl
from jax.experimental.pallas import tpu as pltpu
from jax.sharding import PartitionSpec as P

ABLK = 32
VBLK = 128
LOG2E = 1.4426950408889634
LOWEST = -1e30
VMEM_LIMIT = 48 * 1024 * 1024


def params():
    return pltpu.CompilerParams(vmem_limit_bytes=VMEM_LIMIT)


def whole(shape):
    return pl.BlockSpec(shape, lambda *unused: (0,) * len(shape))


def arrange_kernel(rows, qkv_ref, send_ref, kv_ref):
    for part in range(3):
        by_head = jnp.swapaxes(qkv_ref[:, part], 0, 1)
        send_ref[:, part * rows : (part + 1) * rows] = by_head
        if part:
            kv_ref[:, (part - 1) * rows : part * rows] = by_head


def arrange(audio_qkv):
    rows, unused, heads, size = audio_qkv.shape
    dtype = audio_qkv.dtype
    return pl.pallas_call(
        functools.partial(arrange_kernel, rows),
        out_shape=(
            jax.ShapeDtypeStruct((heads, 3 * rows, size), dtype),
            jax.ShapeDtypeStruct((heads, 2 * rows, size), dtype),
        ),
        compiler_params=params(),
        name="arrange",
    )(audio_qkv)


def attend_kernel(query_rows, rows, scale, fused, *refs):
    if fused:
        recv_ref, out_ref = refs
        query_ref, base = recv_ref, query_rows
    else:
        query_ref, recv_ref, out_ref = refs
        base = 0
    sources = recv_ref.shape[0]
    size = recv_ref.shape[2]
    group = max(1, 256 // query_rows)
    key_group = min(sources, 16)
    factor = scale * LOG2E
    for first in range(0, sources, group):
        queries = query_ref[first : first + group, :query_rows].reshape(group * query_rows, size)

        def advance(step, state):
            top, total, summed = state
            at = pl.ds(step * key_group, key_group)
            keys = recv_ref[at, base : base + rows].reshape(key_group * rows, size)
            values = recv_ref[at, base + rows : base + 2 * rows].reshape(key_group * rows, size)
            scores = lax.dot_general(
                queries, keys, (((1,), (1,)), ((), ())), preferred_element_type=jnp.float32
            )
            new_top = jnp.max(scores, axis=1, keepdims=True)
            if state[0] is not None:
                new_top = jnp.maximum(top, new_top)
            weights = jnp.exp2((scores - new_top) * factor)
            new_total = jnp.sum(weights, axis=1, keepdims=True)
            new_summed = jnp.dot(
                weights.astype(jnp.bfloat16), values, preferred_element_type=jnp.float32
            )
            if state[0] is not None:
                rescale = jnp.exp2((top - new_top) * factor)
                new_total = total * rescale + new_total
                new_summed = summed * rescale + new_summed
            return new_top, new_total, new_summed

        state = advance(0, (None, None, None))
        if sources > key_group:
            state = lax.fori_loop(1, sources // key_group, advance, state)
        result = (state[2] / state[1]).astype(jnp.bfloat16)
        out_ref[first : first + group] = result.reshape(group, query_rows, size)


def attend(operands, sources, query_rows, rows, size, scale):
    work = sources * query_rows * sources * rows
    return pl.pallas_call(
        functools.partial(attend_kernel, query_rows, rows, scale, len(operands) == 1),
        out_shape=jax.ShapeDtypeStruct((sources, query_rows, size), jnp.bfloat16),
        compiler_params=params(),
        cost_estimate=pl.CostEstimate(
            flops=4 * work * size, bytes_accessed=8 * sources * rows * size, transcendentals=work
        ),
        name="attend",
    )(*operands)


def collect_kernel(by_head_ref, out_ref):
    out_ref[...] = jnp.swapaxes(by_head_ref[...], 0, 1)


def collect(by_head):
    heads, rows, size = by_head.shape
    return pl.pallas_call(
        collect_kernel,
        out_shape=jax.ShapeDtypeStruct((rows, heads, size), by_head.dtype),
        compiler_params=params(),
        name="collect",
    )(by_head)


def video_kernel(
    rows, slots, scale, pairs_ref, counts_ref, first_ref,
    video_ref, before_ref, own_ref, after_ref, out_ref,
    near_keys, near_values, keys_ref, values_ref, queries_ref, result_ref,
):
    block = pl.program_id(0)
    heads = own_ref.shape[0]

    @pl.when(block == 0)
    def _():
        for place, ref in enumerate((before_ref, own_ref, after_ref)):
            near_keys[:, place * rows : (place + 1) * rows] = ref[:, :rows]
            near_values[:, place * rows : (place + 1) * rows] = ref[:, rows:]

    queries_ref[...] = jnp.swapaxes(video_ref[...], 0, 1)
    for slot in range(slots):
        start = pl.multiple_of((pairs_ref[block, slot] - first_ref[0]) * ABLK, ABLK)
        here = slice(slot * ABLK, (slot + 1) * ABLK)
        keys_ref[:, here] = near_keys[:, pl.ds(start, ABLK)]
        values_ref[:, here] = near_values[:, pl.ds(start, ABLK)]
    column = lax.broadcasted_iota(jnp.int32, (VBLK, slots * ABLK), 1)
    live = column < counts_ref[block] * ABLK
    factor = scale * LOG2E
    for head in range(heads):
        scores = lax.dot_general(
            queries_ref[head], keys_ref[head], (((1,), (1,)), ((), ())),
            preferred_element_type=jnp.float32,
        )
        scores = jnp.where(live, scores, LOWEST)
        top = jnp.max(scores, axis=1, keepdims=True)
        weights = jnp.exp2((scores - top) * factor)
        total = jnp.sum(weights, axis=1, keepdims=True)
        summed = jnp.dot(
            weights.astype(jnp.bfloat16), values_ref[head], preferred_element_type=jnp.float32
        )
        result_ref[head] = (summed / total).astype(jnp.bfloat16)
    out_ref[...] = jnp.swapaxes(result_ref[...], 0, 1)


def video(video_q, before, own, after, pairs, counts, first, scale):
    total, heads, size = video_q.shape
    rows = own.shape[1] // 2
    slots = pairs.shape[1]
    blocks = total // VBLK
    block_spec = pl.BlockSpec((VBLK, heads, size), lambda i, *unused: (i, 0, 0))
    work = total * heads * slots * ABLK
    return pl.pallas_call(
        functools.partial(video_kernel, rows, slots, scale),
        grid_spec=pltpu.PrefetchScalarGridSpec(
            num_scalar_prefetch=3,
            grid=(blocks,),
            in_specs=[block_spec] + [whole(own.shape)] * 3,
            out_specs=block_spec,
            scratch_shapes=[
                pltpu.VMEM((heads, 3 * rows, size), jnp.bfloat16),
                pltpu.VMEM((heads, 3 * rows, size), jnp.bfloat16),
                pltpu.VMEM((heads, slots * ABLK, size), jnp.bfloat16),
                pltpu.VMEM((heads, slots * ABLK, size), jnp.bfloat16),
                pltpu.VMEM((heads, VBLK, size), jnp.bfloat16),
                pltpu.VMEM((heads, VBLK, size), jnp.bfloat16),
            ],
        ),
        out_shape=jax.ShapeDtypeStruct(video_q.shape, jnp.bfloat16),
        compiler_params=params(),
        cost_estimate=pl.CostEstimate(
            flops=4 * work * size, bytes_accessed=4 * total * heads * size, transcendentals=work
        ),
        name="video",
    )(pairs, counts, first, video_q, before, own, after)


def local(audio_qkv, video_q, pairs, counts):
    devices = lax.axis_size("seq")
    rows, unused, heads, size = audio_qkv.shape
    bands = devices // heads
    band_rows = rows // bands
    scale = size ** (-0.5)
    send, kv = arrange(audio_qkv)
    ends = devices - 1
    before = lax.ppermute(kv, "seq", [(i, i + 1) for i in range(ends)])
    after = lax.ppermute(kv, "seq", [(i + 1, i) for i in range(ends)])

    def exchange(value):
        return lax.all_to_all(value, "seq", split_axis=0, concat_axis=0, tiled=True)

    if bands == 1:
        operands = (exchange(send),)
    else:
        queries = exchange(send[:, :rows].reshape(devices, band_rows, size))
        spread = jnp.broadcast_to(kv[:, None], (heads, bands, 2 * rows, size))
        operands = (queries, exchange(spread.reshape(devices, 2 * rows, size)))
    head_out = attend(operands, devices, band_rows, rows, size, scale)
    audio_attn = collect(exchange(head_out).reshape(heads, rows, size))
    first = (lax.axis_index("seq") * (rows // ABLK) - rows // ABLK).astype(jnp.int32).reshape(1)
    video_cross = video(video_q, before, kv, after, pairs, counts, first, scale)
    return audio_attn, video_cross


def solution(mesh):
    in_specs = (
        P(("groups", "seq"), None, None, None),
        P(("groups", "seq"), None, None),
        P(("groups", "seq"), None),
        P(("groups", "seq")),
    )
    out_specs = (P(("groups", "seq"), None, None), P(("groups", "seq"), None, None))
    return jax.shard_map(local, mesh=mesh, in_specs=in_specs, out_specs=out_specs, check_vma=False)
```

time: 78.2 us -> 57.4 us (0.73)
  Pallas kernels: 0 us -> 21.8 us
  local copies, waits for them, and re-layouts: 21.8 us -> 2.71 us
  matrix products: 10.8 us -> 0 us
  other arithmetic: 9.53 us -> 0 us
  starting transfers between devices: 26.1 us -> 18.3 us
  waiting for transfers between devices: 8.53 us -> 13.6 us
    pallas_call x0 -> x4, Pallas kernels: none -> 21.8 us  [the longest x1 18.7 us: video(): pl.pallas_call(functools.partial(video_kernel, rows, slots, scale), grid_...]
    dot_general x6 -> x0, matrix products: 10.8 us -> none  [the longest x1 5.04 us: local(): jnp.einsum('mhqk,mkhd->mqhd', weights.astype(jnp.bfloat16), cross_values,...]
    all_to_all x3 -> x2, starting transfers between devices: 20.8 us -> 13.1 us  [exchange(): return lax.all_to_all(value, 'seq', split_axis=0, concat_axis=0, tiled=True)]
    slice x2 -> x0, local copies, waits for them, and re-layouts: 5.13 us -> none  [the longest x1 3 us: local(): taken[:, :, :, 0]]
    all_to_all x3 -> x2, waiting for transfers between devices: 8.53 us -> 13.6 us  [exchange(): return lax.all_to_all(value, 'seq', split_axis=0, concat_axis=0, tiled=True)]
    reduce_sum x3 -> x0, other arithmetic: 4.52 us -> none  [the longest x1 3.46 us: local(): row_total = jnp.sum(weights, axis=3)]
    gather x1 -> x0, local copies, waits for them, and re-layouts: 4.43 us -> none  [take_block(): return lax.dynamic_slice_in_dim(extended, start_row, ABLK, 0)]
    unnamed x16 -> x12, local copies, waits for them, and re-layouts: 5.97 us -> 2.71 us
  transfers between devices with their start and end apart: 5 -> 4, of which waited for: 2 -> 1; matrix products, arithmetic and copies ran while one was open for 41% -> 0% of each run, Pallas kernels for 0% -> 36%
where the time goes in v1:
time: 57.4 us; the launch traced here: 57 us
  Pallas kernels  21.8 us (38%)
  starting transfers between devices  18.3 us (32%)
  waiting for transfers between devices  13.6 us (24%)
  local copies, waits for them, and re-layouts  2.71 us (5%)
  between operations  0.73 us (1%)
    pallas_call x1, Pallas kernels, video(): pl.pallas_call(functools.partial(video_kernel, rows, slots, scale), grid_...  18.7 us
    all_to_all x2, waiting for transfers between devices, exchange(): return lax.all_to_all(value, 'seq', split_axis=0, concat_axis=0, tiled=True)  13.6 us
    all_to_all x2, starting transfers between devices, exchange(): return lax.all_to_all(value, 'seq', split_axis=0, concat_axis=0, tiled=True)  13.1 us
    ppermute x1, starting transfers between devices, local(): before = lax.ppermute(kv, 'seq', [(i, i + 1) for i in range(ends)])  3.85 us
    unnamed x12, local copies, waits for them, and re-layouts  2.71 us
    pallas_call x1, Pallas kernels, attend(): pl.pallas_call(functools.partial(attend_kernel, query_rows, rows, scale,...  2.03 us
    ppermute x1, starting transfers between devices, local(): after = lax.ppermute(kv, 'seq', [(i + 1, i) for i in range(ends)])  1.29 us
  transfers between devices with their start and end apart: 4, of which 1 were waited for; matrix products, arithmetic and copies ran while one was open for 0% of the time, Pallas kernels for 36%

profile of v1, /device:TPU:0, one launch (start us, length us, event | category | flops | bytes accessed | tf_op | source)
XLA Modules:
  0.0 57.0 jit_solution(7598835968706912001)
XLA Ops:
  0.6 0.0 copy-start.1
  0.6 1.1 %copy-done.1 = bf16[64,3,16,128]{3,2,1,0:T(8,128)(2,1)S(1)} copy-done((bf16[64,3,16,128]{3,2,1,0:T(8,128)(2,1)S(1)}, bf16[64,3,16,128]{3,2,1,0:T(8,128)(2,1)}, u32[]{:S(2)}) %copy-start.1) | copy-done | bytes 786456
  1.8 0.3 arrange.1
  2.0 0.0 copy-start.2
  2.0 0.9 %copy-done.2 = bf16[16,192,128]{2,1,0:T(8,128)(2,1)} copy-done((bf16[16,192,128]{2,1,0:T(8,128)(2,1)}, bf16[16,192,128]{2,1,0:T(8,128)(2,1)S(1)}, u32[]{:S(2)}) %copy-start.2) | copy-done | bytes 786456
  2.9 0.0 copy-start
  2.9 0.0 copy-start.4
  2.9 0.0 copy-start.5
  2.9 7.5 %all-to-all-start = ((bf16[16,192,128]{2,1,0:T(8,128)(2,1)}), bf16[16,192,128]{2,1,0:T(8,128)(2,1)S(1)}, u32[]{:S(2)}, u32[]{:S(2)}) async-start(bf16[16,192,128]{2,1,0:T(8,128)(2,1)} %copy-done.2), calls=%async_computation | async-start | bytes 1572864 | tf_op jit(solution)/shard_map/all_to_all | solution.py:201
  10.4 1.3 %collective-permute-start.1 = (bf16[16,128,128]{2,1,0:T(8,128)(2,1)S(1)}, bf16[16,128,128]{2,1,0:T(8,128)(2,1)}, u32[]{:S(2)}, u32[]{:S(2)}) collective-permute-start(bf16[16,128,128]{2,1,0:T(8,128)(2,1)S(1)} %get-tuple-element.5.own_ref), channel_id=1, source_target_pairs={{1,0},{2,1},{3,2},{4,3},{5,4},{6,5},{7,6},{8,7},{9,8},{10,9},{11,1... | collective-permute-start | bytes 1572872 | tf_op jit(solution)/shard_map/ppermute | solution.py:198
  11.7 3.8 %collective-permute-start = (bf16[16,128,128]{2,1,0:T(8,128)(2,1)S(1)}, bf16[16,128,128]{2,1,0:T(8,128)(2,1)}, u32[]{:S(2)}, u32[]{:S(2)}) collective-permute-start(bf16[16,128,128]{2,1,0:T(8,128)(2,1)S(1)} %get-tuple-element.5.own_ref), channel_id=1, source_target_pairs={{0,1},{1,2},{2,3},{3,4},{4,5},{5,6},{6,7},{7,8},{8,9},{9,10},{10,1... | collective-permute-start | bytes 1572872 | tf_op jit(solution)/shard_map/ppermute | solution.py:197
  15.6 13.6 %all-to-all-done.refs_0_ = bf16[16,192,128]{2,1,0:T(8,128)(2,1)S(1)} async-done(((bf16[16,192,128]{2,1,0:T(8,128)(2,1)}), bf16[16,192,128]{2,1,0:T(8,128)(2,1)S(1)}, u32[]{:S(2)}, u32[]{:S(2)}) %all-to-all-start) | async-done | bytes 786464 | tf_op jit(solution)/shard_map/all_to_all | solution.py:201
  29.1 2.0 %attend.1 = bf16[16,64,128]{2,1,0:T(8,128)(2,1)S(1)} custom-call(bf16[16,192,128]{2,1,0:T(8,128)(2,1)S(1)} %all-to-all-done.refs_0_), custom_call_target="tpu_custom_call" | custom-call | flops 536870912 | bytes 1048576 | tf_op jit(solution)/shard_map/attend/pallas_call | solution.py:93
  31.2 0.0 copy-start.3
  31.2 0.7 %copy-done.3 = bf16[16,64,128]{2,1,0:T(8,128)(2,1)} copy-done((bf16[16,64,128]{2,1,0:T(8,128)(2,1)}, bf16[16,64,128]{2,1,0:T(8,128)(2,1)S(1)}, u32[]{:S(2)}) %copy-start.3) | copy-done | bytes 262168
  31.9 5.6 %all-to-all-start.1 = ((bf16[16,64,128]{2,1,0:T(8,128)(2,1)}), bf16[16,64,128]{2,1,0:T(8,128)(2,1)S(1)}, u32[]{:S(2)}, u32[]{:S(2)}) async-start(bf16[16,64,128]{2,1,0:T(8,128)(2,1)} %copy-done.3), calls=%async_computation.1 | async-start | bytes 524288 | tf_op jit(solution)/shard_map/all_to_all | solution.py:201
  37.5 0.0 collective-permute-done.1.after_ref
  37.5 0.0 collective-permute-done.before_ref
  37.5 0.0 copy-done
  37.5 0.0 copy-done.4
  37.5 0.0 copy-done.5
  37.6 18.7 %video.1 = bf16[512,16,128]{2,1,0:T(8,128)(2,1)} custom-call(s32[4,4]{1,0:T(4,128)S(1)} %copy-done.4, s32[4]{0:T(128)S(1)} %copy-done.5, s32[1]{0:T(128)} %bitcast.first_ref, bf16[512,16,128]{2,1,0:T(8,128)(2,1)S(1)} %copy-done, bf16[16,128,128]{2,1,0:T(8,128)(2,1)} %collective-permute-done.before_ref, bf16[16,128,128]{2,1,0:T(8,128)(2,1)S(1)} %get-tuple-element.5.own_ref, ...), custom_call_target="tpu_custom_call" | custom-call | flops 536870912 | bytes 4194304 | tf_op jit(solution)/shard_map/video/pallas_call | solution.py:164
  56.3 0.0 all-to-all-done.1.by_head_ref
  56.3 0.8 %collect.1 = bf16[64,16,128]{2,1,0:T(8,128)(2,1)} custom-call(bf16[16,64,128]{2,1,0:T(8,128)(2,1)S(1)} %all-to-all-done.1.by_head_ref), custom_call_target="tpu_custom_call" | custom-call | tf_op jit(solution)/shard_map/collect/pallas_call | solution.py:110
Async XLA Ops:
  0.6 1.1 %copy-start.1 = (bf16[64,3,16,128]{3,2,1,0:T(8,128)(2,1)S(1)}, bf16[64,3,16,128]{3,2,1,0:T(8,128)(2,1)}, u32[]{:S(2)}) copy-start(bf16[64,3,16,128]{3,2,1,0:T(8,128)(2,1)} %qkv_ref.1) | copy-start | bytes 2359300
  2.0 0.9 %copy-start.2 = (bf16[16,192,128]{2,1,0:T(8,128)(2,1)}, bf16[16,192,128]{2,1,0:T(8,128)(2,1)S(1)}, u32[]{:S(2)}) copy-start(bf16[16,192,128]{2,1,0:T(8,128)(2,1)S(1)} %get-tuple-element.4) | copy-start | bytes 2359300
  2.9 34.6 %copy-start = (bf16[512,16,128]{2,1,0:T(8,128)(2,1)S(1)}, bf16[512,16,128]{2,1,0:T(8,128)(2,1)}, u32[]{:S(2)}) copy-start(bf16[512,16,128]{2,1,0:T(8,128)(2,1)} %video_ref.1) | copy-start | bytes 6291460
  2.9 34.6 %copy-start.4 = (s32[4,4]{1,0:T(4,128)S(1)}, s32[4,4]{1,0:T(4,128)}, u32[]{:S(2)}) copy-start(s32[4,4]{1,0:T(4,128)} %pairs_ref.1) | copy-start | bytes 196
  2.9 34.6 %copy-start.5 = (s32[4]{0:T(128)S(1)}, s32[4]{0:T(128)}, u32[]{:S(2)}) copy-start(s32[4]{0:T(128)} %counts_ref.1) | copy-start | bytes 52
  2.9 26.2 %all-to-all-start = ((bf16[16,192,128]{2,1,0:T(8,128)(2,1)}), bf16[16,192,128]{2,1,0:T(8,128)(2,1)S(1)}, u32[]{:S(2)}, u32[]{:S(2)}) async-start(bf16[16,192,128]{2,1,0:T(8,128)(2,1)} %copy-done.2), calls=%async_computation | async-start | bytes 1572864 | tf_op jit(solution)/shard_map/all_to_all | solution.py:201
  10.4 27.1 %collective-permute-start.1 = (bf16[16,128,128]{2,1,0:T(8,128)(2,1)S(1)}, bf16[16,128,128]{2,1,0:T(8,128)(2,1)}, u32[]{:S(2)}, u32[]{:S(2)}) collective-permute-start(bf16[16,128,128]{2,1,0:T(8,128)(2,1)S(1)} %get-tuple-element.5.own_ref), channel_id=1, source_target_pairs={{1,0},{2,1},{3,2},{4,3},{5,4},{6,5},{7,6},{8,7},{9,8},{10,9},{11,1... | collective-permute-start | bytes 1572872 | tf_op jit(solution)/shard_map/ppermute | solution.py:198
  11.7 25.8 %collective-permute-start = (bf16[16,128,128]{2,1,0:T(8,128)(2,1)S(1)}, bf16[16,128,128]{2,1,0:T(8,128)(2,1)}, u32[]{:S(2)}, u32[]{:S(2)}) collective-permute-start(bf16[16,128,128]{2,1,0:T(8,128)(2,1)S(1)} %get-tuple-element.5.own_ref), channel_id=1, source_target_pairs={{0,1},{1,2},{2,3},{3,4},{4,5},{5,6},{6,7},{7,8},{8,9},{9,10},{10,1... | collective-permute-start | bytes 1572872 | tf_op jit(solution)/shard_map/ppermute | solution.py:197
  31.2 0.7 %copy-start.3 = (bf16[16,64,128]{2,1,0:T(8,128)(2,1)}, bf16[16,64,128]{2,1,0:T(8,128)(2,1)S(1)}, u32[]{:S(2)}) copy-start(bf16[16,64,128]{2,1,0:T(8,128)(2,1)S(1)} %attend.1) | copy-start | bytes 786436
  31.9 24.4 %all-to-all-start.1 = ((bf16[16,64,128]{2,1,0:T(8,128)(2,1)}), bf16[16,64,128]{2,1,0:T(8,128)(2,1)S(1)}, u32[]{:S(2)}, u32[]{:S(2)}) async-start(bf16[16,64,128]{2,1,0:T(8,128)(2,1)} %copy-done.3), calls=%async_computation.1 | async-start | bytes 524288 | tf_op jit(solution)/shard_map/all_to_all | solution.py:201

commit v2 on v1

--- a/solution.py
+++ b/solution.py
@@ -22,40 +22,67 @@
     return pl.BlockSpec(shape, lambda *unused: (0,) * len(shape))
 
 
-def arrange_kernel(rows, qkv_ref, send_ref, kv_ref):
-    for part in range(3):
-        by_head = jnp.swapaxes(qkv_ref[:, part], 0, 1)
-        send_ref[:, part * rows : (part + 1) * rows] = by_head
+def arrange_kernel(rows, qkv_ref, send_ref, kv_ref, came, turned, in_sems, out_sems):
+    order = (1, 2, 0)
+    arrivals = [
+        pltpu.make_async_copy(qkv_ref.at[:, part], came.at[part], in_sems.at[part]) for part in order
+    ]
+    for arrival in arrivals:
+        arrival.start()
+    departures = []
+    for arrival, part in zip(arrivals, order):
+        arrival.wait()
+        by_head = jnp.swapaxes(came[part], 0, 1)
+        turned[part] = by_head
+        departure = pltpu.make_async_copy(
+            turned.at[part], send_ref.at[:, pl.ds(part * rows, rows)], out_sems.at[part]
+        )
+        departure.start()
+        departures.append(departure)
         if part:
             kv_ref[:, (part - 1) * rows : part * rows] = by_head
+    for departure in departures:
+        departure.wait()
 
 
 def arrange(audio_qkv):
-    rows, unused, heads, size = audio_qkv.shape
+    rows, parts, heads, size = audio_qkv.shape
     dtype = audio_qkv.dtype
     return pl.pallas_call(
         functools.partial(arrange_kernel, rows),
+        in_specs=[pl.BlockSpec(memory_space=pltpu.HBM)],
+        out_specs=(
+            pl.BlockSpec(memory_space=pltpu.HBM),
+            pl.BlockSpec(memory_space=pltpu.VMEM),
+        ),
         out_shape=(
-            jax.ShapeDtypeStruct((heads, 3 * rows, size), dtype),
+            pltpu.HBM((heads, parts * rows, size), dtype),
             jax.ShapeDtypeStruct((heads, 2 * rows, size), dtype),
         ),
+        scratch_shapes=[
+            pltpu.VMEM((parts, rows, heads, size), dtype),
+            pltpu.VMEM((parts, heads, rows, size), dtype),
+            pltpu.SemaphoreType.DMA((parts,)),
+            pltpu.SemaphoreType.DMA((parts,)),
+        ],
         compiler_params=params(),
         name="arrange",
-    )(audio_qkv)
+    )(pltpu.with_memory_space_constraint(audio_qkv, pltpu.HBM))
 
 
 def attend_kernel(query_rows, rows, scale, fused, *refs):
     if fused:
-        recv_ref, out_ref = refs
+        recv_ref, out_ref, held, sems = refs
         query_ref, base = recv_ref, query_rows
     else:
-        query_ref, recv_ref, out_ref = refs
+        query_ref, recv_ref, out_ref, held, sems = refs
         base = 0
     sources = recv_ref.shape[0]
     size = recv_ref.shape[2]
     group = max(1, 256 // query_rows)
     key_group = min(sources, 16)
     factor = scale * LOG2E
+    departures = []
     for first in range(0, sources, group):
         queries = query_ref[first : first + group, :query_rows].reshape(group * query_rows, size)
 
@@ -85,14 +112,27 @@
         if sources > key_group:
             state = lax.fori_loop(1, sources // key_group, advance, state)
         result = (state[2] / state[1]).astype(jnp.bfloat16)
-        out_ref[first : first + group] = result.reshape(group, query_rows, size)
+        held[first : first + group] = result.reshape(group, query_rows, size)
+        departure = pltpu.make_async_copy(
+            held.at[pl.ds(first, group)], out_ref.at[pl.ds(first, group)], sems.at[first // group]
+        )
+        departure.start()
+        departures.append(departure)
+    for departure in departures:
+        departure.wait()
 
 
 def attend(operands, sources, query_rows, rows, size, scale):
     work = sources * query_rows * sources * rows
     return pl.pallas_call(
         functools.partial(attend_kernel, query_rows, rows, scale, len(operands) == 1),
-        out_shape=jax.ShapeDtypeStruct((sources, query_rows, size), jnp.bfloat16),
+        in_specs=[pl.BlockSpec(memory_space=pltpu.VMEM)] * len(operands),
+        out_specs=pl.BlockSpec(memory_space=pltpu.HBM),
+        out_shape=pltpu.HBM((sources, query_rows, size), jnp.bfloat16),
+        scratch_shapes=[
+            pltpu.VMEM((sources, query_rows, size), jnp.bfloat16),
+            pltpu.SemaphoreType.DMA((sources * query_rows // 256,)),
+        ],
         compiler_params=params(),
         cost_estimate=pl.CostEstimate(
             flops=4 * work * size, bytes_accessed=8 * sources * rows * size, transcendentals=work
@@ -116,45 +156,53 @@
 
 
 def video_kernel(
-    rows, slots, scale, pairs_ref, counts_ref, first_ref,
-    video_ref, before_ref, own_ref, after_ref, out_ref,
+    rows, slots, scale, group, pairs_ref, counts_ref, where_ref,
+    video_ref, own_ref, core_ref, chip_ref, out_ref,
     near_keys, near_values, keys_ref, values_ref, queries_ref, result_ref,
 ):
     block = pl.program_id(0)
-    heads = own_ref.shape[0]
+    heads, unused, size = own_ref.shape
 
     @pl.when(block == 0)
     def _():
-        for place, ref in enumerate((before_ref, own_ref, after_ref)):
-            near_keys[:, place * rows : (place + 1) * rows] = ref[:, :rows]
-            near_values[:, place * rows : (place + 1) * rows] = ref[:, rows:]
+        for ref, place in ((own_ref, rows), (core_ref, where_ref[1]), (chip_ref, where_ref[2])):
+            at = pl.ds(pl.multiple_of(place, rows), rows)
+            near_keys[:, at] = ref[:, :rows]
+            near_values[:, at] = ref[:, rows:]
+        values_ref[:, :, size:] = jnp.ones((heads, slots * ABLK, size), jnp.bfloat16)
 
     queries_ref[...] = jnp.swapaxes(video_ref[...], 0, 1)
     for slot in range(slots):
-        start = pl.multiple_of((pairs_ref[block, slot] - first_ref[0]) * ABLK, ABLK)
+        start = pl.multiple_of((pairs_ref[block, slot] - where_ref[0]) * ABLK, ABLK)
         here = slice(slot * ABLK, (slot + 1) * ABLK)
         keys_ref[:, here] = near_keys[:, pl.ds(start, ABLK)]
-        values_ref[:, here] = near_values[:, pl.ds(start, ABLK)]
+        values_ref[:, here, :size] = near_values[:, pl.ds(start, ABLK)]
     column = lax.broadcasted_iota(jnp.int32, (VBLK, slots * ABLK), 1)
     live = column < counts_ref[block] * ABLK
     factor = scale * LOG2E
-    for head in range(heads):
-        scores = lax.dot_general(
-            queries_ref[head], keys_ref[head], (((1,), (1,)), ((), ())),
-            preferred_element_type=jnp.float32,
-        )
-        scores = jnp.where(live, scores, LOWEST)
-        top = jnp.max(scores, axis=1, keepdims=True)
-        weights = jnp.exp2((scores - top) * factor)
-        total = jnp.sum(weights, axis=1, keepdims=True)
-        summed = jnp.dot(
-            weights.astype(jnp.bfloat16), values_ref[head], preferred_element_type=jnp.float32
-        )
-        result_ref[head] = (summed / total).astype(jnp.bfloat16)
+    for first in range(0, heads, group):
+        members = range(first, first + group)
+        scores = [
+            lax.dot_general(
+                queries_ref[head], keys_ref[head], (((1,), (1,)), ((), ())),
+                preferred_element_type=jnp.float32,
+            )
+            for head in members
+        ]
+        scores = jnp.stack([jnp.where(live, one, LOWEST) for one in scores])
+        top = jnp.max(scores, axis=2, keepdims=True)
+        weights = jnp.exp2((scores - top) * factor).astype(jnp.bfloat16)
+        summed = [
+            jnp.dot(weights[head - first], values_ref[head], preferred_element_type=jnp.float32)
+            for head in members
+        ]
+        for head in members:
+            both = summed[head - first]
+            result_ref[head] = (both[:, :size] / both[:, size:]).astype(jnp.bfloat16)
     out_ref[...] = jnp.swapaxes(result_ref[...], 0, 1)
 
 
-def video(video_q, before, own, after, pairs, counts, first, scale):
+def video(video_q, own, core, chip, pairs, counts, where, scale):
     total, heads, size = video_q.shape
     rows = own.shape[1] // 2
     slots = pairs.shape[1]
@@ -162,7 +210,7 @@
     block_spec = pl.BlockSpec((VBLK, heads, size), lambda i, *unused: (i, 0, 0))
     work = total * heads * slots * ABLK
     return pl.pallas_call(
-        functools.partial(video_kernel, rows, slots, scale),
+        functools.partial(video_kernel, rows, slots, scale, 4),
         grid_spec=pltpu.PrefetchScalarGridSpec(
             num_scalar_prefetch=3,
             grid=(blocks,),
@@ -172,7 +220,7 @@
                 pltpu.VMEM((heads, 3 * rows, size), jnp.bfloat16),
                 pltpu.VMEM((heads, 3 * rows, size), jnp.bfloat16),
                 pltpu.VMEM((heads, slots * ABLK, size), jnp.bfloat16),
-                pltpu.VMEM((heads, slots * ABLK, size), jnp.bfloat16),
+                pltpu.VMEM((heads, slots * ABLK, 2 * size), jnp.bfloat16),
                 pltpu.VMEM((heads, VBLK, size), jnp.bfloat16),
                 pltpu.VMEM((heads, VBLK, size), jnp.bfloat16),
             ],
@@ -183,7 +231,7 @@
             flops=4 * work * size, bytes_accessed=4 * total * heads * size, transcendentals=work
         ),
         name="video",
-    )(pairs, counts, first, video_q, before, own, after)
+    )(pairs, counts, where, video_q, own, core, chip)
 
 
 def local(audio_qkv, video_q, pairs, counts):
@@ -193,9 +241,8 @@
     band_rows = rows // bands
     scale = size ** (-0.5)
     send, kv = arrange(audio_qkv)
-    ends = devices - 1
-    before = lax.ppermute(kv, "seq", [(i, i + 1) for i in range(ends)])
-    after = lax.ppermute(kv, "seq", [(i + 1, i) for i in range(ends)])
+    core_pairs = [(i, i ^ 1) for i in range(devices)]
+    chip_pairs = [(i, ((i + 1) ^ 1) - 1) for i in range(1, devices - 1)]
 
     def exchange(value):
         return lax.all_to_all(value, "seq", split_axis=0, concat_axis=0, tiled=True)
@@ -206,10 +253,17 @@
         queries = exchange(send[:, :rows].reshape(devices, band_rows, size))
         spread = jnp.broadcast_to(kv[:, None], (heads, bands, 2 * rows, size))
         operands = (queries, exchange(spread.reshape(devices, 2 * rows, size)))
+    core = lax.ppermute(kv, "seq", core_pairs)
+    operands, late = lax.optimization_barrier((operands, kv))
+    chip = lax.ppermute(late, "seq", chip_pairs)
     head_out = attend(operands, devices, band_rows, rows, size, scale)
     audio_attn = collect(exchange(head_out).reshape(heads, rows, size))
-    first = (lax.axis_index("seq") * (rows // ABLK) - rows // ABLK).astype(jnp.int32).reshape(1)
-    video_cross = video(video_q, before, kv, after, pairs, counts, first, scale)
+    me = lax.axis_index("seq")
+    odd = me & 1
+    where = jnp.stack([(me - 1) * (rows // ABLK), 2 * (1 - odd) * rows, 2 * odd * rows])
+    video_cross = video(
+        video_q, kv, core, chip, pairs, counts, where.astype(jnp.int32), scale
+    )
     return audio_attn, video_cross
 
 

time: 57.4 us -> 59.5 us (1.037)
  waiting for transfers between devices: 13.6 us -> 28.3 us
  Pallas kernels: 21.8 us -> 14 us
  local copies, waits for them, and re-layouts: 2.71 us -> 0.02 us
  starting transfers between devices: 18.3 us -> 16.1 us
    all_to_all x2, waiting for transfers between devices: 13.6 us -> 28.3 us  [exchange(): return lax.all_to_all(value, 'seq', split_axis=0, concat_axis=0, tiled=True)]
    pallas_call x2, Pallas kernels: 19 us -> 10.5 us  [the longest x1 8.52 us: video(): pl.pallas_call(functools.partial(video_kernel, rows, slots, scale, 4), gr...]
    ppermute x2, starting transfers between devices: 5.14 us -> 1.85 us  [the longest x1 1.44 us: local(): chip = lax.ppermute(late, 'seq', chip_pairs)]
    unnamed x12 -> x6, local copies, waits for them, and re-layouts: 2.71 us -> 0.02 us
    all_to_all x2, starting transfers between devices: 13.1 us -> 14.3 us  [exchange(): return lax.all_to_all(value, 'seq', split_axis=0, concat_axis=0, tiled=True)]
    pallas_call x1, Pallas kernels: 2.03 us -> 2.72 us  [attend(): pl.pallas_call(functools.partial(attend_kernel, query_rows, rows, scale,...]
  transfers between devices with their start and end apart: 4 -> 4, of which waited for: 1 -> 2; matrix products, arithmetic and copies ran while one was open for 0% -> 0% of each run, Pallas kernels for 36% -> 6%
where the time goes in v2:
time: 59.5 us; the launch traced here: 59.2 us
  waiting for transfers between devices  28.3 us (48%)
  starting transfers between devices  16.1 us (27%)
  Pallas kernels  14 us (24%)
  between operations  0.71 us (1%)
    all_to_all x2, waiting for transfers between devices, exchange(): return lax.all_to_all(value, 'seq', split_axis=0, concat_axis=0, tiled=True)  28.3 us
    all_to_all x2, starting transfers between devices, exchange(): return lax.all_to_all(value, 'seq', split_axis=0, concat_axis=0, tiled=True)  14.3 us
    pallas_call x1, Pallas kernels, video(): pl.pallas_call(functools.partial(video_kernel, rows, slots, scale, 4), gr...  8.52 us
    pallas_call x1, Pallas kernels, attend(): pl.pallas_call(functools.partial(attend_kernel, query_rows, rows, scale,...  2.72 us
    pallas_call x1, Pallas kernels, arrange(): pl.pallas_call(functools.partial(arrange_kernel, rows), in_specs=[pl.Bloc...  1.98 us
    ppermute x1, starting transfers between devices, local(): chip = lax.ppermute(late, 'seq', chip_pairs)  1.44 us
  transfers between devices with their start and end apart: 4, of which 2 were waited for; matrix products, arithmetic and copies ran while one was open for 0% of the time, Pallas kernels for 6%

profile of v2, /device:TPU:0, one launch (start us, length us, event | category | flops | bytes accessed | tf_op | source)
XLA Modules:
  0.0 59.2 jit_solution(6615148854504518707)
XLA Ops:
  0.6 2.0 %arrange.1 = (bf16[16,192,128]{2,1,0:T(8,128)(2,1)}, bf16[16,128,128]{2,1,0:T(8,128)(2,1)S(1)}) custom-call(bf16[64,3,16,128]{3,2,1,0:T(8,128)(2,1)} %qkv_ref.1), custom_call_target="tpu_custom_call" | custom-call | tf_op jit(solution)/shard_map/arrange/pallas_call | solution.py:51
  2.6 0.0 copy-start
  2.6 0.0 copy-start.1
  2.6 0.0 copy-start.2
  2.7 7.5 %all-to-all-start = ((bf16[16,192,128]{2,1,0:T(8,128)(2,1)}), bf16[16,192,128]{2,1,0:T(8,128)(2,1)S(1)}, u32[]{:S(2)}, u32[]{:S(2)}) async-start(bf16[16,192,128]{2,1,0:T(8,128)(2,1)} %get-tuple-element.6), calls=%async_computation | async-start | bytes 1572864 | tf_op jit(solution)/shard_map/all_to_all | solution.py:248
  10.2 0.4 collective-permute-start
  10.6 18.3 %all-to-all-done.refs_0_ = bf16[16,192,128]{2,1,0:T(8,128)(2,1)S(1)} async-done(((bf16[16,192,128]{2,1,0:T(8,128)(2,1)}), bf16[16,192,128]{2,1,0:T(8,128)(2,1)S(1)}, u32[]{:S(2)}, u32[]{:S(2)}) %all-to-all-start) | async-done | bytes 786464 | tf_op jit(solution)/shard_map/all_to_all | solution.py:248
  28.9 1.4 %collective-permute-start.1 = (bf16[16,128,128]{2,1,0:T(8,128)(2,1)S(1)}, bf16[16,128,128]{2,1,0:T(8,128)(2,1)}, u32[]{:S(2)}, u32[]{:S(2)}) collective-permute-start(bf16[16,128,128]{2,1,0:T(8,128)(2,1)S(1)} %get-tuple-element.9.own_ref), channel_id=1, source_target_pairs={{1,2},{2,1},{3,4},{4,3},{5,6},{6,5},{7,8},{8,7},{9,10},{10,9},{11,... | collective-permute-start | bytes 1572872 | tf_op jit(solution)/shard_map/ppermute | solution.py:258
  30.3 2.7 %attend.1 = bf16[16,64,128]{2,1,0:T(8,128)(2,1)} custom-call(bf16[16,192,128]{2,1,0:T(8,128)(2,1)S(1)} %all-to-all-done.refs_0_), custom_call_target="tpu_custom_call" | custom-call | flops 536870912 | bytes 1048576 | tf_op jit(solution)/shard_map/attend/pallas_call | solution.py:127
  33.1 6.7 %all-to-all-start.1 = ((bf16[16,64,128]{2,1,0:T(8,128)(2,1)}), bf16[16,64,128]{2,1,0:T(8,128)(2,1)S(1)}, u32[]{:S(2)}, u32[]{:S(2)}) async-start(bf16[16,64,128]{2,1,0:T(8,128)(2,1)} %attend.1), calls=%async_computation.1 | async-start | bytes 524288 | tf_op jit(solution)/shard_map/all_to_all | solution.py:248
  39.8 0.1 pad_add_fusion.where_ref
  39.9 10.0 %all-to-all-done.1.by_head_ref = bf16[16,64,128]{2,1,0:T(8,128)(2,1)S(1)} async-done(((bf16[16,64,128]{2,1,0:T(8,128)(2,1)}), bf16[16,64,128]{2,1,0:T(8,128)(2,1)S(1)}, u32[]{:S(2)}, u32[]{:S(2)}) %all-to-all-start.1) | async-done | bytes 262176 | tf_op jit(solution)/shard_map/all_to_all | solution.py:248
  49.8 0.8 %collect.1 = bf16[64,16,128]{2,1,0:T(8,128)(2,1)} custom-call(bf16[16,64,128]{2,1,0:T(8,128)(2,1)S(1)} %all-to-all-done.1.by_head_ref), custom_call_target="tpu_custom_call" | custom-call | tf_op jit(solution)/shard_map/collect/pallas_call | solution.py:150
  50.6 0.0 collective-permute-done.core_ref
  50.6 0.0 collective-permute-done.1.chip_ref
  50.6 0.0 copy-done
  50.6 0.0 copy-done.1
  50.6 0.0 copy-done.2
  50.6 8.5 %video.1 = bf16[512,16,128]{2,1,0:T(8,128)(2,1)} custom-call(s32[4,4]{1,0:T(4,128)S(1)} %copy-done.1, s32[4]{0:T(128)S(1)} %copy-done.2, s32[3]{0:T(128)S(1)} %pad_add_fusion.where_ref, bf16[512,16,128]{2,1,0:T(8,128)(2,1)S(1)} %copy-done, bf16[16,128,128]{2,1,0:T(8,128)(2,1)S(1)} %get-tuple-element.9.own_ref, ...), custom_call_target="tpu_custom_call" | custom-call | flops 536870912 | bytes 4194304 | tf_op jit(solution)/shard_map/video/pallas_call | solution.py:212
Async XLA Ops:
  2.6 48.0 %copy-start = (bf16[512,16,128]{2,1,0:T(8,128)(2,1)S(1)}, bf16[512,16,128]{2,1,0:T(8,128)(2,1)}, u32[]{:S(2)}) copy-start(bf16[512,16,128]{2,1,0:T(8,128)(2,1)} %video_ref.1) | copy-start | bytes 6291460
  2.6 48.0 %copy-start.1 = (s32[4,4]{1,0:T(4,128)S(1)}, s32[4,4]{1,0:T(4,128)}, u32[]{:S(2)}) copy-start(s32[4,4]{1,0:T(4,128)} %pairs_ref.1) | copy-start | bytes 196
  2.6 48.0 %copy-start.2 = (s32[4]{0:T(128)S(1)}, s32[4]{0:T(128)}, u32[]{:S(2)}) copy-start(s32[4]{0:T(128)} %counts_ref.1) | copy-start | bytes 52
  2.7 26.2 %all-to-all-start = ((bf16[16,192,128]{2,1,0:T(8,128)(2,1)}), bf16[16,192,128]{2,1,0:T(8,128)(2,1)S(1)}, u32[]{:S(2)}, u32[]{:S(2)}) async-start(bf16[16,192,128]{2,1,0:T(8,128)(2,1)} %get-tuple-element.6), calls=%async_computation | async-start | bytes 1572864 | tf_op jit(solution)/shard_map/all_to_all | solution.py:248
  10.2 40.4 %collective-permute-start = (bf16[16,128,128]{2,1,0:T(8,128)(2,1)S(1)}, bf16[16,128,128]{2,1,0:T(8,128)(2,1)}, u32[]{:S(2)}, u32[]{:S(2)}) collective-permute-start(bf16[16,128,128]{2,1,0:T(8,128)(2,1)S(1)} %get-tuple-element.9.own_ref), channel_id=1, source_target_pairs={{0,1},{1,0},{2,3},{3,2},{4,5},{5,4},{6,7},{7,6},{8,9},{9,8},{10,11... | collective-permute-start | bytes 1572872 | tf_op jit(solution)/shard_map/ppermute | solution.py:256
  28.9 21.7 %collective-permute-start.1 = (bf16[16,128,128]{2,1,0:T(8,128)(2,1)S(1)}, bf16[16,128,128]{2,1,0:T(8,128)(2,1)}, u32[]{:S(2)}, u32[]{:S(2)}) collective-permute-start(bf16[16,128,128]{2,1,0:T(8,128)(2,1)S(1)} %get-tuple-element.9.own_ref), channel_id=1, source_target_pairs={{1,2},{2,1},{3,4},{4,3},{5,6},{6,5},{7,8},{8,7},{9,10},{10,9},{11,... | collective-permute-start | bytes 1572872 | tf_op jit(solution)/shard_map/ppermute | solution.py:258
  33.1 16.8 %all-to-all-start.1 = ((bf16[16,64,128]{2,1,0:T(8,128)(2,1)}), bf16[16,64,128]{2,1,0:T(8,128)(2,1)S(1)}, u32[]{:S(2)}, u32[]{:S(2)}) async-start(bf16[16,64,128]{2,1,0:T(8,128)(2,1)} %attend.1), calls=%async_computation.1 | async-start | bytes 524288 | tf_op jit(solution)/shard_map/all_to_all | solution.py:248

commit v3 on v2

--- a/solution.py
+++ b/solution.py
@@ -254,16 +254,16 @@
         spread = jnp.broadcast_to(kv[:, None], (heads, bands, 2 * rows, size))
         operands = (queries, exchange(spread.reshape(devices, 2 * rows, size)))
     core = lax.ppermute(kv, "seq", core_pairs)
-    operands, late = lax.optimization_barrier((operands, kv))
-    chip = lax.ppermute(late, "seq", chip_pairs)
-    head_out = attend(operands, devices, band_rows, rows, size, scale)
-    audio_attn = collect(exchange(head_out).reshape(heads, rows, size))
+    chip = lax.ppermute(kv, "seq", chip_pairs)
     me = lax.axis_index("seq")
     odd = me & 1
     where = jnp.stack([(me - 1) * (rows // ABLK), 2 * (1 - odd) * rows, 2 * odd * rows])
     video_cross = video(
         video_q, kv, core, chip, pairs, counts, where.astype(jnp.int32), scale
     )
+    operands, video_cross = lax.optimization_barrier((operands, video_cross))
+    head_out = attend(operands, devices, band_rows, rows, size, scale)
+    audio_attn = collect(exchange(head_out).reshape(heads, rows, size))
     return audio_attn, video_cross
 
 

time: 59.5 us -> 62.3 us (1.047)
  blocking collectives: 0 us -> 29.5 us
  waiting for transfers between devices: 28.3 us -> 6.11 us
  starting transfers between devices: 16.1 us -> 11.4 us
    all_to_all x0 -> x1, blocking collectives: none -> 29.5 us  [exchange(): return lax.all_to_all(value, 'seq', split_axis=0, concat_axis=0, tiled=True)]
    all_to_all x2 -> x1, waiting for transfers between devices: 28.3 us -> 4.52 us  [exchange(): return lax.all_to_all(value, 'seq', split_axis=0, concat_axis=0, tiled=True)]
    all_to_all x2 -> x1, starting transfers between devices: 14.3 us -> 7.4 us  [exchange(): return lax.all_to_all(value, 'seq', split_axis=0, concat_axis=0, tiled=True)]
    ppermute x1, starting transfers between devices: 0.41 us -> 2.54 us  [local(): core = lax.ppermute(kv, 'seq', core_pairs)]
    ppermute x1, waiting for transfers between devices: 0.01 us -> 1.59 us  [local(): core = lax.ppermute(kv, 'seq', core_pairs)]
  transfers between devices with their start and end apart: 4 -> 3, of which waited for: 2 -> 2; matrix products, arithmetic and copies ran while one was open for 0% -> 0% of each run, Pallas kernels for 6% -> 14%
where the time goes in v3:
time: 62.3 us; the launch traced here: 61.9 us
  blocking collectives  29.5 us (47%)
  Pallas kernels  14.2 us (23%)
  starting transfers between devices  11.4 us (18%)
  waiting for transfers between devices  6.11 us (10%)
  between operations  0.68 us (1%)
    all_to_all x1, blocking collectives, exchange(): return lax.all_to_all(value, 'seq', split_axis=0, concat_axis=0, tiled=True)  29.5 us
    pallas_call x1, Pallas kernels, video(): pl.pallas_call(functools.partial(video_kernel, rows, slots, scale, 4), gr...  8.5 us
    all_to_all x1, starting transfers between devices, exchange(): return lax.all_to_all(value, 'seq', split_axis=0, concat_axis=0, tiled=True)  7.4 us
    all_to_all x1, waiting for transfers between devices, exchange(): return lax.all_to_all(value, 'seq', split_axis=0, concat_axis=0, tiled=True)  4.52 us
    pallas_call x1, Pallas kernels, attend(): pl.pallas_call(functools.partial(attend_kernel, query_rows, rows, scale,...  2.72 us
    ppermute x1, starting transfers between devices, local(): core = lax.ppermute(kv, 'seq', core_pairs)  2.54 us
    pallas_call x1, Pallas kernels, arrange(): pl.pallas_call(functools.partial(arrange_kernel, rows), in_specs=[pl.Bloc...  2.18 us
    ppermute x1, waiting for transfers between devices, local(): core = lax.ppermute(kv, 'seq', core_pairs)  1.59 us
  transfers between devices with their start and end apart: 3, of which 2 were waited for; matrix products, arithmetic and copies ran while one was open for 0% of the time, Pallas kernels for 14%

profile of v3, /device:TPU:0, one launch (start us, length us, event | category | flops | bytes accessed | tf_op | source)
XLA Modules:
  0.0 61.9 jit_solution(2014615042901781977)
XLA Ops:
  0.6 0.0 copy-start.2
  0.6 0.0 copy-start.1
  0.7 0.0 copy-start
  0.7 2.2 %arrange.1 = (bf16[16,192,128]{2,1,0:T(8,128)(2,1)}, bf16[16,128,128]{2,1,0:T(8,128)(2,1)S(1)}) custom-call(bf16[64,3,16,128]{3,2,1,0:T(8,128)(2,1)} %qkv_ref.1), custom_call_target="tpu_custom_call" | custom-call | tf_op jit(solution)/shard_map/arrange/pallas_call | solution.py:51
  2.9 7.4 %all-to-all-start = ((bf16[16,192,128]{2,1,0:T(8,128)(2,1)}), bf16[16,192,128]{2,1,0:T(8,128)(2,1)S(1)}, u32[]{:S(2)}, u32[]{:S(2)}) async-start(bf16[16,192,128]{2,1,0:T(8,128)(2,1)} %get-tuple-element.6), calls=%async_computation | async-start | bytes 1572864 | tf_op jit(solution)/shard_map/all_to_all | solution.py:248
  10.3 1.5 %collective-permute-start.1 = (bf16[16,128,128]{2,1,0:T(8,128)(2,1)S(1)}, bf16[16,128,128]{2,1,0:T(8,128)(2,1)}, u32[]{:S(2)}, u32[]{:S(2)}) collective-permute-start(bf16[16,128,128]{2,1,0:T(8,128)(2,1)S(1)} %get-tuple-element.7.own_ref), channel_id=1, source_target_pairs={{1,2},{2,1},{3,4},{4,3},{5,6},{6,5},{7,8},{8,7},{9,10},{10,9},{11,... | collective-permute-start | bytes 1572872 | tf_op jit(solution)/shard_map/ppermute | solution.py:257
  11.7 2.5 %collective-permute-start = (bf16[16,128,128]{2,1,0:T(8,128)(2,1)S(1)}, bf16[16,128,128]{2,1,0:T(8,128)(2,1)}, u32[]{:S(2)}, u32[]{:S(2)}) collective-permute-start(bf16[16,128,128]{2,1,0:T(8,128)(2,1)S(1)} %get-tuple-element.7.own_ref), channel_id=1, source_target_pairs={{0,1},{1,0},{2,3},{3,2},{4,5},{5,4},{6,7},{7,6},{8,9},{9,8},{10,11... | collective-permute-start | bytes 1572872 | tf_op jit(solution)/shard_map/ppermute | solution.py:256
  14.3 0.1 pad_add_fusion.where_ref
  14.3 0.0 collective-permute-done.1.chip_ref
  14.3 1.6 %collective-permute-done.core_ref = bf16[16,128,128]{2,1,0:T(8,128)(2,1)} collective-permute-done((bf16[16,128,128]{2,1,0:T(8,128)(2,1)S(1)}, bf16[16,128,128]{2,1,0:T(8,128)(2,1)}, u32[]{:S(2)}, u32[]{:S(2)}) %collective-permute-start) | collective-permute-done | bytes 524320 | tf_op jit(solution)/shard_map/ppermute | solution.py:256
  15.9 0.0 copy-done.2
  15.9 0.0 copy-done.1
  15.9 0.0 copy-done
  15.9 8.5 %video.1 = bf16[512,16,128]{2,1,0:T(8,128)(2,1)} custom-call(s32[4,4]{1,0:T(4,128)S(1)} %copy-done.1, s32[4]{0:T(128)S(1)} %copy-done.2, s32[3]{0:T(128)S(1)} %pad_add_fusion.where_ref, bf16[512,16,128]{2,1,0:T(8,128)(2,1)S(1)} %copy-done, bf16[16,128,128]{2,1,0:T(8,128)(2,1)S(1)} %get-tuple-element.7.own_ref, ...), custom_call_target="tpu_custom_call" | custom-call | flops 536870912 | bytes 4194304 | tf_op jit(solution)/shard_map/video/pallas_call | solution.py:212
  24.4 4.5 %all-to-all-done.refs_0_ = bf16[16,192,128]{2,1,0:T(8,128)(2,1)S(1)} async-done(((bf16[16,192,128]{2,1,0:T(8,128)(2,1)}), bf16[16,192,128]{2,1,0:T(8,128)(2,1)S(1)}, u32[]{:S(2)}, u32[]{:S(2)}) %all-to-all-start) | async-done | bytes 786464 | tf_op jit(solution)/shard_map/all_to_all | solution.py:248
  29.0 2.7 %attend.1 = bf16[16,64,128]{2,1,0:T(8,128)(2,1)} custom-call(bf16[16,192,128]{2,1,0:T(8,128)(2,1)S(1)} %all-to-all-done.refs_0_), custom_call_target="tpu_custom_call" | custom-call | flops 536870912 | bytes 1048576 | tf_op jit(solution)/shard_map/attend/pallas_call | solution.py:127
  31.7 29.5 %all_to_all.10.by_head_ref = bf16[16,64,128]{2,1,0:T(8,128)(2,1)S(1)} all-to-all(bf16[16,64,128]{2,1,0:T(8,128)(2,1)} %attend.1), channel_id=1, replica_groups=mesh['groups'=2,'seq'=16] {'seq'}, dimensions={0} | all-to-all | bytes 524288 | tf_op jit(solution)/shard_map/all_to_all | solution.py:248
  61.2 0.8 %collect.1 = bf16[64,16,128]{2,1,0:T(8,128)(2,1)} custom-call(bf16[16,64,128]{2,1,0:T(8,128)(2,1)S(1)} %all_to_all.10.by_head_ref), custom_call_target="tpu_custom_call" | custom-call | tf_op jit(solution)/shard_map/collect/pallas_call | solution.py:150
Async XLA Ops:
  0.6 15.3 %copy-start.2 = (s32[4]{0:T(128)S(1)}, s32[4]{0:T(128)}, u32[]{:S(2)}) copy-start(s32[4]{0:T(128)} %counts_ref.1) | copy-start | bytes 52
  0.6 15.3 %copy-start.1 = (s32[4,4]{1,0:T(4,128)S(1)}, s32[4,4]{1,0:T(4,128)}, u32[]{:S(2)}) copy-start(s32[4,4]{1,0:T(4,128)} %pairs_ref.1) | copy-start | bytes 196
  0.7 15.3 %copy-start = (bf16[512,16,128]{2,1,0:T(8,128)(2,1)S(1)}, bf16[512,16,128]{2,1,0:T(8,128)(2,1)}, u32[]{:S(2)}) copy-start(bf16[512,16,128]{2,1,0:T(8,128)(2,1)} %video_ref.1) | copy-start | bytes 6291460
  2.9 26.1 %all-to-all-start = ((bf16[16,192,128]{2,1,0:T(8,128)(2,1)}), bf16[16,192,128]{2,1,0:T(8,128)(2,1)S(1)}, u32[]{:S(2)}, u32[]{:S(2)}) async-start(bf16[16,192,128]{2,1,0:T(8,128)(2,1)} %get-tuple-element.6), calls=%async_computation | async-start | bytes 1572864 | tf_op jit(solution)/shard_map/all_to_all | solution.py:248
  10.3 4.1 %collective-permute-start.1 = (bf16[16,128,128]{2,1,0:T(8,128)(2,1)S(1)}, bf16[16,128,128]{2,1,0:T(8,128)(2,1)}, u32[]{:S(2)}, u32[]{:S(2)}) collective-permute-start(bf16[16,128,128]{2,1,0:T(8,128)(2,1)S(1)} %get-tuple-element.7.own_ref), channel_id=1, source_target_pairs={{1,2},{2,1},{3,4},{4,3},{5,6},{6,5},{7,8},{8,7},{9,10},{10,9},{11,... | collective-permute-start | bytes 1572872 | tf_op jit(solution)/shard_map/ppermute | solution.py:257
  11.7 4.2 %collective-permute-start = (bf16[16,128,128]{2,1,0:T(8,128)(2,1)S(1)}, bf16[16,128,128]{2,1,0:T(8,128)(2,1)}, u32[]{:S(2)}, u32[]{:S(2)}) collective-permute-start(bf16[16,128,128]{2,1,0:T(8,128)(2,1)S(1)} %get-tuple-element.7.own_ref), channel_id=1, source_target_pairs={{0,1},{1,0},{2,3},{3,2},{4,5},{5,4},{6,7},{7,6},{8,9},{9,8},{10,11... | collective-permute-start | bytes 1572872 | tf_op jit(solution)/shard_map/ppermute | solution.py:256

commit v4 on v3

--- a/solution.py
+++ b/solution.py
@@ -22,52 +22,77 @@
     return pl.BlockSpec(shape, lambda *unused: (0,) * len(shape))
 
 
-def arrange_kernel(rows, qkv_ref, send_ref, kv_ref, came, turned, in_sems, out_sems):
-    order = (1, 2, 0)
+def arrange_kernel(rows, pieces, qkv_ref, queries_ref, kv_ref, came, sems):
+    step = rows // pieces
     arrivals = [
-        pltpu.make_async_copy(qkv_ref.at[:, part], came.at[part], in_sems.at[part]) for part in order
+        pltpu.make_async_copy(
+            qkv_ref.at[pl.ds(piece * step, step)], came.at[piece], sems.at[piece]
+        )
+        for piece in range(pieces)
     ]
     for arrival in arrivals:
         arrival.start()
-    departures = []
-    for arrival, part in zip(arrivals, order):
+    for piece, arrival in enumerate(arrivals):
         arrival.wait()
-        by_head = jnp.swapaxes(came[part], 0, 1)
-        turned[part] = by_head
-        departure = pltpu.make_async_copy(
-            turned.at[part], send_ref.at[:, pl.ds(part * rows, rows)], out_sems.at[part]
-        )
-        departure.start()
-        departures.append(departure)
-        if part:
-            kv_ref[:, (part - 1) * rows : part * rows] = by_head
-    for departure in departures:
-        departure.wait()
+        at = piece * step
+        queries_ref[:, at : at + step] = jnp.swapaxes(came[piece, :, 0], 0, 1)
+        kv_ref[:, at : at + step] = jnp.swapaxes(came[piece, :, 1], 0, 1)
+        kv_ref[:, rows + at : rows + at + step] = jnp.swapaxes(came[piece, :, 2], 0, 1)
 
 
 def arrange(audio_qkv):
     rows, parts, heads, size = audio_qkv.shape
     dtype = audio_qkv.dtype
-    return pl.pallas_call(
-        functools.partial(arrange_kernel, rows),
+    pieces = 4
+    return pl.pallas_call(
+        functools.partial(arrange_kernel, rows, pieces),
         in_specs=[pl.BlockSpec(memory_space=pltpu.HBM)],
-        out_specs=(
-            pl.BlockSpec(memory_space=pltpu.HBM),
-            pl.BlockSpec(memory_space=pltpu.VMEM),
-        ),
+        out_specs=(pl.BlockSpec(memory_space=pltpu.VMEM),) * 2,
         out_shape=(
-            pltpu.HBM((heads, parts * rows, size), dtype),
+            jax.ShapeDtypeStruct((heads, rows, size), dtype),
             jax.ShapeDtypeStruct((heads, 2 * rows, size), dtype),
         ),
         scratch_shapes=[
-            pltpu.VMEM((parts, rows, heads, size), dtype),
-            pltpu.VMEM((parts, heads, rows, size), dtype),
-            pltpu.SemaphoreType.DMA((parts,)),
-            pltpu.SemaphoreType.DMA((parts,)),
+            pltpu.VMEM((pieces, rows // pieces, parts, heads, size), dtype),
+            pltpu.SemaphoreType.DMA((pieces,)),
         ],
         compiler_params=params(),
         name="arrange",
     )(pltpu.with_memory_space_constraint(audio_qkv, pltpu.HBM))
+
+
+def join_kernel(pieces, queries_ref, kv_ref, send_ref, sems):
+    heads, rows, unused = queries_ref.shape
+    step = heads // pieces
+    departures = []
+    for piece in range(pieces):
+        at = pl.ds(piece * step, step)
+        for half, ref in enumerate((queries_ref, kv_ref)):
+            departures.append(
+                pltpu.make_async_copy(
+                    ref.at[at],
+                    send_ref.at[at, pl.ds(half * rows, ref.shape[1])],
+                    sems.at[2 * piece + half],
+                )
+            )
+    for departure in departures:
+        departure.start()
+    for departure in departures:
+        departure.wait()
+
+
+def join(queries, kv):
+    heads, rows, size = queries.shape
+    pieces = 2
+    return pl.pallas_call(
+        functools.partial(join_kernel, pieces),
+        in_specs=[pl.BlockSpec(memory_space=pltpu.VMEM)] * 2,
+        out_specs=pl.BlockSpec(memory_space=pltpu.HBM),
+        out_shape=pltpu.HBM((heads, rows + kv.shape[1], size), queries.dtype),
+        scratch_shapes=[pltpu.SemaphoreType.DMA((2 * pieces,))],
+        compiler_params=params(),
+        name="join",
+    )(queries, kv)
 
 
 def attend_kernel(query_rows, rows, scale, fused, *refs):
@@ -240,21 +265,22 @@
     bands = devices // heads
     band_rows = rows // bands
     scale = size ** (-0.5)
-    send, kv = arrange(audio_qkv)
+    queries, kv = arrange(audio_qkv)
     core_pairs = [(i, i ^ 1) for i in range(devices)]
     chip_pairs = [(i, ((i + 1) ^ 1) - 1) for i in range(1, devices - 1)]
 
+    chip = lax.ppermute(kv, "seq", chip_pairs)
+
     def exchange(value):
         return lax.all_to_all(value, "seq", split_axis=0, concat_axis=0, tiled=True)
 
     if bands == 1:
-        operands = (exchange(send),)
+        operands = (exchange(join(queries, kv)),)
     else:
-        queries = exchange(send[:, :rows].reshape(devices, band_rows, size))
+        queries = exchange(queries.reshape(devices, band_rows, size))
         spread = jnp.broadcast_to(kv[:, None], (heads, bands, 2 * rows, size))
         operands = (queries, exchange(spread.reshape(devices, 2 * rows, size)))
     core = lax.ppermute(kv, "seq", core_pairs)
-    chip = lax.ppermute(kv, "seq", chip_pairs)
     me = lax.axis_index("seq")
     odd = me & 1
     where = jnp.stack([(me - 1) * (rows // ABLK), 2 * (1 - odd) * rows, 2 * odd * rows])

time: 62.3 us -> 62.5 us (level)
  starting transfers between devices: 11.4 us -> 9.27 us
  waiting for transfers between devices: 6.11 us -> 8.2 us
    all_to_all x1, waiting for transfers between devices: 4.52 us -> 8.04 us  [exchange(): return lax.all_to_all(value, 'seq', split_axis=0, concat_axis=0, tiled=True)]
    ppermute x1, starting transfers between devices: 2.54 us -> 0.41 us  [local(): core = lax.ppermute(kv, 'seq', core_pairs)]
    ppermute x1, waiting for transfers between devices: 1.59 us -> 0.16 us  [local(): core = lax.ppermute(kv, 'seq', core_pairs)]
    pallas_call x1 -> x2, Pallas kernels: 2.18 us -> 2.39 us  [the longest x1 1.45 us: arrange(): pl.pallas_call(functools.partial(arrange_kernel, rows, pieces), in_specs=...]
where the time goes in v4:
time: 62.5 us; the launch traced here: 62.1 us
  blocking collectives  29.4 us (47%)
  Pallas kernels  14.4 us (23%)
  starting transfers between devices  9.27 us (15%)
  waiting for transfers between devices  8.2 us (13%)
  between operations  0.7 us (1%)
    all_to_all x1, blocking collectives, exchange(): return lax.all_to_all(value, 'seq', split_axis=0, concat_axis=0, tiled=True)  29.4 us
    pallas_call x1, Pallas kernels, video(): pl.pallas_call(functools.partial(video_kernel, rows, slots, scale, 4), gr...  8.54 us
    all_to_all x1, waiting for transfers between devices, exchange(): return lax.all_to_all(value, 'seq', split_axis=0, concat_axis=0, tiled=True)  8.04 us
    all_to_all x1, starting transfers between devices, exchange(): return lax.all_to_all(value, 'seq', split_axis=0, concat_axis=0, tiled=True)  7.4 us
    pallas_call x1, Pallas kernels, attend(): pl.pallas_call(functools.partial(attend_kernel, query_rows, rows, scale,...  2.72 us
    ppermute x1, starting transfers between devices, local(): chip = lax.ppermute(kv, 'seq', chip_pairs)  1.46 us
    pallas_call x1, Pallas kernels, arrange(): pl.pallas_call(functools.partial(arrange_kernel, rows, pieces), in_specs=...  1.45 us
  transfers between devices with their start and end apart: 3, of which 2 were waited for; matrix products, arithmetic and copies ran while one was open for 0% of the time, Pallas kernels for 14%

profile of v4, /device:TPU:0, one launch (start us, length us, event | category | flops | bytes accessed | tf_op | source)
XLA Modules:
  0.0 62.1 jit_solution(6675372292579497471)
XLA Ops:
  0.6 0.0 copy-start
  0.6 0.0 copy-start.1
  0.7 0.0 copy-start.2
  0.7 1.5 %arrange.1 = (bf16[16,64,128]{2,1,0:T(8,128)(2,1)S(1)}, bf16[16,128,128]{2,1,0:T(8,128)(2,1)S(1)}) custom-call(bf16[64,3,16,128]{3,2,1,0:T(8,128)(2,1)} %qkv_ref.1), custom_call_target="tpu_custom_call" | custom-call | tf_op jit(solution)/shard_map/arrange/pallas_call | solution.py:47
  2.1 0.9 %join.1 = bf16[16,192,128]{2,1,0:T(8,128)(2,1)} custom-call(bf16[16,64,128]{2,1,0:T(8,128)(2,1)S(1)} %get-tuple-element.6.queries_ref, bf16[16,128,128]{2,1,0:T(8,128)(2,1)S(1)} %get-tuple-element.7.kv_ref.own_ref), custom_call_target="tpu_custom_call" | custom-call | tf_op jit(solution)/shard_map/join/pallas_call | solution.py:87
  3.1 7.4 %all-to-all-start = ((bf16[16,192,128]{2,1,0:T(8,128)(2,1)}), bf16[16,192,128]{2,1,0:T(8,128)(2,1)S(1)}, u32[]{:S(2)}, u32[]{:S(2)}) async-start(bf16[16,192,128]{2,1,0:T(8,128)(2,1)} %join.1), calls=%async_computation | async-start | bytes 1572864 | tf_op jit(solution)/shard_map/all_to_all | solution.py:275
  10.5 0.4 collective-permute-start
  10.9 1.5 %collective-permute-start.1 = (bf16[16,128,128]{2,1,0:T(8,128)(2,1)S(1)}, bf16[16,128,128]{2,1,0:T(8,128)(2,1)}, u32[]{:S(2)}, u32[]{:S(2)}) collective-permute-start(bf16[16,128,128]{2,1,0:T(8,128)(2,1)S(1)} %get-tuple-element.7.kv_ref.own_ref), channel_id=1, source_target_pairs={{1,2},{2,1},{3,4},{4,3},{5,6},{6,5},{7,8},{8,7},{9,10},{10,9},{11,... | collective-permute-start | bytes 1572872 | tf_op jit(solution)/shard_map/ppermute | solution.py:272
  12.3 0.1 pad_add_fusion.where_ref
  12.4 0.2 collective-permute-done.core_ref
  12.6 0.0 collective-permute-done.1.chip_ref
  12.6 0.0 copy-done
  12.6 0.0 copy-done.1
  12.6 0.0 copy-done.2
  12.6 8.5 %video.1 = bf16[512,16,128]{2,1,0:T(8,128)(2,1)} custom-call(s32[4,4]{1,0:T(4,128)S(1)} %copy-done.1, s32[4]{0:T(128)S(1)} %copy-done.2, s32[3]{0:T(128)S(1)} %pad_add_fusion.where_ref, bf16[512,16,128]{2,1,0:T(8,128)(2,1)S(1)} %copy-done, bf16[16,128,128]{2,1,0:T(8,128)(2,1)S(1)} %get-tuple-element.7.kv_ref.own_ref, ...), custom_call_target="tpu_custom_call" | custom-call | flops 536870912 | bytes 4194304 | tf_op jit(solution)/shard_map/video/pallas_call | solution.py:237
  21.1 8.0 %all-to-all-done.refs_0_ = bf16[16,192,128]{2,1,0:T(8,128)(2,1)S(1)} async-done(((bf16[16,192,128]{2,1,0:T(8,128)(2,1)}), bf16[16,192,128]{2,1,0:T(8,128)(2,1)S(1)}, u32[]{:S(2)}, u32[]{:S(2)}) %all-to-all-start) | async-done | bytes 786464 | tf_op jit(solution)/shard_map/all_to_all | solution.py:275
  29.2 2.7 %attend.1 = bf16[16,64,128]{2,1,0:T(8,128)(2,1)} custom-call(bf16[16,192,128]{2,1,0:T(8,128)(2,1)S(1)} %all-to-all-done.refs_0_), custom_call_target="tpu_custom_call" | custom-call | flops 536870912 | bytes 1048576 | tf_op jit(solution)/shard_map/attend/pallas_call | solution.py:152
  31.9 29.4 %all_to_all.10.by_head_ref = bf16[16,64,128]{2,1,0:T(8,128)(2,1)S(1)} all-to-all(bf16[16,64,128]{2,1,0:T(8,128)(2,1)} %attend.1), channel_id=1, replica_groups=mesh['groups'=2,'seq'=16] {'seq'}, dimensions={0} | all-to-all | bytes 524288 | tf_op jit(solution)/shard_map/all_to_all | solution.py:275
  61.4 0.8 %collect.1 = bf16[64,16,128]{2,1,0:T(8,128)(2,1)} custom-call(bf16[16,64,128]{2,1,0:T(8,128)(2,1)S(1)} %all_to_all.10.by_head_ref), custom_call_target="tpu_custom_call" | custom-call | tf_op jit(solution)/shard_map/collect/pallas_call | solution.py:175
Async XLA Ops:
  0.6 12.0 %copy-start = (bf16[512,16,128]{2,1,0:T(8,128)(2,1)S(1)}, bf16[512,16,128]{2,1,0:T(8,128)(2,1)}, u32[]{:S(2)}) copy-start(bf16[512,16,128]{2,1,0:T(8,128)(2,1)} %video_ref.1) | copy-start | bytes 6291460
  0.6 11.9 %copy-start.1 = (s32[4,4]{1,0:T(4,128)S(1)}, s32[4,4]{1,0:T(4,128)}, u32[]{:S(2)}) copy-start(s32[4,4]{1,0:T(4,128)} %pairs_ref.1) | copy-start | bytes 196
  0.7 11.9 %copy-start.2 = (s32[4]{0:T(128)S(1)}, s32[4]{0:T(128)}, u32[]{:S(2)}) copy-start(s32[4]{0:T(128)} %counts_ref.1) | copy-start | bytes 52
  3.1 26.1 %all-to-all-start = ((bf16[16,192,128]{2,1,0:T(8,128)(2,1)}), bf16[16,192,128]{2,1,0:T(8,128)(2,1)S(1)}, u32[]{:S(2)}, u32[]{:S(2)}) async-start(bf16[16,192,128]{2,1,0:T(8,128)(2,1)} %join.1), calls=%async_computation | async-start | bytes 1572864 | tf_op jit(solution)/shard_map/all_to_all | solution.py:275
  10.5 2.1 %collective-permute-start = (bf16[16,128,128]{2,1,0:T(8,128)(2,1)S(1)}, bf16[16,128,128]{2,1,0:T(8,128)(2,1)}, u32[]{:S(2)}, u32[]{:S(2)}) collective-permute-start(bf16[16,128,128]{2,1,0:T(8,128)(2,1)S(1)} %get-tuple-element.7.kv_ref.own_ref), channel_id=1, source_target_pairs={{0,1},{1,0},{2,3},{3,2},{4,5},{5,4},{6,7},{7,6},{8,9},{9,8},{10,11... | collective-permute-start | bytes 1572872 | tf_op jit(solution)/shard_map/ppermute | solution.py:283
  10.9 1.7 %collective-permute-start.1 = (bf16[16,128,128]{2,1,0:T(8,128)(2,1)S(1)}, bf16[16,128,128]{2,1,0:T(8,128)(2,1)}, u32[]{:S(2)}, u32[]{:S(2)}) collective-permute-start(bf16[16,128,128]{2,1,0:T(8,128)(2,1)S(1)} %get-tuple-element.7.kv_ref.own_ref), channel_id=1, source_target_pairs={{1,2},{2,1},{3,4},{4,3},{5,6},{6,5},{7,8},{8,7},{9,10},{10,9},{11,... | collective-permute-start | bytes 1572872 | tf_op jit(solution)/shard_map/ppermute | solution.py:272

commit v5 on v4

--- a/solution.py
+++ b/solution.py
@@ -239,7 +239,12 @@
         grid_spec=pltpu.PrefetchScalarGridSpec(
             num_scalar_prefetch=3,
             grid=(blocks,),
-            in_specs=[block_spec] + [whole(own.shape)] * 3,
+            in_specs=[
+                block_spec,
+                whole(own.shape),
+                whole(core.shape),
+                pl.BlockSpec((None,) + own.shape, lambda i, p, c, where: (where[3], 0, 0, 0)),
+            ],
             out_specs=block_spec,
             scratch_shapes=[
                 pltpu.VMEM((heads, 3 * rows, size), jnp.bfloat16),
@@ -267,9 +272,18 @@
     scale = size ** (-0.5)
     queries, kv = arrange(audio_qkv)
     core_pairs = [(i, i ^ 1) for i in range(devices)]
-    chip_pairs = [(i, ((i + 1) ^ 1) - 1) for i in range(1, devices - 1)]
-
-    chip = lax.ppermute(kv, "seq", chip_pairs)
+    clips = lax.axis_size("groups")
+    chip_pairs = [
+        [clip * devices + i, clip * devices + i + 1]
+        for clip in range(clips)
+        for i in range(1, devices - 1, 2)
+    ] + [
+        [clip * devices + i, (clip + 1) * devices + i]
+        for clip in range(0, clips, 2)
+        for i in (0, devices - 1)
+    ]
+
+    chip = lax.all_gather(kv, ("groups", "seq"), axis_index_groups=chip_pairs)
 
     def exchange(value):
         return lax.all_to_all(value, "seq", split_axis=0, concat_axis=0, tiled=True)
@@ -283,7 +297,7 @@
     core = lax.ppermute(kv, "seq", core_pairs)
     me = lax.axis_index("seq")
     odd = me & 1
-    where = jnp.stack([(me - 1) * (rows // ABLK), 2 * (1 - odd) * rows, 2 * odd * rows])
+    where = jnp.stack([(me - 1) * (rows // ABLK), 2 * (1 - odd) * rows, 2 * odd * rows, odd])
     video_cross = video(
         video_q, kv, core, chip, pairs, counts, where.astype(jnp.int32), scale
     )

time: 62.5 us -> 80.4 us (1.29)
  between operations: 0.7 us -> 14.1 us
  waiting for transfers between devices: 8.2 us -> 19.2 us
  blocking collectives: 29.4 us -> 21.3 us
  Pallas kernels: 14.4 us -> 16.1 us
  starting transfers between devices: 9.27 us -> 7.91 us
  local copies, waits for them, and re-layouts: 0.01 us -> 1.24 us
    all_gather x0 -> x1, waiting for transfers between devices: none -> 16.9 us  [local(): chip = lax.all_gather(kv, ('groups', 'seq'), axis_index_groups=chip_pairs)]
    all_to_all x1, blocking collectives: 29.4 us -> 21.3 us  [exchange(): return lax.all_to_all(value, 'seq', split_axis=0, concat_axis=0, tiled=True)]
    all_to_all x1, waiting for transfers between devices: 8.04 us -> 0.01 us  [exchange(): return lax.all_to_all(value, 'seq', split_axis=0, concat_axis=0, tiled=True)]
    ppermute x1, waiting for transfers between devices: 0.16 us -> 1.67 us  [local(): core = lax.ppermute(kv, 'seq', core_pairs)]
    ppermute x1 -> x0, starting transfers between devices: 1.46 us -> none  [local(): chip = lax.ppermute(kv, 'seq', chip_pairs)]
    unnamed x6 -> x8, local copies, waits for them, and re-layouts: 0.01 us -> 1.24 us
    pallas_call x1, Pallas kernels: 0.94 us -> 2.02 us  [join(): pl.pallas_call(functools.partial(join_kernel, pieces), in_specs=[pl.Block...]
  transfers between devices with their start and end apart: 3 -> 3, of which waited for: 2 -> 2; matrix products, arithmetic and copies ran while one was open for 0% -> 0% of each run, Pallas kernels for 14% -> 10%
where the time goes in v5:
time: 80.4 us; the launch traced here: 80 us
  blocking collectives  21.3 us (26%)
  waiting for transfers between devices  19.2 us (24%)
  Pallas kernels  16.1 us (20%)
  between operations  14.1 us (18%)
  starting transfers between devices  7.91 us (10%)
  local copies, waits for them, and re-layouts  1.24 us (2%)
    all_to_all x1, blocking collectives, exchange(): return lax.all_to_all(value, 'seq', split_axis=0, concat_axis=0, tiled=True)  21.3 us
    all_gather x1, waiting for transfers between devices, local(): chip = lax.all_gather(kv, ('groups', 'seq'), axis_index_groups=chip_pairs)  16.9 us
    pallas_call x1, Pallas kernels, video(): pl.pallas_call(functools.partial(video_kernel, rows, slots, scale, 4), gr...  8.37 us
    all_to_all x1, starting transfers between devices, exchange(): return lax.all_to_all(value, 'seq', split_axis=0, concat_axis=0, tiled=True)  7.4 us
    pallas_call x1, Pallas kernels, attend(): pl.pallas_call(functools.partial(attend_kernel, query_rows, rows, scale,...  2.72 us
    pallas_call x1, Pallas kernels, arrange(): pl.pallas_call(functools.partial(arrange_kernel, rows, pieces), in_specs=...  2.22 us
    pallas_call x1, Pallas kernels, join(): pl.pallas_call(functools.partial(join_kernel, pieces), in_specs=[pl.Block...  2.02 us
    ppermute x1, waiting for transfers between devices, local(): core = lax.ppermute(kv, 'seq', core_pairs)  1.67 us
  transfers between devices with their start and end apart: 3, of which 2 were waited for; matrix products, arithmetic and copies ran while one was open for 0% of the time, Pallas kernels for 10%

profile of v5, /device:TPU:0, one launch (start us, length us, event | category | flops | bytes accessed | tf_op | source)
XLA Modules:
  0.0 80.0 jit_solution(13247478181719034857)
XLA Ops:
  7.2 0.0 copy-start
  7.2 0.0 copy-start.2
  7.2 0.0 copy-start.3
  7.2 2.2 %arrange.1 = (bf16[16,64,128]{2,1,0:T(8,128)(2,1)S(1)}, bf16[16,128,128]{2,1,0:T(8,128)(2,1)}) custom-call(bf16[64,3,16,128]{3,2,1,0:T(8,128)(2,1)} %qkv_ref.1), custom_call_target="tpu_custom_call" | custom-call | tf_op jit(solution)/shard_map/arrange/pallas_call | solution.py:47
  9.4 2.0 %join.1 = bf16[16,192,128]{2,1,0:T(8,128)(2,1)} custom-call(bf16[16,64,128]{2,1,0:T(8,128)(2,1)S(1)} %get-tuple-element.6.queries_ref, bf16[16,128,128]{2,1,0:T(8,128)(2,1)} %get-tuple-element.7.kv_ref.own_ref), custom_call_target="tpu_custom_call" | custom-call | tf_op jit(solution)/shard_map/join/pallas_call | solution.py:87
  11.4 7.4 %all-to-all-start = ((bf16[16,192,128]{2,1,0:T(8,128)(2,1)}), bf16[16,192,128]{2,1,0:T(8,128)(2,1)S(1)}, u32[]{:S(2)}, u32[]{:S(2)}) async-start(bf16[16,192,128]{2,1,0:T(8,128)(2,1)} %join.1), calls=%async_computation | async-start | bytes 1572864 | tf_op jit(solution)/shard_map/all_to_all | solution.py:289
  18.9 0.0 all-gather.3.cloned.1.call-start
  18.9 0.7 all-gather.3.cloned.1.call-update
  19.6 0.5 collective-permute-start
  20.1 0.1 pad_add_fusion.where_ref
  20.1 1.7 %collective-permute-done.core_ref = bf16[16,128,128]{2,1,0:T(8,128)(2,1)S(1)} collective-permute-done((bf16[16,128,128]{2,1,0:T(8,128)(2,1)}, bf16[16,128,128]{2,1,0:T(8,128)(2,1)S(1)}, u32[]{:S(2)}, u32[]{:S(2)}) %collective-permute-start) | collective-permute-done | bytes 524320 | tf_op jit(solution)/shard_map/ppermute | solution.py:297
  21.8 16.9 %all-gather.3.cloned.1.call-done = bf16[32,128,128]{2,1,0:T(8,128)(2,1)} async-done(((bf16[16,128,128]{2,1,0:T(8,128)(2,1)}), bf16[32,128,128]{2,1,0:T(8,128)(2,1)}) %all-gather.3.cloned.1.call-update) | async-done | bytes 1048592 | tf_op jit(solution)/shard_map/all_gather | solution.py:286
  38.7 0.0 copy-done
  38.7 0.0 copy-done.2
  38.7 0.0 copy-done.3
  38.7 0.0 copy-start.1
  38.7 1.2 %copy-done.1 = bf16[32,128,128]{2,1,0:T(8,128)(2,1)S(1)} copy-done((bf16[32,128,128]{2,1,0:T(8,128)(2,1)S(1)}, bf16[32,128,128]{2,1,0:T(8,128)(2,1)}, u32[]{:S(2)}) %copy-start.1) | copy-done | bytes 1048600
  39.9 8.4 %video.1 = bf16[512,16,128]{2,1,0:T(8,128)(2,1)} custom-call(s32[4,4]{1,0:T(4,128)S(1)} %copy-done.2, s32[4]{0:T(128)S(1)} %copy-done.3, s32[4]{0:T(128)S(1)} %pad_add_fusion.where_ref, bf16[512,16,128]{2,1,0:T(8,128)(2,1)S(1)} %copy-done, bf16[16,128,128]{2,1,0:T(8,128)(2,1)} %get-tuple-element.7.kv_ref.own_ref, ...), custom_call_target="tpu_custom_call" | custom-call | flops 536870912 | bytes 4194304 | tf_op jit(solution)/shard_map/video/pallas_call | solution.py:237
  48.3 0.0 all-to-all-done.refs_0_
  48.3 2.7 %attend.1 = bf16[16,64,128]{2,1,0:T(8,128)(2,1)} custom-call(bf16[16,192,128]{2,1,0:T(8,128)(2,1)S(1)} %all-to-all-done.refs_0_), custom_call_target="tpu_custom_call" | custom-call | flops 536870912 | bytes 1048576 | tf_op jit(solution)/shard_map/attend/pallas_call | solution.py:152
  51.0 21.3 %all_to_all.10.by_head_ref = bf16[16,64,128]{2,1,0:T(8,128)(2,1)S(1)} all-to-all(bf16[16,64,128]{2,1,0:T(8,128)(2,1)} %attend.1), channel_id=1, replica_groups=mesh['groups'=2,'seq'=16] {'seq'}, dimensions={0} | all-to-all | bytes 524288 | tf_op jit(solution)/shard_map/all_to_all | solution.py:289
  72.4 0.8 collect.1
Async XLA Ops:
  7.2 31.5 %copy-start = (bf16[512,16,128]{2,1,0:T(8,128)(2,1)S(1)}, bf16[512,16,128]{2,1,0:T(8,128)(2,1)}, u32[]{:S(2)}) copy-start(bf16[512,16,128]{2,1,0:T(8,128)(2,1)} %video_ref.1) | copy-start | bytes 6291460
  7.2 31.5 %copy-start.2 = (s32[4,4]{1,0:T(4,128)S(1)}, s32[4,4]{1,0:T(4,128)}, u32[]{:S(2)}) copy-start(s32[4,4]{1,0:T(4,128)} %pairs_ref.1) | copy-start | bytes 196
  7.2 31.5 %copy-start.3 = (s32[4]{0:T(128)S(1)}, s32[4]{0:T(128)}, u32[]{:S(2)}) copy-start(s32[4]{0:T(128)} %counts_ref.1) | copy-start | bytes 52
  11.4 36.8 %all-to-all-start = ((bf16[16,192,128]{2,1,0:T(8,128)(2,1)}), bf16[16,192,128]{2,1,0:T(8,128)(2,1)S(1)}, u32[]{:S(2)}, u32[]{:S(2)}) async-start(bf16[16,192,128]{2,1,0:T(8,128)(2,1)} %join.1), calls=%async_computation | async-start | bytes 1572864 | tf_op jit(solution)/shard_map/all_to_all | solution.py:289
  18.9 19.8 %all-gather.3.cloned.1.call-start = ((), (), s32[]{:S(2)}) async-start(), calls=%async_computation.2 | async-start | bytes 1572864 | tf_op jit(solution)/shard_map/all_gather | solution.py:286
  19.6 2.2 %collective-permute-start = (bf16[16,128,128]{2,1,0:T(8,128)(2,1)}, bf16[16,128,128]{2,1,0:T(8,128)(2,1)S(1)}, u32[]{:S(2)}, u32[]{:S(2)}) collective-permute-start(bf16[16,128,128]{2,1,0:T(8,128)(2,1)} %get-tuple-element.7.kv_ref.own_ref), channel_id=1, source_target_pairs={{0,1},{1,0},{2,3},{3,2},{4,5},{5,4},{6,7},{7,6},{8,9},{9,8},{10,11... | collective-permute-start | bytes 1572872 | tf_op jit(solution)/shard_map/ppermute | solution.py:297
  38.7 1.2 %copy-start.1 = (bf16[32,128,128]{2,1,0:T(8,128)(2,1)S(1)}, bf16[32,128,128]{2,1,0:T(8,128)(2,1)}, u32[]{:S(2)}) copy-start(bf16[32,128,128]{2,1,0:T(8,128)(2,1)} %all-gather.3.cloned.1.call-done) | copy-start | bytes 3145732
Sparse Core Ops, SparseCore 0:
  21.2 17.3 all-gather.2

commit v6 on v4

--- a/solution.py
+++ b/solution.py
@@ -91,6 +91,7 @@
         out_shape=pltpu.HBM((heads, rows + kv.shape[1], size), queries.dtype),
         scratch_shapes=[pltpu.SemaphoreType.DMA((2 * pieces,))],
         compiler_params=params(),
+        cost_estimate=pl.CostEstimate(flops=0, bytes_accessed=64 * 1024 * 1024, transcendentals=0),
         name="join",
     )(queries, kv)
 
@@ -253,7 +254,7 @@
         out_shape=jax.ShapeDtypeStruct(video_q.shape, jnp.bfloat16),
         compiler_params=params(),
         cost_estimate=pl.CostEstimate(
-            flops=4 * work * size, bytes_accessed=4 * total * heads * size, transcendentals=work
+            flops=4 * work * size, bytes_accessed=160 * total * heads * size, transcendentals=work
         ),
         name="video",
     )(pairs, counts, where, video_q, own, core, chip)

time: 62.5 us -> 62.5 us (level)
  no operation moved by 1% of the time
where the time goes in v6:
time: 62.5 us; the launch traced here: 62.1 us
  blocking collectives  29.5 us (47%)
  Pallas kernels  14.4 us (23%)
  starting transfers between devices  9.27 us (15%)
  waiting for transfers between devices  8.22 us (13%)
  between operations  0.7 us (1%)
    all_to_all x1, blocking collectives, exchange(): return lax.all_to_all(value, 'seq', split_axis=0, concat_axis=0, tiled=True)  29.5 us
    pallas_call x1, Pallas kernels, video(): pl.pallas_call(functools.partial(video_kernel, rows, slots, scale, 4), gr...  8.53 us
    all_to_all x1, waiting for transfers between devices, exchange(): return lax.all_to_all(value, 'seq', split_axis=0, concat_axis=0, tiled=True)  8.05 us
    all_to_all x1, starting transfers between devices, exchange(): return lax.all_to_all(value, 'seq', split_axis=0, concat_axis=0, tiled=True)  7.4 us
    pallas_call x1, Pallas kernels, attend(): pl.pallas_call(functools.partial(attend_kernel, query_rows, rows, scale,...  2.72 us
    ppermute x1, starting transfers between devices, local(): chip = lax.ppermute(kv, 'seq', chip_pairs)  1.46 us
    pallas_call x1, Pallas kernels, arrange(): pl.pallas_call(functools.partial(arrange_kernel, rows, pieces), in_specs=...  1.45 us
  transfers between devices with their start and end apart: 3, of which 2 were waited for; matrix products, arithmetic and copies ran while one was open for 0% of the time, Pallas kernels for 14%

profile of v6, /device:TPU:0, one launch (start us, length us, event | category | flops | bytes accessed | tf_op | source)
XLA Modules:
  0.0 62.1 jit_solution(6675372292579497471)
XLA Ops:
  0.6 0.0 copy-start
  0.6 0.0 copy-start.1
  0.7 0.0 copy-start.2
  0.7 1.5 %arrange.1 = (bf16[16,64,128]{2,1,0:T(8,128)(2,1)S(1)}, bf16[16,128,128]{2,1,0:T(8,128)(2,1)S(1)}) custom-call(bf16[64,3,16,128]{3,2,1,0:T(8,128)(2,1)} %qkv_ref.1), custom_call_target="tpu_custom_call" | custom-call | tf_op jit(solution)/shard_map/arrange/pallas_call | solution.py:47
  2.1 0.9 %join.1 = bf16[16,192,128]{2,1,0:T(8,128)(2,1)} custom-call(bf16[16,64,128]{2,1,0:T(8,128)(2,1)S(1)} %get-tuple-element.6.queries_ref, bf16[16,128,128]{2,1,0:T(8,128)(2,1)S(1)} %get-tuple-element.7.kv_ref.own_ref), custom_call_target="tpu_custom_call" | custom-call | bytes 67108864 | tf_op jit(solution)/shard_map/join/pallas_call | solution.py:87
  3.1 7.4 %all-to-all-start = ((bf16[16,192,128]{2,1,0:T(8,128)(2,1)}), bf16[16,192,128]{2,1,0:T(8,128)(2,1)S(1)}, u32[]{:S(2)}, u32[]{:S(2)}) async-start(bf16[16,192,128]{2,1,0:T(8,128)(2,1)} %join.1), calls=%async_computation | async-start | bytes 1572864 | tf_op jit(solution)/shard_map/all_to_all | solution.py:276
  10.5 0.4 collective-permute-start
  10.9 1.5 %collective-permute-start.1 = (bf16[16,128,128]{2,1,0:T(8,128)(2,1)S(1)}, bf16[16,128,128]{2,1,0:T(8,128)(2,1)}, u32[]{:S(2)}, u32[]{:S(2)}) collective-permute-start(bf16[16,128,128]{2,1,0:T(8,128)(2,1)S(1)} %get-tuple-element.7.kv_ref.own_ref), channel_id=1, source_target_pairs={{1,2},{2,1},{3,4},{4,3},{5,6},{6,5},{7,8},{8,7},{9,10},{10,9},{11,... | collective-permute-start | bytes 1572872 | tf_op jit(solution)/shard_map/ppermute | solution.py:273
  12.3 0.1 pad_add_fusion.where_ref
  12.4 0.2 collective-permute-done.core_ref
  12.6 0.0 collective-permute-done.1.chip_ref
  12.6 0.0 copy-done
  12.6 0.0 copy-done.1
  12.6 0.0 copy-done.2
  12.6 8.5 %video.1 = bf16[512,16,128]{2,1,0:T(8,128)(2,1)} custom-call(s32[4,4]{1,0:T(4,128)S(1)} %copy-done.1, s32[4]{0:T(128)S(1)} %copy-done.2, s32[3]{0:T(128)S(1)} %pad_add_fusion.where_ref, bf16[512,16,128]{2,1,0:T(8,128)(2,1)S(1)} %copy-done, bf16[16,128,128]{2,1,0:T(8,128)(2,1)S(1)} %get-tuple-element.7.kv_ref.own_ref, ...), custom_call_target="tpu_custom_call" | custom-call | flops 536870912 | bytes 167772160 | tf_op jit(solution)/shard_map/video/pallas_call | solution.py:238
  21.1 8.1 %all-to-all-done.refs_0_ = bf16[16,192,128]{2,1,0:T(8,128)(2,1)S(1)} async-done(((bf16[16,192,128]{2,1,0:T(8,128)(2,1)}), bf16[16,192,128]{2,1,0:T(8,128)(2,1)S(1)}, u32[]{:S(2)}, u32[]{:S(2)}) %all-to-all-start) | async-done | bytes 786464 | tf_op jit(solution)/shard_map/all_to_all | solution.py:276
  29.2 2.7 %attend.1 = bf16[16,64,128]{2,1,0:T(8,128)(2,1)} custom-call(bf16[16,192,128]{2,1,0:T(8,128)(2,1)S(1)} %all-to-all-done.refs_0_), custom_call_target="tpu_custom_call" | custom-call | flops 536870912 | bytes 1048576 | tf_op jit(solution)/shard_map/attend/pallas_call | solution.py:153
  31.9 29.5 %all_to_all.10.by_head_ref = bf16[16,64,128]{2,1,0:T(8,128)(2,1)S(1)} all-to-all(bf16[16,64,128]{2,1,0:T(8,128)(2,1)} %attend.1), channel_id=1, replica_groups=mesh['groups'=2,'seq'=16] {'seq'}, dimensions={0} | all-to-all | bytes 524288 | tf_op jit(solution)/shard_map/all_to_all | solution.py:276
  61.4 0.8 %collect.1 = bf16[64,16,128]{2,1,0:T(8,128)(2,1)} custom-call(bf16[16,64,128]{2,1,0:T(8,128)(2,1)S(1)} %all_to_all.10.by_head_ref), custom_call_target="tpu_custom_call" | custom-call | tf_op jit(solution)/shard_map/collect/pallas_call | solution.py:176
Async XLA Ops:
  0.6 12.0 %copy-start = (bf16[512,16,128]{2,1,0:T(8,128)(2,1)S(1)}, bf16[512,16,128]{2,1,0:T(8,128)(2,1)}, u32[]{:S(2)}) copy-start(bf16[512,16,128]{2,1,0:T(8,128)(2,1)} %video_ref.1) | copy-start | bytes 6291460
  0.6 11.9 %copy-start.1 = (s32[4,4]{1,0:T(4,128)S(1)}, s32[4,4]{1,0:T(4,128)}, u32[]{:S(2)}) copy-start(s32[4,4]{1,0:T(4,128)} %pairs_ref.1) | copy-start | bytes 196
  0.7 11.9 %copy-start.2 = (s32[4]{0:T(128)S(1)}, s32[4]{0:T(128)}, u32[]{:S(2)}) copy-start(s32[4]{0:T(128)} %counts_ref.1) | copy-start | bytes 52
  3.1 26.1 %all-to-all-start = ((bf16[16,192,128]{2,1,0:T(8,128)(2,1)}), bf16[16,192,128]{2,1,0:T(8,128)(2,1)S(1)}, u32[]{:S(2)}, u32[]{:S(2)}) async-start(bf16[16,192,128]{2,1,0:T(8,128)(2,1)} %join.1), calls=%async_computation | async-start | bytes 1572864 | tf_op jit(solution)/shard_map/all_to_all | solution.py:276
  10.5 2.1 %collective-permute-start = (bf16[16,128,128]{2,1,0:T(8,128)(2,1)S(1)}, bf16[16,128,128]{2,1,0:T(8,128)(2,1)}, u32[]{:S(2)}, u32[]{:S(2)}) collective-permute-start(bf16[16,128,128]{2,1,0:T(8,128)(2,1)S(1)} %get-tuple-element.7.kv_ref.own_ref), channel_id=1, source_target_pairs={{0,1},{1,0},{2,3},{3,2},{4,5},{5,4},{6,7},{7,6},{8,9},{9,8},{10,11... | collective-permute-start | bytes 1572872 | tf_op jit(solution)/shard_map/ppermute | solution.py:284
  10.9 1.7 %collective-permute-start.1 = (bf16[16,128,128]{2,1,0:T(8,128)(2,1)S(1)}, bf16[16,128,128]{2,1,0:T(8,128)(2,1)}, u32[]{:S(2)}, u32[]{:S(2)}) collective-permute-start(bf16[16,128,128]{2,1,0:T(8,128)(2,1)S(1)} %get-tuple-element.7.kv_ref.own_ref), channel_id=1, source_target_pairs={{1,2},{2,1},{3,4},{4,3},{5,6},{6,5},{7,8},{8,7},{9,10},{10,9},{11,... | collective-permute-start | bytes 1572872 | tf_op jit(solution)/shard_map/ppermute | solution.py:273

commit v7 on v4

--- a/solution.py
+++ b/solution.py
@@ -253,7 +253,7 @@
         out_shape=jax.ShapeDtypeStruct(video_q.shape, jnp.bfloat16),
         compiler_params=params(),
         cost_estimate=pl.CostEstimate(
-            flops=4 * work * size, bytes_accessed=4 * total * heads * size, transcendentals=work
+            flops=4 * work * size, bytes_accessed=32 * total * heads * size, transcendentals=work
         ),
         name="video",
     )(pairs, counts, where, video_q, own, core, chip)
@@ -287,9 +287,9 @@
     video_cross = video(
         video_q, kv, core, chip, pairs, counts, where.astype(jnp.int32), scale
     )
-    operands, video_cross = lax.optimization_barrier((operands, video_cross))
     head_out = attend(operands, devices, band_rows, rows, size, scale)
-    audio_attn = collect(exchange(head_out).reshape(heads, rows, size))
+    returned, video_cross = lax.optimization_barrier((exchange(head_out), video_cross))
+    audio_attn = collect(returned.reshape(heads, rows, size))
     return audio_attn, video_cross
 
 

time: 62.5 us -> 48.7 us (0.78)
  blocking collectives: 29.4 us -> 0 us
  starting transfers between devices: 9.27 us -> 17.2 us
  waiting for transfers between devices: 8.2 us -> 16.1 us
    all_to_all x1 -> x0, blocking collectives: 29.4 us -> none  [exchange(): return lax.all_to_all(value, 'seq', split_axis=0, concat_axis=0, tiled=True)]
    all_to_all x1 -> x2, waiting for transfers between devices: 8.04 us -> 16.1 us  [exchange(): return lax.all_to_all(value, 'seq', split_axis=0, concat_axis=0, tiled=True)]
    all_to_all x1 -> x2, starting transfers between devices: 7.4 us -> 13.1 us  [exchange(): return lax.all_to_all(value, 'seq', split_axis=0, concat_axis=0, tiled=True)]
    ppermute x1, starting transfers between devices: 0.41 us -> 2.56 us  [local(): core = lax.ppermute(kv, 'seq', core_pairs)]
  transfers between devices with their start and end apart: 3 -> 4, of which waited for: 2 -> 2; matrix products, arithmetic and copies ran while one was open for 0% -> 0% of each run, Pallas kernels for 14% -> 23%
where the time goes in v7:
time: 48.7 us; the launch traced here: 48.3 us
  starting transfers between devices  17.2 us (35%)
  waiting for transfers between devices  16.1 us (33%)
  Pallas kernels  14.2 us (29%)
  between operations  0.72 us (1%)
    all_to_all x2, waiting for transfers between devices, exchange(): return lax.all_to_all(value, 'seq', split_axis=0, concat_axis=0, tiled=True)  16.1 us
    all_to_all x2, starting transfers between devices, exchange(): return lax.all_to_all(value, 'seq', split_axis=0, concat_axis=0, tiled=True)  13.1 us
    pallas_call x1, Pallas kernels, video(): pl.pallas_call(functools.partial(video_kernel, rows, slots, scale, 4), gr...  8.52 us
    pallas_call x1, Pallas kernels, attend(): pl.pallas_call(functools.partial(attend_kernel, query_rows, rows, scale,...  2.72 us
    ppermute x1, starting transfers between devices, local(): core = lax.ppermute(kv, 'seq', core_pairs)  2.56 us
    ppermute x1, starting transfers between devices, local(): chip = lax.ppermute(kv, 'seq', chip_pairs)  1.45 us
    pallas_call x1, Pallas kernels, arrange(): pl.pallas_call(functools.partial(arrange_kernel, rows, pieces), in_specs=...  1.32 us
  transfers between devices with their start and end apart: 4, of which 2 were waited for; matrix products, arithmetic and copies ran while one was open for 0% of the time, Pallas kernels for 23%

profile of v7, /device:TPU:0, one launch (start us, length us, event | category | flops | bytes accessed | tf_op | source)
XLA Modules:
  0.0 48.3 jit_solution(7693563211296080238)
XLA Ops:
  0.6 1.3 %arrange.1 = (bf16[16,64,128]{2,1,0:T(8,128)(2,1)S(1)}, bf16[16,128,128]{2,1,0:T(8,128)(2,1)S(1)}) custom-call(bf16[64,3,16,128]{3,2,1,0:T(8,128)(2,1)} %qkv_ref.1), custom_call_target="tpu_custom_call" | custom-call | tf_op jit(solution)/shard_map/arrange/pallas_call | solution.py:47
  2.0 0.9 %join.1 = bf16[16,192,128]{2,1,0:T(8,128)(2,1)} custom-call(bf16[16,64,128]{2,1,0:T(8,128)(2,1)S(1)} %get-tuple-element.6.queries_ref, bf16[16,128,128]{2,1,0:T(8,128)(2,1)S(1)} %get-tuple-element.7.kv_ref.own_ref), custom_call_target="tpu_custom_call" | custom-call | tf_op jit(solution)/shard_map/join/pallas_call | solution.py:87
  2.9 0.0 copy-start
  2.9 0.0 copy-start.1
  2.9 0.0 copy-start.2
  2.9 7.5 %all-to-all-start = ((bf16[16,192,128]{2,1,0:T(8,128)(2,1)}), bf16[16,192,128]{2,1,0:T(8,128)(2,1)S(1)}, u32[]{:S(2)}, u32[]{:S(2)}) async-start(bf16[16,192,128]{2,1,0:T(8,128)(2,1)} %join.1), calls=%async_computation | async-start | bytes 1572864 | tf_op jit(solution)/shard_map/all_to_all | solution.py:275
  10.4 1.5 %collective-permute-start.1 = (bf16[16,128,128]{2,1,0:T(8,128)(2,1)S(1)}, bf16[16,128,128]{2,1,0:T(8,128)(2,1)}, u32[]{:S(2)}, u32[]{:S(2)}) collective-permute-start(bf16[16,128,128]{2,1,0:T(8,128)(2,1)S(1)} %get-tuple-element.7.kv_ref.own_ref), channel_id=1, source_target_pairs={{1,2},{2,1},{3,4},{4,3},{5,6},{6,5},{7,8},{8,7},{9,10},{10,9},{11,... | collective-permute-start | bytes 1572872 | tf_op jit(solution)/shard_map/ppermute | solution.py:272
  11.9 2.6 %collective-permute-start = (bf16[16,128,128]{2,1,0:T(8,128)(2,1)S(1)}, bf16[16,128,128]{2,1,0:T(8,128)(2,1)}, u32[]{:S(2)}, u32[]{:S(2)}) collective-permute-start(bf16[16,128,128]{2,1,0:T(8,128)(2,1)S(1)} %get-tuple-element.7.kv_ref.own_ref), channel_id=1, source_target_pairs={{0,1},{1,0},{2,3},{3,2},{4,5},{5,4},{6,7},{7,6},{8,9},{9,8},{10,11... | collective-permute-start | bytes 1572872 | tf_op jit(solution)/shard_map/ppermute | solution.py:283
  14.5 14.7 %all-to-all-done.refs_0_ = bf16[16,192,128]{2,1,0:T(8,128)(2,1)S(1)} async-done(((bf16[16,192,128]{2,1,0:T(8,128)(2,1)}), bf16[16,192,128]{2,1,0:T(8,128)(2,1)S(1)}, u32[]{:S(2)}, u32[]{:S(2)}) %all-to-all-start) | async-done | bytes 786464 | tf_op jit(solution)/shard_map/all_to_all | solution.py:275
  29.2 2.7 %attend.1 = bf16[16,64,128]{2,1,0:T(8,128)(2,1)} custom-call(bf16[16,192,128]{2,1,0:T(8,128)(2,1)S(1)} %all-to-all-done.refs_0_), custom_call_target="tpu_custom_call" | custom-call | flops 536870912 | bytes 1048576 | tf_op jit(solution)/shard_map/attend/pallas_call | solution.py:152
  31.9 5.6 %all-to-all-start.1 = ((bf16[16,64,128]{2,1,0:T(8,128)(2,1)}), bf16[16,64,128]{2,1,0:T(8,128)(2,1)S(1)}, u32[]{:S(2)}, u32[]{:S(2)}) async-start(bf16[16,64,128]{2,1,0:T(8,128)(2,1)} %attend.1), calls=%async_computation.1 | async-start | bytes 524288 | tf_op jit(solution)/shard_map/all_to_all | solution.py:275
  37.5 0.1 pad_add_fusion.where_ref
  37.6 0.0 collective-permute-done.1.chip_ref
  37.6 0.0 collective-permute-done.core_ref
  37.6 0.0 copy-done
  37.6 0.0 copy-done.1
  37.6 0.0 copy-done.2
  37.6 8.5 %video.1 = bf16[512,16,128]{2,1,0:T(8,128)(2,1)} custom-call(s32[4,4]{1,0:T(4,128)S(1)} %copy-done.1, s32[4]{0:T(128)S(1)} %copy-done.2, s32[3]{0:T(128)S(1)} %pad_add_fusion.where_ref, bf16[512,16,128]{2,1,0:T(8,128)(2,1)S(1)} %copy-done, bf16[16,128,128]{2,1,0:T(8,128)(2,1)S(1)} %get-tuple-element.7.kv_ref.own_ref, ...), custom_call_target="tpu_custom_call" | custom-call | flops 536870912 | bytes 33554432 | tf_op jit(solution)/shard_map/video/pallas_call | solution.py:237
  46.1 1.4 %all-to-all-done.1.by_head_ref = bf16[16,64,128]{2,1,0:T(8,128)(2,1)S(1)} async-done(((bf16[16,64,128]{2,1,0:T(8,128)(2,1)}), bf16[16,64,128]{2,1,0:T(8,128)(2,1)S(1)}, u32[]{:S(2)}, u32[]{:S(2)}) %all-to-all-start.1) | async-done | bytes 262176 | tf_op jit(solution)/shard_map/all_to_all | solution.py:275
  47.6 0.8 %collect.1 = bf16[64,16,128]{2,1,0:T(8,128)(2,1)} custom-call(bf16[16,64,128]{2,1,0:T(8,128)(2,1)S(1)} %all-to-all-done.1.by_head_ref), custom_call_target="tpu_custom_call" | custom-call | tf_op jit(solution)/shard_map/collect/pallas_call | solution.py:175
Async XLA Ops:
  2.9 34.7 %copy-start = (bf16[512,16,128]{2,1,0:T(8,128)(2,1)S(1)}, bf16[512,16,128]{2,1,0:T(8,128)(2,1)}, u32[]{:S(2)}) copy-start(bf16[512,16,128]{2,1,0:T(8,128)(2,1)} %video_ref.1) | copy-start | bytes 6291460
  2.9 34.7 %copy-start.1 = (s32[4,4]{1,0:T(4,128)S(1)}, s32[4,4]{1,0:T(4,128)}, u32[]{:S(2)}) copy-start(s32[4,4]{1,0:T(4,128)} %pairs_ref.1) | copy-start | bytes 196
  2.9 34.7 %copy-start.2 = (s32[4]{0:T(128)S(1)}, s32[4]{0:T(128)}, u32[]{:S(2)}) copy-start(s32[4]{0:T(128)} %counts_ref.1) | copy-start | bytes 52
  2.9 26.2 %all-to-all-start = ((bf16[16,192,128]{2,1,0:T(8,128)(2,1)}), bf16[16,192,128]{2,1,0:T(8,128)(2,1)S(1)}, u32[]{:S(2)}, u32[]{:S(2)}) async-start(bf16[16,192,128]{2,1,0:T(8,128)(2,1)} %join.1), calls=%async_computation | async-start | bytes 1572864 | tf_op jit(solution)/shard_map/all_to_all | solution.py:275
  10.4 27.1 %collective-permute-start.1 = (bf16[16,128,128]{2,1,0:T(8,128)(2,1)S(1)}, bf16[16,128,128]{2,1,0:T(8,128)(2,1)}, u32[]{:S(2)}, u32[]{:S(2)}) collective-permute-start(bf16[16,128,128]{2,1,0:T(8,128)(2,1)S(1)} %get-tuple-element.7.kv_ref.own_ref), channel_id=1, source_target_pairs={{1,2},{2,1},{3,4},{4,3},{5,6},{6,5},{7,8},{8,7},{9,10},{10,9},{11,... | collective-permute-start | bytes 1572872 | tf_op jit(solution)/shard_map/ppermute | solution.py:272
  11.9 25.7 %collective-permute-start = (bf16[16,128,128]{2,1,0:T(8,128)(2,1)S(1)}, bf16[16,128,128]{2,1,0:T(8,128)(2,1)}, u32[]{:S(2)}, u32[]{:S(2)}) collective-permute-start(bf16[16,128,128]{2,1,0:T(8,128)(2,1)S(1)} %get-tuple-element.7.kv_ref.own_ref), channel_id=1, source_target_pairs={{0,1},{1,0},{2,3},{3,2},{4,5},{5,4},{6,7},{7,6},{8,9},{9,8},{10,11... | collective-permute-start | bytes 1572872 | tf_op jit(solution)/shard_map/ppermute | solution.py:283
  31.9 15.7 %all-to-all-start.1 = ((bf16[16,64,128]{2,1,0:T(8,128)(2,1)}), bf16[16,64,128]{2,1,0:T(8,128)(2,1)S(1)}, u32[]{:S(2)}, u32[]{:S(2)}) async-start(bf16[16,64,128]{2,1,0:T(8,128)(2,1)} %attend.1), calls=%async_computation.1 | async-start | bytes 524288 | tf_op jit(solution)/shard_map/all_to_all | solution.py:275

commit v8 on v3

v8 whole, which is shorter than its diff:
```python
import functools

import jax
import jax.numpy as jnp
from jax import lax
from jax.experimental import pallas as pl
from jax.experimental.pallas import tpu as pltpu
from jax.sharding import PartitionSpec as P

ABLK = 32
VBLK = 128
LOG2E = 1.4426950408889634
LOWEST = -1e30
VMEM_LIMIT = 48 * 1024 * 1024


def params():
    return pltpu.CompilerParams(vmem_limit_bytes=VMEM_LIMIT)


def whole(shape):
    return pl.BlockSpec(shape, lambda *unused: (0,) * len(shape))


PIECE = 16


def arrange_kernel(pieces, qkv_ref, send_ref, kv_ref, came, turned, in_sems, out_sems):
    rows = pieces * PIECE
    arrivals = [
        pltpu.make_async_copy(
            qkv_ref.at[pl.ds(piece * PIECE, PIECE)], came.at[piece], in_sems.at[piece]
        )
        for piece in range(pieces)
    ]
    for arrival in arrivals:
        arrival.start()
    departures = []
    for piece, arrival in enumerate(arrivals):
        arrival.wait()
        for part in range(3):
            by_head = jnp.swapaxes(came[piece, :, part], 0, 1)
            turned[piece, :, part * PIECE : (part + 1) * PIECE] = by_head
            if part:
                at = (part - 1) * rows + piece * PIECE
                kv_ref[:, at : at + PIECE] = by_head
        departure = pltpu.make_async_copy(
            turned.at[piece], send_ref.at[:, piece], out_sems.at[piece]
        )
        departure.start()
        departures.append(departure)
    for departure in departures:
        departure.wait()


def arrange(audio_qkv):
    rows, parts, heads, size = audio_qkv.shape
    dtype = audio_qkv.dtype
    pieces = rows // PIECE
    return pl.pallas_call(
        functools.partial(arrange_kernel, pieces),
        in_specs=[pl.BlockSpec(memory_space=pltpu.HBM)],
        out_specs=(
            pl.BlockSpec(memory_space=pltpu.HBM),
            pl.BlockSpec(memory_space=pltpu.VMEM),
        ),
        out_shape=(
            pltpu.HBM((heads, pieces, parts * PIECE, size), dtype),
            jax.ShapeDtypeStruct((heads, 2 * rows, size), dtype),
        ),
        scratch_shapes=[
            pltpu.VMEM((pieces, PIECE, parts, heads, size), dtype),
            pltpu.VMEM((pieces, heads, parts * PIECE, size), dtype),
            pltpu.SemaphoreType.DMA((pieces,)),
            pltpu.SemaphoreType.DMA((pieces,)),
        ],
        compiler_params=params(),
        name="arrange",
    )(pltpu.with_memory_space_constraint(audio_qkv, pltpu.HBM))


def scores_of(queries, keys):
    return lax.dot_general(
        queries, keys, (((1,), (1,)), ((), ())), preferred_element_type=jnp.float32
    )


def attend_kernel(scale, recv_ref, out_ref, held, sems):
    sources, pieces, unused, size = recv_ref.shape
    total = sources * pieces * PIECE
    chunk = total // sems.shape[0]
    group = chunk // (pieces * PIECE)
    factor = scale * LOG2E
    keys = recv_ref[:, :, PIECE : 2 * PIECE].reshape(total, size)
    values = recv_ref[:, :, 2 * PIECE :].reshape(total, size)
    chunks = total // chunk
    scores, weights, sums, departures = {}, {}, {}, []
    for step in range(chunks + 2):
        if step < chunks:
            first = step * group
            queries = recv_ref[first : first + group, :, :PIECE].reshape(chunk, size)
            scores[step] = scores_of(queries, keys)
        if 0 <= step - 1 < chunks:
            now = scores.pop(step - 1)
            top = jnp.max(now, axis=1, keepdims=True)
            exact = jnp.exp2((now - top) * factor)
            sums[step - 1] = jnp.sum(exact, axis=1, keepdims=True)
            weights[step - 1] = exact.astype(jnp.bfloat16)
        if step >= 2:
            summed = jnp.dot(
                weights.pop(step - 2), values, preferred_element_type=jnp.float32
            )
            result = (summed / sums.pop(step - 2)).astype(jnp.bfloat16)
            at = (step - 2) * group
            held[at : at + group] = result.reshape(group, pieces * PIECE, size)
            departure = pltpu.make_async_copy(
                held.at[pl.ds(at, group)], out_ref.at[pl.ds(at, group)], sems.at[step - 2]
            )
            departure.start()
            departures.append(departure)
    for departure in departures:
        departure.wait()


def attend(recv, scale):
    sources, pieces, unused, size = recv.shape
    rows = pieces * PIECE
    total = sources * rows
    return pl.pallas_call(
        functools.partial(attend_kernel, scale),
        in_specs=[pl.BlockSpec(memory_space=pltpu.VMEM)],
        out_specs=pl.BlockSpec(memory_space=pltpu.HBM),
        out_shape=pltpu.HBM((sources, rows, size), jnp.bfloat16),
        scratch_shapes=[
            pltpu.VMEM((sources, rows, size), jnp.bfloat16),
            pltpu.SemaphoreType.DMA((total // 128,)),
        ],
        compiler_params=params(),
        cost_estimate=pl.CostEstimate(
            flops=4 * total * total * size, bytes_accessed=8 * total * size,
            transcendentals=total * total,
        ),
        name="attend",
    )(recv)


def attend_band_kernel(query_rows, scale, query_ref, recv_ref, out_ref):
    sources, both, size = recv_ref.shape
    rows = both // 2
    group = 256 // query_rows
    factor = scale * LOG2E
    for first in range(0, sources, group):
        queries = query_ref[first : first + group].reshape(group * query_rows, size)

        def advance(step, state):
            top, total, summed = state
            at = pl.ds(step * PIECE, PIECE)
            keys = recv_ref[at, :rows].reshape(PIECE * rows, size)
            values = recv_ref[at, rows:].reshape(PIECE * rows, size)
            scores = scores_of(queries, keys)
            new_top = jnp.maximum(top, jnp.max(scores, axis=1, keepdims=True))
            weights = jnp.exp2((scores - new_top) * factor)
            rescale = jnp.exp2((top - new_top) * factor)
            new_total = total * rescale + jnp.sum(weights, axis=1, keepdims=True)
            new_summed = summed * rescale + jnp.dot(
                weights.astype(jnp.bfloat16), values, preferred_element_type=jnp.float32
            )
            return new_top, new_total, new_summed

        start = (
            jnp.full((group * query_rows, 1), LOWEST, jnp.float32),
            jnp.zeros((group * query_rows, 1), jnp.float32),
            jnp.zeros((group * query_rows, size), jnp.float32),
        )
        state = lax.fori_loop(0, sources // PIECE, advance, start)
        result = (state[2] / state[1]).astype(jnp.bfloat16)
        out_ref[first : first + group] = result.reshape(group, query_rows, size)


def attend_band(queries, recv, scale):
    return pl.pallas_call(
        functools.partial(attend_band_kernel, queries.shape[1], scale),
        out_shape=jax.ShapeDtypeStruct(queries.shape, jnp.bfloat16),
        compiler_params=params(),
        name="attend_band",
    )(queries, recv)


def collect_kernel(by_head_ref, out_ref, turned, sems):
    departures = []
    for piece in range(by_head_ref.shape[1] // PIECE):
        at = pl.ds(piece * PIECE, PIECE)
        turned[at] = jnp.swapaxes(by_head_ref[:, at], 0, 1)
        departure = pltpu.make_async_copy(turned.at[at], out_ref.at[at], sems.at[piece])
        departure.start()
        departures.append(departure)
    for departure in departures:
        departure.wait()


def collect(by_head):
    heads, rows, size = by_head.shape
    return pl.pallas_call(
        collect_kernel,
        in_specs=[pl.BlockSpec(memory_space=pltpu.VMEM)],
        out_specs=pl.BlockSpec(memory_space=pltpu.HBM),
        out_shape=pltpu.HBM((rows, heads, size), by_head.dtype),
        scratch_shapes=[
            pltpu.VMEM((rows, heads, size), by_head.dtype),
            pltpu.SemaphoreType.DMA((rows // PIECE,)),
        ],
        compiler_params=params(),
        name="collect",
    )(by_head)


def video_kernel(
    rows, slots, scale, group, pairs_ref, counts_ref, where_ref,
    video_ref, own_ref, core_ref, chip_ref, out_ref,
    near_keys, near_values, keys_ref, values_ref, queries_ref, result_ref,
):
    block = pl.program_id(0)
    heads, unused, size = own_ref.shape

    @pl.when(block == 0)
    def _():
        for ref, place in ((own_ref, rows), (core_ref, where_ref[1]), (chip_ref, where_ref[2])):
            at = pl.ds(pl.multiple_of(place, rows), rows)
            near_keys[:, at] = ref[:, :rows]
            near_values[:, at] = ref[:, rows:]
        values_ref[:, :, size:] = jnp.ones((heads, slots * ABLK, size), jnp.bfloat16)

    queries_ref[...] = jnp.swapaxes(video_ref[...], 0, 1)
    for slot in range(slots):
        start = pl.multiple_of((pairs_ref[block, slot] - where_ref[0]) * ABLK, ABLK)
        here = slice(slot * ABLK, (slot + 1) * ABLK)
        keys_ref[:, here] = near_keys[:, pl.ds(start, ABLK)]
        values_ref[:, here, :size] = near_values[:, pl.ds(start, ABLK)]
    column = lax.broadcasted_iota(jnp.int32, (VBLK, slots * ABLK), 1)
    live = column < counts_ref[block] * ABLK
    factor = scale * LOG2E
    for first in range(0, heads, group):
        members = range(first, first + group)
        scores = [
            lax.dot_general(
                queries_ref[head], keys_ref[head], (((1,), (1,)), ((), ())),
                preferred_element_type=jnp.float32,
            )
            for head in members
        ]
        scores = jnp.stack([jnp.where(live, one, LOWEST) for one in scores])
        top = jnp.max(scores, axis=2, keepdims=True)
        weights = jnp.exp2((scores - top) * factor).astype(jnp.bfloat16)
        summed = [
            jnp.dot(weights[head - first], values_ref[head], preferred_element_type=jnp.float32)
            for head in members
        ]
        for head in members:
            both = summed[head - first]
            result_ref[head] = (both[:, :size] / both[:, size:]).astype(jnp.bfloat16)
    out_ref[...] = jnp.swapaxes(result_ref[...], 0, 1)


def video(video_q, own, core, chip, pairs, counts, where, scale):
    total, heads, size = video_q.shape
    rows = own.shape[1] // 2
    slots = pairs.shape[1]
    blocks = total // VBLK
    block_spec = pl.BlockSpec((VBLK, heads, size), lambda i, *unused: (i, 0, 0))
    work = total * heads * slots * ABLK
    return pl.pallas_call(
        functools.partial(video_kernel, rows, slots, scale, 4),
        grid_spec=pltpu.PrefetchScalarGridSpec(
            num_scalar_prefetch=3,
            grid=(blocks,),
            in_specs=[block_spec] + [whole(own.shape)] * 3,
            out_specs=block_spec,
            scratch_shapes=[
                pltpu.VMEM((heads, 3 * rows, size), jnp.bfloat16),
                pltpu.VMEM((heads, 3 * rows, size), jnp.bfloat16),
                pltpu.VMEM((heads, slots * ABLK, size), jnp.bfloat16),
                pltpu.VMEM((heads, slots * ABLK, 2 * size), jnp.bfloat16),
                pltpu.VMEM((heads, VBLK, size), jnp.bfloat16),
                pltpu.VMEM((heads, VBLK, size), jnp.bfloat16),
            ],
        ),
        out_shape=jax.ShapeDtypeStruct(video_q.shape, jnp.bfloat16),
        compiler_params=params(),
        cost_estimate=pl.CostEstimate(
            flops=4 * work * size, bytes_accessed=32 * total * heads * size, transcendentals=work
        ),
        name="video",
    )(pairs, counts, where, video_q, own, core, chip)


def local(audio_qkv, video_q, pairs, counts):
    devices = lax.axis_size("seq")
    rows, unused, heads, size = audio_qkv.shape
    bands = devices // heads
    band_rows = rows // bands
    scale = size ** (-0.5)
    send, kv = arrange(audio_qkv)
    core_pairs = [(i, i ^ 1) for i in range(devices)]
    chip_pairs = [(i, ((i + 1) ^ 1) - 1) for i in range(1, devices - 1)]

    chip = lax.ppermute(kv, "seq", chip_pairs)

    def exchange(value):
        return lax.all_to_all(value, "seq", split_axis=0, concat_axis=0, tiled=True)

    core = lax.ppermute(kv, "seq", core_pairs)
    me = lax.axis_index("seq")
    odd = me & 1
    where = jnp.stack([(me - 1) * (rows // ABLK), 2 * (1 - odd) * rows, 2 * odd * rows])
    video_cross = video(
        video_q, kv, core, chip, pairs, counts, where.astype(jnp.int32), scale
    )
    if bands == 1:
        head_out = attend(exchange(send), scale)
    else:
        queries = exchange(send[:, :, :PIECE].reshape(devices, band_rows, size))
        spread = jnp.broadcast_to(kv[:, None], (heads, bands, 2 * rows, size))
        recv = exchange(spread.reshape(devices, 2 * rows, size))
        head_out = attend_band(queries, recv, scale)
    returned, video_cross = lax.optimization_barrier((exchange(head_out), video_cross))
    audio_attn = collect(returned.reshape(heads, rows, size))
    return audio_attn, video_cross


def solution(mesh):
    in_specs = (
        P(("groups", "seq"), None, None, None),
        P(("groups", "seq"), None, None),
        P(("groups", "seq"), None),
        P(("groups", "seq")),
    )
    out_specs = (P(("groups", "seq"), None, None), P(("groups", "seq"), None, None))
    return jax.shard_map(local, mesh=mesh, in_specs=in_specs, out_specs=out_specs, check_vma=False)
```

time: 62.3 us -> 48 us (0.77)
  blocking collectives: 29.5 us -> 0 us
  waiting for transfers between devices: 6.11 us -> 16.1 us
  starting transfers between devices: 11.4 us -> 17.2 us
    all_to_all x1 -> x0, blocking collectives: 29.5 us -> none  [exchange(): return lax.all_to_all(value, 'seq', split_axis=0, concat_axis=0, tiled=True)]
    all_to_all x1 -> x2, waiting for transfers between devices: 4.52 us -> 16.1 us  [exchange(): return lax.all_to_all(value, 'seq', split_axis=0, concat_axis=0, tiled=True)]
    all_to_all x1 -> x2, starting transfers between devices: 7.4 us -> 13.1 us  [exchange(): return lax.all_to_all(value, 'seq', split_axis=0, concat_axis=0, tiled=True)]
    ppermute x1, waiting for transfers between devices: 1.59 us -> 0.01 us  [local(): core = lax.ppermute(kv, 'seq', core_pairs)]
  transfers between devices with their start and end apart: 3 -> 4, of which waited for: 2 -> 2; matrix products, arithmetic and copies ran while one was open for 0% -> 0% of each run, Pallas kernels for 14% -> 23%
where the time goes in v8:
time: 48 us; the launch traced here: 47.7 us
  starting transfers between devices  17.2 us (36%)
  waiting for transfers between devices  16.1 us (34%)
  Pallas kernels  13.6 us (28%)
  between operations  0.72 us (2%)
    all_to_all x2, waiting for transfers between devices, exchange(): return lax.all_to_all(value, 'seq', split_axis=0, concat_axis=0, tiled=True)  16.1 us
    all_to_all x2, starting transfers between devices, exchange(): return lax.all_to_all(value, 'seq', split_axis=0, concat_axis=0, tiled=True)  13.1 us
    pallas_call x1, Pallas kernels, video(): pl.pallas_call(functools.partial(video_kernel, rows, slots, scale, 4), gr...  8.52 us
    ppermute x1, starting transfers between devices, local(): core = lax.ppermute(kv, 'seq', core_pairs)  2.56 us
    pallas_call x1, Pallas kernels, attend(): pl.pallas_call(functools.partial(attend_kernel, scale), in_specs=[pl.Bloc...  2.28 us
    pallas_call x1, Pallas kernels, arrange(): pl.pallas_call(functools.partial(arrange_kernel, pieces), in_specs=[pl.Bl...  2.03 us
    ppermute x1, starting transfers between devices, local(): chip = lax.ppermute(kv, 'seq', chip_pairs)  1.45 us
  transfers between devices with their start and end apart: 4, of which 2 were waited for; matrix products, arithmetic and copies ran while one was open for 0% of the time, Pallas kernels for 23%

profile of v8, /device:TPU:0, one launch (start us, length us, event | category | flops | bytes accessed | tf_op | source)
XLA Modules:
  0.0 47.7 jit_solution(15291305712102602242)
XLA Ops:
  0.6 2.0 %arrange.1 = (bf16[16,4,48,128]{3,2,1,0:T(8,128)(2,1)}, bf16[16,128,128]{2,1,0:T(8,128)(2,1)S(1)}) custom-call(bf16[64,3,16,128]{3,2,1,0:T(8,128)(2,1)} %qkv_ref.1), custom_call_target="tpu_custom_call" | custom-call | tf_op jit(solution)/shard_map/arrange/pallas_call | solution.py:60
  2.7 0.0 copy-start
  2.7 0.0 copy-start.1
  2.7 0.0 copy-start.2
  2.7 7.5 %all-to-all-start = ((bf16[16,4,48,128]{3,2,1,0:T(8,128)(2,1)}), bf16[16,4,48,128]{3,2,1,0:T(8,128)(2,1)S(1)}, u32[]{:S(2)}, u32[]{:S(2)}) async-start(bf16[16,4,48,128]{3,2,1,0:T(8,128)(2,1)} %get-tuple-element.6), calls=%async_computation | async-start | bytes 1572864 | tf_op jit(solution)/shard_map/all_to_all | solution.py:309
  10.2 1.5 %collective-permute-start.1 = (bf16[16,128,128]{2,1,0:T(8,128)(2,1)S(1)}, bf16[16,128,128]{2,1,0:T(8,128)(2,1)}, u32[]{:S(2)}, u32[]{:S(2)}) collective-permute-start(bf16[16,128,128]{2,1,0:T(8,128)(2,1)S(1)} %get-tuple-element.7.own_ref), channel_id=1, source_target_pairs={{1,2},{2,1},{3,4},{4,3},{5,6},{6,5},{7,8},{8,7},{9,10},{10,9},{11,... | collective-permute-start | bytes 1572872 | tf_op jit(solution)/shard_map/ppermute | solution.py:306
  11.7 2.6 %collective-permute-start = (bf16[16,128,128]{2,1,0:T(8,128)(2,1)S(1)}, bf16[16,128,128]{2,1,0:T(8,128)(2,1)}, u32[]{:S(2)}, u32[]{:S(2)}) collective-permute-start(bf16[16,128,128]{2,1,0:T(8,128)(2,1)S(1)} %get-tuple-element.7.own_ref), channel_id=1, source_target_pairs={{0,1},{1,0},{2,3},{3,2},{4,5},{5,4},{6,7},{7,6},{8,9},{9,8},{10,11... | collective-permute-start | bytes 1572872 | tf_op jit(solution)/shard_map/ppermute | solution.py:311
  14.3 14.7 %all-to-all-done.recv_ref = bf16[16,4,48,128]{3,2,1,0:T(8,128)(2,1)S(1)} async-done(((bf16[16,4,48,128]{3,2,1,0:T(8,128)(2,1)}), bf16[16,4,48,128]{3,2,1,0:T(8,128)(2,1)S(1)}, u32[]{:S(2)}, u32[]{:S(2)}) %all-to-all-start) | async-done | bytes 786464 | tf_op jit(solution)/shard_map/all_to_all | solution.py:309
  28.9 2.3 %attend.1 = bf16[16,64,128]{2,1,0:T(8,128)(2,1)} custom-call(bf16[16,4,48,128]{3,2,1,0:T(8,128)(2,1)S(1)} %all-to-all-done.recv_ref), custom_call_target="tpu_custom_call" | custom-call | flops 536870912 | bytes 1048576 | tf_op jit(solution)/shard_map/attend/pallas_call | solution.py:129
  31.2 5.6 %all-to-all-start.1 = ((bf16[16,64,128]{2,1,0:T(8,128)(2,1)}), bf16[16,64,128]{2,1,0:T(8,128)(2,1)S(1)}, u32[]{:S(2)}, u32[]{:S(2)}) async-start(bf16[16,64,128]{2,1,0:T(8,128)(2,1)} %attend.1), calls=%async_computation.1 | async-start | bytes 524288 | tf_op jit(solution)/shard_map/all_to_all | solution.py:309
  36.9 0.1 pad_add_fusion.where_ref
  36.9 0.0 collective-permute-done.1.chip_ref
  36.9 0.0 collective-permute-done.core_ref
  37.0 0.0 copy-done
  37.0 0.0 copy-done.1
  37.0 0.0 copy-done.2
  37.0 8.5 %video.1 = bf16[512,16,128]{2,1,0:T(8,128)(2,1)} custom-call(s32[4,4]{1,0:T(4,128)S(1)} %copy-done.1, s32[4]{0:T(128)S(1)} %copy-done.2, s32[3]{0:T(128)S(1)} %pad_add_fusion.where_ref, bf16[512,16,128]{2,1,0:T(8,128)(2,1)S(1)} %copy-done, bf16[16,128,128]{2,1,0:T(8,128)(2,1)S(1)} %get-tuple-element.7.own_ref, ...), custom_call_target="tpu_custom_call" | custom-call | flops 536870912 | bytes 33554432 | tf_op jit(solution)/shard_map/video/pallas_call | solution.py:271
  45.5 1.4 %all-to-all-done.1.by_head_ref = bf16[16,64,128]{2,1,0:T(8,128)(2,1)S(1)} async-done(((bf16[16,64,128]{2,1,0:T(8,128)(2,1)}), bf16[16,64,128]{2,1,0:T(8,128)(2,1)S(1)}, u32[]{:S(2)}, u32[]{:S(2)}) %all-to-all-start.1) | async-done | bytes 262176 | tf_op jit(solution)/shard_map/all_to_all | solution.py:309
  46.9 0.8 %collect.1 = bf16[64,16,128]{2,1,0:T(8,128)(2,1)} custom-call(bf16[16,64,128]{2,1,0:T(8,128)(2,1)S(1)} %all-to-all-done.1.by_head_ref), custom_call_target="tpu_custom_call" | custom-call | tf_op jit(solution)/shard_map/collect/pallas_call | solution.py:203
Async XLA Ops:
  2.7 34.3 %copy-start = (bf16[512,16,128]{2,1,0:T(8,128)(2,1)S(1)}, bf16[512,16,128]{2,1,0:T(8,128)(2,1)}, u32[]{:S(2)}) copy-start(bf16[512,16,128]{2,1,0:T(8,128)(2,1)} %video_ref.1) | copy-start | bytes 6291460
  2.7 34.3 %copy-start.1 = (s32[4,4]{1,0:T(4,128)S(1)}, s32[4,4]{1,0:T(4,128)}, u32[]{:S(2)}) copy-start(s32[4,4]{1,0:T(4,128)} %pairs_ref.1) | copy-start | bytes 196
  2.7 34.3 %copy-start.2 = (s32[4]{0:T(128)S(1)}, s32[4]{0:T(128)}, u32[]{:S(2)}) copy-start(s32[4]{0:T(128)} %counts_ref.1) | copy-start | bytes 52
  2.7 26.2 %all-to-all-start = ((bf16[16,4,48,128]{3,2,1,0:T(8,128)(2,1)}), bf16[16,4,48,128]{3,2,1,0:T(8,128)(2,1)S(1)}, u32[]{:S(2)}, u32[]{:S(2)}) async-start(bf16[16,4,48,128]{3,2,1,0:T(8,128)(2,1)} %get-tuple-element.6), calls=%async_computation | async-start | bytes 1572864 | tf_op jit(solution)/shard_map/all_to_all | solution.py:309
  10.2 26.7 %collective-permute-start.1 = (bf16[16,128,128]{2,1,0:T(8,128)(2,1)S(1)}, bf16[16,128,128]{2,1,0:T(8,128)(2,1)}, u32[]{:S(2)}, u32[]{:S(2)}) collective-permute-start(bf16[16,128,128]{2,1,0:T(8,128)(2,1)S(1)} %get-tuple-element.7.own_ref), channel_id=1, source_target_pairs={{1,2},{2,1},{3,4},{4,3},{5,6},{6,5},{7,8},{8,7},{9,10},{10,9},{11,... | collective-permute-start | bytes 1572872 | tf_op jit(solution)/shard_map/ppermute | solution.py:306
  11.7 25.3 %collective-permute-start = (bf16[16,128,128]{2,1,0:T(8,128)(2,1)S(1)}, bf16[16,128,128]{2,1,0:T(8,128)(2,1)}, u32[]{:S(2)}, u32[]{:S(2)}) collective-permute-start(bf16[16,128,128]{2,1,0:T(8,128)(2,1)S(1)} %get-tuple-element.7.own_ref), channel_id=1, source_target_pairs={{0,1},{1,0},{2,3},{3,2},{4,5},{5,4},{6,7},{7,6},{8,9},{9,8},{10,11... | collective-permute-start | bytes 1572872 | tf_op jit(solution)/shard_map/ppermute | solution.py:311
  31.2 15.7 %all-to-all-start.1 = ((bf16[16,64,128]{2,1,0:T(8,128)(2,1)}), bf16[16,64,128]{2,1,0:T(8,128)(2,1)S(1)}, u32[]{:S(2)}, u32[]{:S(2)}) async-start(bf16[16,64,128]{2,1,0:T(8,128)(2,1)} %attend.1), calls=%async_computation.1 | async-start | bytes 524288 | tf_op jit(solution)/shard_map/all_to_all | solution.py:309

commit v9 on v8

--- a/solution.py
+++ b/solution.py
@@ -305,8 +305,13 @@
 
     chip = lax.ppermute(kv, "seq", chip_pairs)
 
+    planes = 4
+    spread_out = [(p % planes) * (devices // planes) + p // planes for p in range(devices)]
+
     def exchange(value):
-        return lax.all_to_all(value, "seq", split_axis=0, concat_axis=0, tiled=True)
+        return lax.all_to_all(
+            value, "seq", split_axis=0, concat_axis=0, tiled=True, axis_index_groups=[spread_out]
+        )
 
     core = lax.ppermute(kv, "seq", core_pairs)
     me = lax.axis_index("seq")

time: 48 us -> 48.6 us (1.012)
  waiting for transfers between devices: 16.1 us -> 18.7 us
  starting transfers between devices: 17.2 us -> 15.1 us
    all_to_all x2, waiting for transfers between devices: 16.1 us -> 18.7 us  [exchange(): lax.all_to_all(value, 'seq', split_axis=0, concat_axis=0, tiled=True, axi...]
    all_to_all x2, starting transfers between devices: 13.1 us -> 11.1 us  [exchange(): lax.all_to_all(value, 'seq', split_axis=0, concat_axis=0, tiled=True, axi...]
  transfers between devices with their start and end apart: 4 -> 4, of which waited for: 2 -> 2; matrix products, arithmetic and copies ran while one was open for 0% -> 0% of each run, Pallas kernels for 23% -> 22%
where the time goes in v9:
time: 48.6 us; the launch traced here: 48.2 us
  waiting for transfers between devices  18.7 us (38%)
  starting transfers between devices  15.1 us (31%)
  Pallas kernels  13.6 us (28%)
  between operations  0.72 us (1%)
    all_to_all x2, waiting for transfers between devices, exchange(): lax.all_to_all(value, 'seq', split_axis=0, concat_axis=0, tiled=True, axi...  18.7 us
    all_to_all x2, starting transfers between devices, exchange(): lax.all_to_all(value, 'seq', split_axis=0, concat_axis=0, tiled=True, axi...  11.1 us
    pallas_call x1, Pallas kernels, video(): pl.pallas_call(functools.partial(video_kernel, rows, slots, scale, 4), gr...  8.51 us
    ppermute x1, starting transfers between devices, local(): core = lax.ppermute(kv, 'seq', core_pairs)  2.56 us
    pallas_call x1, Pallas kernels, attend(): pl.pallas_call(functools.partial(attend_kernel, scale), in_specs=[pl.Bloc...  2.28 us
    pallas_call x1, Pallas kernels, arrange(): pl.pallas_call(functools.partial(arrange_kernel, pieces), in_specs=[pl.Bl...  2.03 us
    ppermute x1, starting transfers between devices, local(): chip = lax.ppermute(kv, 'seq', chip_pairs)  1.45 us
  transfers between devices with their start and end apart: 4, of which 2 were waited for; matrix products, arithmetic and copies ran while one was open for 0% of the time, Pallas kernels for 22%

profile of v9, /device:TPU:0, one launch (start us, length us, event | category | flops | bytes accessed | tf_op | source)
XLA Modules:
  0.0 48.2 jit_solution(3195379372675738141)
XLA Ops:
  0.6 2.0 %arrange.1 = (bf16[16,4,48,128]{3,2,1,0:T(8,128)(2,1)}, bf16[16,128,128]{2,1,0:T(8,128)(2,1)S(1)}) custom-call(bf16[64,3,16,128]{3,2,1,0:T(8,128)(2,1)} %qkv_ref.1), custom_call_target="tpu_custom_call" | custom-call | tf_op jit(solution)/shard_map/arrange/pallas_call | solution.py:60
  2.7 0.0 copy-start
  2.7 0.0 copy-start.1
  2.7 0.0 copy-start.2
  2.7 7.5 %all-to-all-start = ((bf16[16,4,48,128]{3,2,1,0:T(8,128)(2,1)}), bf16[16,4,48,128]{3,2,1,0:T(8,128)(2,1)S(1)}, u32[]{:S(2)}, u32[]{:S(2)}) async-start(bf16[16,4,48,128]{3,2,1,0:T(8,128)(2,1)} %get-tuple-element.6), calls=%async_computation | async-start | bytes 1572864 | tf_op jit(solution)/shard_map/all_to_all | solution.py:312
  10.2 1.5 %collective-permute-start.1 = (bf16[16,128,128]{2,1,0:T(8,128)(2,1)S(1)}, bf16[16,128,128]{2,1,0:T(8,128)(2,1)}, u32[]{:S(2)}, u32[]{:S(2)}) collective-permute-start(bf16[16,128,128]{2,1,0:T(8,128)(2,1)S(1)} %get-tuple-element.7.own_ref), channel_id=1, source_target_pairs={{1,2},{2,1},{3,4},{4,3},{5,6},{6,5},{7,8},{8,7},{9,10},{10,9},{11,... | collective-permute-start | bytes 1572872 | tf_op jit(solution)/shard_map/ppermute | solution.py:306
  11.7 2.6 %collective-permute-start = (bf16[16,128,128]{2,1,0:T(8,128)(2,1)S(1)}, bf16[16,128,128]{2,1,0:T(8,128)(2,1)}, u32[]{:S(2)}, u32[]{:S(2)}) collective-permute-start(bf16[16,128,128]{2,1,0:T(8,128)(2,1)S(1)} %get-tuple-element.7.own_ref), channel_id=1, source_target_pairs={{0,1},{1,0},{2,3},{3,2},{4,5},{5,4},{6,7},{7,6},{8,9},{9,8},{10,11... | collective-permute-start | bytes 1572872 | tf_op jit(solution)/shard_map/ppermute | solution.py:316
  14.3 17.3 %all-to-all-done.recv_ref = bf16[16,4,48,128]{3,2,1,0:T(8,128)(2,1)S(1)} async-done(((bf16[16,4,48,128]{3,2,1,0:T(8,128)(2,1)}), bf16[16,4,48,128]{3,2,1,0:T(8,128)(2,1)S(1)}, u32[]{:S(2)}, u32[]{:S(2)}) %all-to-all-start) | async-done | bytes 786464 | tf_op jit(solution)/shard_map/all_to_all | solution.py:312
  31.6 2.3 %attend.1 = bf16[16,64,128]{2,1,0:T(8,128)(2,1)} custom-call(bf16[16,4,48,128]{3,2,1,0:T(8,128)(2,1)S(1)} %all-to-all-done.recv_ref), custom_call_target="tpu_custom_call" | custom-call | flops 536870912 | bytes 1048576 | tf_op jit(solution)/shard_map/attend/pallas_call | solution.py:129
  33.9 3.5 %all-to-all-start.1 = ((bf16[16,64,128]{2,1,0:T(8,128)(2,1)}), bf16[16,64,128]{2,1,0:T(8,128)(2,1)S(1)}, u32[]{:S(2)}, u32[]{:S(2)}) async-start(bf16[16,64,128]{2,1,0:T(8,128)(2,1)} %attend.1), calls=%async_computation.1 | async-start | bytes 524288 | tf_op jit(solution)/shard_map/all_to_all | solution.py:312
  37.4 0.1 pad_add_fusion.where_ref
  37.5 0.0 collective-permute-done.1.chip_ref
  37.5 0.0 collective-permute-done.core_ref
  37.5 0.0 copy-done
  37.5 0.0 copy-done.1
  37.5 0.0 copy-done.2
  37.5 8.5 %video.1 = bf16[512,16,128]{2,1,0:T(8,128)(2,1)} custom-call(s32[4,4]{1,0:T(4,128)S(1)} %copy-done.1, s32[4]{0:T(128)S(1)} %copy-done.2, s32[3]{0:T(128)S(1)} %pad_add_fusion.where_ref, bf16[512,16,128]{2,1,0:T(8,128)(2,1)S(1)} %copy-done, bf16[16,128,128]{2,1,0:T(8,128)(2,1)S(1)} %get-tuple-element.7.own_ref, ...), custom_call_target="tpu_custom_call" | custom-call | flops 536870912 | bytes 33554432 | tf_op jit(solution)/shard_map/video/pallas_call | solution.py:271
  46.1 1.4 %all-to-all-done.1.by_head_ref = bf16[16,64,128]{2,1,0:T(8,128)(2,1)S(1)} async-done(((bf16[16,64,128]{2,1,0:T(8,128)(2,1)}), bf16[16,64,128]{2,1,0:T(8,128)(2,1)S(1)}, u32[]{:S(2)}, u32[]{:S(2)}) %all-to-all-start.1) | async-done | bytes 262176 | tf_op jit(solution)/shard_map/all_to_all | solution.py:312
  47.5 0.8 %collect.1 = bf16[64,16,128]{2,1,0:T(8,128)(2,1)} custom-call(bf16[16,64,128]{2,1,0:T(8,128)(2,1)S(1)} %all-to-all-done.1.by_head_ref), custom_call_target="tpu_custom_call" | custom-call | tf_op jit(solution)/shard_map/collect/pallas_call | solution.py:203
Async XLA Ops:
  2.7 34.9 %copy-start = (bf16[512,16,128]{2,1,0:T(8,128)(2,1)S(1)}, bf16[512,16,128]{2,1,0:T(8,128)(2,1)}, u32[]{:S(2)}) copy-start(bf16[512,16,128]{2,1,0:T(8,128)(2,1)} %video_ref.1) | copy-start | bytes 6291460
  2.7 34.8 %copy-start.1 = (s32[4,4]{1,0:T(4,128)S(1)}, s32[4,4]{1,0:T(4,128)}, u32[]{:S(2)}) copy-start(s32[4,4]{1,0:T(4,128)} %pairs_ref.1) | copy-start | bytes 196
  2.7 34.8 %copy-start.2 = (s32[4]{0:T(128)S(1)}, s32[4]{0:T(128)}, u32[]{:S(2)}) copy-start(s32[4]{0:T(128)} %counts_ref.1) | copy-start | bytes 52
  2.7 28.9 %all-to-all-start = ((bf16[16,4,48,128]{3,2,1,0:T(8,128)(2,1)}), bf16[16,4,48,128]{3,2,1,0:T(8,128)(2,1)S(1)}, u32[]{:S(2)}, u32[]{:S(2)}) async-start(bf16[16,4,48,128]{3,2,1,0:T(8,128)(2,1)} %get-tuple-element.6), calls=%async_computation | async-start | bytes 1572864 | tf_op jit(solution)/shard_map/all_to_all | solution.py:312
  10.2 27.3 %collective-permute-start.1 = (bf16[16,128,128]{2,1,0:T(8,128)(2,1)S(1)}, bf16[16,128,128]{2,1,0:T(8,128)(2,1)}, u32[]{:S(2)}, u32[]{:S(2)}) collective-permute-start(bf16[16,128,128]{2,1,0:T(8,128)(2,1)S(1)} %get-tuple-element.7.own_ref), channel_id=1, source_target_pairs={{1,2},{2,1},{3,4},{4,3},{5,6},{6,5},{7,8},{8,7},{9,10},{10,9},{11,... | collective-permute-start | bytes 1572872 | tf_op jit(solution)/shard_map/ppermute | solution.py:306
  11.7 25.8 %collective-permute-start = (bf16[16,128,128]{2,1,0:T(8,128)(2,1)S(1)}, bf16[16,128,128]{2,1,0:T(8,128)(2,1)}, u32[]{:S(2)}, u32[]{:S(2)}) collective-permute-start(bf16[16,128,128]{2,1,0:T(8,128)(2,1)S(1)} %get-tuple-element.7.own_ref), channel_id=1, source_target_pairs={{0,1},{1,0},{2,3},{3,2},{4,5},{5,4},{6,7},{7,6},{8,9},{9,8},{10,11... | collective-permute-start | bytes 1572872 | tf_op jit(solution)/shard_map/ppermute | solution.py:316
  33.9 13.6 %all-to-all-start.1 = ((bf16[16,64,128]{2,1,0:T(8,128)(2,1)}), bf16[16,64,128]{2,1,0:T(8,128)(2,1)S(1)}, u32[]{:S(2)}, u32[]{:S(2)}) async-start(bf16[16,64,128]{2,1,0:T(8,128)(2,1)} %attend.1), calls=%async_computation.1 | async-start | bytes 524288 | tf_op jit(solution)/shard_map/all_to_all | solution.py:312

commit v10 on v9

--- a/solution.py
+++ b/solution.py
@@ -305,12 +305,11 @@
 
     chip = lax.ppermute(kv, "seq", chip_pairs)
 
-    planes = 4
-    spread_out = [(p % planes) * (devices // planes) + p // planes for p in range(devices)]
+    order = list(range(devices))[::-1]
 
     def exchange(value):
         return lax.all_to_all(
-            value, "seq", split_axis=0, concat_axis=0, tiled=True, axis_index_groups=[spread_out]
+            value, "seq", split_axis=0, concat_axis=0, tiled=True, axis_index_groups=[order]
         )
 
     core = lax.ppermute(kv, "seq", core_pairs)

time: 48.6 us -> 47.7 us (0.981)
  waiting for transfers between devices: 18.7 us -> 15.3 us
  starting transfers between devices: 15.1 us -> 17.7 us
    all_to_all x2, starting transfers between devices: 11.1 us -> 15 us  [exchange(): lax.all_to_all(value, 'seq', split_axis=0, concat_axis=0, tiled=True, axi...]
    all_to_all x2, waiting for transfers between devices: 18.7 us -> 15.3 us  [exchange(): lax.all_to_all(value, 'seq', split_axis=0, concat_axis=0, tiled=True, axi...]
    ppermute x1, starting transfers between devices: 2.56 us -> 1.2 us  [local(): core = lax.ppermute(kv, 'seq', core_pairs)]
  transfers between devices with their start and end apart: 4 -> 4, of which waited for: 2 -> 1; matrix products, arithmetic and copies ran while one was open for 0% -> 0% of each run, Pallas kernels for 22% -> 23%
where the time goes in v10:
time: 47.7 us; the launch traced here: 47.4 us
  starting transfers between devices  17.7 us (37%)
  waiting for transfers between devices  15.3 us (32%)
  Pallas kernels  13.6 us (29%)
  between operations  0.69 us (1%)
    all_to_all x2, waiting for transfers between devices, exchange(): lax.all_to_all(value, 'seq', split_axis=0, concat_axis=0, tiled=True, axi...  15.3 us
    all_to_all x2, starting transfers between devices, exchange(): lax.all_to_all(value, 'seq', split_axis=0, concat_axis=0, tiled=True, axi...  15 us
    pallas_call x1, Pallas kernels, video(): pl.pallas_call(functools.partial(video_kernel, rows, slots, scale, 4), gr...  8.52 us
    pallas_call x1, Pallas kernels, attend(): pl.pallas_call(functools.partial(attend_kernel, scale), in_specs=[pl.Bloc...  2.28 us
    pallas_call x1, Pallas kernels, arrange(): pl.pallas_call(functools.partial(arrange_kernel, pieces), in_specs=[pl.Bl...  2.03 us
    ppermute x1, starting transfers between devices, local(): chip = lax.ppermute(kv, 'seq', chip_pairs)  1.44 us
    ppermute x1, starting transfers between devices, local(): core = lax.ppermute(kv, 'seq', core_pairs)  1.2 us
  transfers between devices with their start and end apart: 4, of which 1 were waited for; matrix products, arithmetic and copies ran while one was open for 0% of the time, Pallas kernels for 23%

profile of v10, /device:TPU:0, one launch (start us, length us, event | category | flops | bytes accessed | tf_op | source)
XLA Modules:
  0.0 47.4 jit_solution(17543857689290161541)
XLA Ops:
  0.6 2.0 %arrange.1 = (bf16[16,4,48,128]{3,2,1,0:T(8,128)(2,1)}, bf16[16,128,128]{2,1,0:T(8,128)(2,1)S(1)}) custom-call(bf16[64,3,16,128]{3,2,1,0:T(8,128)(2,1)} %qkv_ref.1), custom_call_target="tpu_custom_call" | custom-call | tf_op jit(solution)/shard_map/arrange/pallas_call | solution.py:60
  2.7 0.0 copy-start
  2.7 0.0 copy-start.1
  2.7 0.0 copy-start.2
  2.7 9.1 %all-to-all-start = ((bf16[16,4,48,128]{3,2,1,0:T(8,128)(2,1)}), bf16[16,4,48,128]{3,2,1,0:T(8,128)(2,1)S(1)}, u32[]{:S(2)}, u32[]{:S(2)}) async-start(bf16[16,4,48,128]{3,2,1,0:T(8,128)(2,1)} %get-tuple-element.6), calls=%async_computation | async-start | bytes 1572864 | tf_op jit(solution)/shard_map/all_to_all | solution.py:311
  11.8 1.4 %collective-permute-start.1 = (bf16[16,128,128]{2,1,0:T(8,128)(2,1)S(1)}, bf16[16,128,128]{2,1,0:T(8,128)(2,1)}, u32[]{:S(2)}, u32[]{:S(2)}) collective-permute-start(bf16[16,128,128]{2,1,0:T(8,128)(2,1)S(1)} %get-tuple-element.7.own_ref), channel_id=1, source_target_pairs={{1,2},{2,1},{3,4},{4,3},{5,6},{6,5},{7,8},{8,7},{9,10},{10,9},{11,... | collective-permute-start | bytes 1572872 | tf_op jit(solution)/shard_map/ppermute | solution.py:306
  13.3 1.2 %collective-permute-start = (bf16[16,128,128]{2,1,0:T(8,128)(2,1)S(1)}, bf16[16,128,128]{2,1,0:T(8,128)(2,1)}, u32[]{:S(2)}, u32[]{:S(2)}) collective-permute-start(bf16[16,128,128]{2,1,0:T(8,128)(2,1)S(1)} %get-tuple-element.7.own_ref), channel_id=1, source_target_pairs={{0,1},{1,0},{2,3},{3,2},{4,5},{5,4},{6,7},{7,6},{8,9},{9,8},{10,11... | collective-permute-start | bytes 1572872 | tf_op jit(solution)/shard_map/ppermute | solution.py:315
  14.5 15.3 %all-to-all-done.recv_ref = bf16[16,4,48,128]{3,2,1,0:T(8,128)(2,1)S(1)} async-done(((bf16[16,4,48,128]{3,2,1,0:T(8,128)(2,1)}), bf16[16,4,48,128]{3,2,1,0:T(8,128)(2,1)S(1)}, u32[]{:S(2)}, u32[]{:S(2)}) %all-to-all-start) | async-done | bytes 786464 | tf_op jit(solution)/shard_map/all_to_all | solution.py:311
  29.7 2.3 %attend.1 = bf16[16,64,128]{2,1,0:T(8,128)(2,1)} custom-call(bf16[16,4,48,128]{3,2,1,0:T(8,128)(2,1)S(1)} %all-to-all-done.recv_ref), custom_call_target="tpu_custom_call" | custom-call | flops 536870912 | bytes 1048576 | tf_op jit(solution)/shard_map/attend/pallas_call | solution.py:129
  32.0 5.9 %all-to-all-start.1 = ((bf16[16,64,128]{2,1,0:T(8,128)(2,1)}), bf16[16,64,128]{2,1,0:T(8,128)(2,1)S(1)}, u32[]{:S(2)}, u32[]{:S(2)}) async-start(bf16[16,64,128]{2,1,0:T(8,128)(2,1)} %attend.1), calls=%async_computation.1 | async-start | bytes 524288 | tf_op jit(solution)/shard_map/all_to_all | solution.py:311
  38.0 0.1 pad_add_fusion.where_ref
  38.0 0.0 collective-permute-done.1.chip_ref
  38.0 0.0 collective-permute-done.core_ref
  38.0 0.0 copy-done
  38.0 0.0 copy-done.1
  38.1 0.0 copy-done.2
  38.1 8.5 %video.1 = bf16[512,16,128]{2,1,0:T(8,128)(2,1)} custom-call(s32[4,4]{1,0:T(4,128)S(1)} %copy-done.1, s32[4]{0:T(128)S(1)} %copy-done.2, s32[3]{0:T(128)S(1)} %pad_add_fusion.where_ref, bf16[512,16,128]{2,1,0:T(8,128)(2,1)S(1)} %copy-done, bf16[16,128,128]{2,1,0:T(8,128)(2,1)S(1)} %get-tuple-element.7.own_ref, ...), custom_call_target="tpu_custom_call" | custom-call | flops 536870912 | bytes 33554432 | tf_op jit(solution)/shard_map/video/pallas_call | solution.py:271
  46.6 0.0 all-to-all-done.1.by_head_ref
  46.6 0.8 %collect.1 = bf16[64,16,128]{2,1,0:T(8,128)(2,1)} custom-call(bf16[16,64,128]{2,1,0:T(8,128)(2,1)S(1)} %all-to-all-done.1.by_head_ref), custom_call_target="tpu_custom_call" | custom-call | tf_op jit(solution)/shard_map/collect/pallas_call | solution.py:203
Async XLA Ops:
  2.7 35.4 %copy-start = (bf16[512,16,128]{2,1,0:T(8,128)(2,1)S(1)}, bf16[512,16,128]{2,1,0:T(8,128)(2,1)}, u32[]{:S(2)}) copy-start(bf16[512,16,128]{2,1,0:T(8,128)(2,1)} %video_ref.1) | copy-start | bytes 6291460
  2.7 35.4 %copy-start.1 = (s32[4,4]{1,0:T(4,128)S(1)}, s32[4,4]{1,0:T(4,128)}, u32[]{:S(2)}) copy-start(s32[4,4]{1,0:T(4,128)} %pairs_ref.1) | copy-start | bytes 196
  2.7 35.4 %copy-start.2 = (s32[4]{0:T(128)S(1)}, s32[4]{0:T(128)}, u32[]{:S(2)}) copy-start(s32[4]{0:T(128)} %counts_ref.1) | copy-start | bytes 52
  2.7 27.0 %all-to-all-start = ((bf16[16,4,48,128]{3,2,1,0:T(8,128)(2,1)}), bf16[16,4,48,128]{3,2,1,0:T(8,128)(2,1)S(1)}, u32[]{:S(2)}, u32[]{:S(2)}) async-start(bf16[16,4,48,128]{3,2,1,0:T(8,128)(2,1)} %get-tuple-element.6), calls=%async_computation | async-start | bytes 1572864 | tf_op jit(solution)/shard_map/all_to_all | solution.py:311
  11.8 26.2 %collective-permute-start.1 = (bf16[16,128,128]{2,1,0:T(8,128)(2,1)S(1)}, bf16[16,128,128]{2,1,0:T(8,128)(2,1)}, u32[]{:S(2)}, u32[]{:S(2)}) collective-permute-start(bf16[16,128,128]{2,1,0:T(8,128)(2,1)S(1)} %get-tuple-element.7.own_ref), channel_id=1, source_target_pairs={{1,2},{2,1},{3,4},{4,3},{5,6},{6,5},{7,8},{8,7},{9,10},{10,9},{11,... | collective-permute-start | bytes 1572872 | tf_op jit(solution)/shard_map/ppermute | solution.py:306
  13.3 24.8 %collective-permute-start = (bf16[16,128,128]{2,1,0:T(8,128)(2,1)S(1)}, bf16[16,128,128]{2,1,0:T(8,128)(2,1)}, u32[]{:S(2)}, u32[]{:S(2)}) collective-permute-start(bf16[16,128,128]{2,1,0:T(8,128)(2,1)S(1)} %get-tuple-element.7.own_ref), channel_id=1, source_target_pairs={{0,1},{1,0},{2,3},{3,2},{4,5},{5,4},{6,7},{7,6},{8,9},{9,8},{10,11... | collective-permute-start | bytes 1572872 | tf_op jit(solution)/shard_map/ppermute | solution.py:315
  32.0 14.6 %all-to-all-start.1 = ((bf16[16,64,128]{2,1,0:T(8,128)(2,1)}), bf16[16,64,128]{2,1,0:T(8,128)(2,1)S(1)}, u32[]{:S(2)}, u32[]{:S(2)}) async-start(bf16[16,64,128]{2,1,0:T(8,128)(2,1)} %attend.1), calls=%async_computation.1 | async-start | bytes 524288 | tf_op jit(solution)/shard_map/all_to_all | solution.py:311

commit v11 on v10

--- a/solution.py
+++ b/solution.py
@@ -217,7 +217,7 @@
 def video_kernel(
     rows, slots, scale, group, pairs_ref, counts_ref, where_ref,
     video_ref, own_ref, core_ref, chip_ref, out_ref,
-    near_keys, near_values, keys_ref, values_ref, queries_ref, result_ref,
+    near_keys, near_values, keys_ref, values_ref, queries_ref, result_ref, identity_ref,
 ):
     block = pl.program_id(0)
     heads, unused, size = own_ref.shape
@@ -228,36 +228,34 @@
             at = pl.ds(pl.multiple_of(place, rows), rows)
             near_keys[:, at] = ref[:, :rows]
             near_values[:, at] = ref[:, rows:]
-        values_ref[:, :, size:] = jnp.ones((heads, slots * ABLK, size), jnp.bfloat16)
+        row = lax.broadcasted_iota(jnp.int32, (VBLK, VBLK), 0)
+        column = lax.broadcasted_iota(jnp.int32, (VBLK, VBLK), 1)
+        identity_ref[...] = jnp.where(row == column, 1.0, 0.0).astype(jnp.bfloat16)
 
     queries_ref[...] = jnp.swapaxes(video_ref[...], 0, 1)
     for slot in range(slots):
         start = pl.multiple_of((pairs_ref[block, slot] - where_ref[0]) * ABLK, ABLK)
         here = slice(slot * ABLK, (slot + 1) * ABLK)
         keys_ref[:, here] = near_keys[:, pl.ds(start, ABLK)]
-        values_ref[:, here, :size] = near_values[:, pl.ds(start, ABLK)]
-    column = lax.broadcasted_iota(jnp.int32, (VBLK, slots * ABLK), 1)
-    live = column < counts_ref[block] * ABLK
+        values_ref[:, here] = near_values[:, pl.ds(start, ABLK)]
+    key_row = lax.broadcasted_iota(jnp.int32, (slots * ABLK, VBLK), 0)
+    live = key_row < counts_ref[block] * ABLK
     factor = scale * LOG2E
     for first in range(0, heads, group):
         members = range(first, first + group)
-        scores = [
-            lax.dot_general(
-                queries_ref[head], keys_ref[head], (((1,), (1,)), ((), ())),
-                preferred_element_type=jnp.float32,
-            )
-            for head in members
+        scores = [scores_of(keys_ref[head], queries_ref[head]) for head in members]
+        scores = jnp.stack([jnp.where(live, one, LOWEST) for one in scores])
+        top = jnp.max(scores, axis=1, keepdims=True)
+        exact = jnp.exp2((scores - top) * factor)
+        share = 1.0 / jnp.sum(exact, axis=1, keepdims=True)
+        weights = (exact * share).astype(jnp.bfloat16)
+        turned = [
+            scores_of(identity_ref[...], weights[i]).astype(jnp.bfloat16) for i in range(group)
         ]
-        scores = jnp.stack([jnp.where(live, one, LOWEST) for one in scores])
-        top = jnp.max(scores, axis=2, keepdims=True)
-        weights = jnp.exp2((scores - top) * factor).astype(jnp.bfloat16)
-        summed = [
-            jnp.dot(weights[head - first], values_ref[head], preferred_element_type=jnp.float32)
-            for head in members
-        ]
-        for head in members:
-            both = summed[head - first]
-            result_ref[head] = (both[:, :size] / both[:, size:]).astype(jnp.bfloat16)
+        for i, head in enumerate(members):
+            result_ref[head] = jnp.dot(
+                turned[i], values_ref[head], preferred_element_type=jnp.float32
+            ).astype(jnp.bfloat16)
     out_ref[...] = jnp.swapaxes(result_ref[...], 0, 1)
 
 
@@ -279,9 +277,10 @@
                 pltpu.VMEM((heads, 3 * rows, size), jnp.bfloat16),
                 pltpu.VMEM((heads, 3 * rows, size), jnp.bfloat16),
                 pltpu.VMEM((heads, slots * ABLK, size), jnp.bfloat16),
-                pltpu.VMEM((heads, slots * ABLK, 2 * size), jnp.bfloat16),
+                pltpu.VMEM((heads, slots * ABLK, size), jnp.bfloat16),
                 pltpu.VMEM((heads, VBLK, size), jnp.bfloat16),
                 pltpu.VMEM((heads, VBLK, size), jnp.bfloat16),
+                pltpu.VMEM((VBLK, VBLK), jnp.bfloat16),
             ],
         ),
         out_shape=jax.ShapeDtypeStruct(video_q.shape, jnp.bfloat16),

time: 47.7 us -> 49.4 us (1.036)
  Pallas kernels: 13.6 us -> 15.3 us
    pallas_call x1, Pallas kernels: 8.52 us -> 10.2 us  [video(): pl.pallas_call(functools.partial(video_kernel, rows, slots, scale, 4), gr...]
  transfers between devices with their start and end apart: 4 -> 4, of which waited for: 1 -> 1; matrix products, arithmetic and copies ran while one was open for 0% -> 0% of each run, Pallas kernels for 23% -> 25%
where the time goes in v11:
time: 49.4 us; the launch traced here: 49.1 us
  starting transfers between devices  17.7 us (36%)
  Pallas kernels  15.3 us (31%)
  waiting for transfers between devices  15.3 us (31%)
  between operations  0.69 us (1%)
    all_to_all x2, waiting for transfers between devices, exchange(): lax.all_to_all(value, 'seq', split_axis=0, concat_axis=0, tiled=True, axi...  15.3 us
    all_to_all x2, starting transfers between devices, exchange(): lax.all_to_all(value, 'seq', split_axis=0, concat_axis=0, tiled=True, axi...  15 us
    pallas_call x1, Pallas kernels, video(): pl.pallas_call(functools.partial(video_kernel, rows, slots, scale, 4), gr...  10.2 us
    pallas_call x1, Pallas kernels, attend(): pl.pallas_call(functools.partial(attend_kernel, scale), in_specs=[pl.Bloc...  2.28 us
    pallas_call x1, Pallas kernels, arrange(): pl.pallas_call(functools.partial(arrange_kernel, pieces), in_specs=[pl.Bl...  2.03 us
    ppermute x1, starting transfers between devices, local(): chip = lax.ppermute(kv, 'seq', chip_pairs)  1.44 us
    ppermute x1, starting transfers between devices, local(): core = lax.ppermute(kv, 'seq', core_pairs)  1.2 us
  transfers between devices with their start and end apart: 4, of which 1 were waited for; matrix products, arithmetic and copies ran while one was open for 0% of the time, Pallas kernels for 25%

profile of v11, /device:TPU:0, one launch (start us, length us, event | category | flops | bytes accessed | tf_op | source)
XLA Modules:
  0.0 49.1 jit_solution(10378696707593431320)
XLA Ops:
  0.6 2.0 %arrange.1 = (bf16[16,4,48,128]{3,2,1,0:T(8,128)(2,1)}, bf16[16,128,128]{2,1,0:T(8,128)(2,1)S(1)}) custom-call(bf16[64,3,16,128]{3,2,1,0:T(8,128)(2,1)} %qkv_ref.1), custom_call_target="tpu_custom_call" | custom-call | tf_op jit(solution)/shard_map/arrange/pallas_call | solution.py:60
  2.7 0.0 copy-start
  2.7 0.0 copy-start.1
  2.7 0.0 copy-start.2
  2.7 9.1 %all-to-all-start = ((bf16[16,4,48,128]{3,2,1,0:T(8,128)(2,1)}), bf16[16,4,48,128]{3,2,1,0:T(8,128)(2,1)S(1)}, u32[]{:S(2)}, u32[]{:S(2)}) async-start(bf16[16,4,48,128]{3,2,1,0:T(8,128)(2,1)} %get-tuple-element.6), calls=%async_computation | async-start | bytes 1572864 | tf_op jit(solution)/shard_map/all_to_all | solution.py:310
  11.8 1.4 %collective-permute-start.1 = (bf16[16,128,128]{2,1,0:T(8,128)(2,1)S(1)}, bf16[16,128,128]{2,1,0:T(8,128)(2,1)}, u32[]{:S(2)}, u32[]{:S(2)}) collective-permute-start(bf16[16,128,128]{2,1,0:T(8,128)(2,1)S(1)} %get-tuple-element.7.own_ref), channel_id=1, source_target_pairs={{1,2},{2,1},{3,4},{4,3},{5,6},{6,5},{7,8},{8,7},{9,10},{10,9},{11,... | collective-permute-start | bytes 1572872 | tf_op jit(solution)/shard_map/ppermute | solution.py:305
  13.3 1.2 %collective-permute-start = (bf16[16,128,128]{2,1,0:T(8,128)(2,1)S(1)}, bf16[16,128,128]{2,1,0:T(8,128)(2,1)}, u32[]{:S(2)}, u32[]{:S(2)}) collective-permute-start(bf16[16,128,128]{2,1,0:T(8,128)(2,1)S(1)} %get-tuple-element.7.own_ref), channel_id=1, source_target_pairs={{0,1},{1,0},{2,3},{3,2},{4,5},{5,4},{6,7},{7,6},{8,9},{9,8},{10,11... | collective-permute-start | bytes 1572872 | tf_op jit(solution)/shard_map/ppermute | solution.py:314
  14.5 15.3 %all-to-all-done.recv_ref = bf16[16,4,48,128]{3,2,1,0:T(8,128)(2,1)S(1)} async-done(((bf16[16,4,48,128]{3,2,1,0:T(8,128)(2,1)}), bf16[16,4,48,128]{3,2,1,0:T(8,128)(2,1)S(1)}, u32[]{:S(2)}, u32[]{:S(2)}) %all-to-all-start) | async-done | bytes 786464 | tf_op jit(solution)/shard_map/all_to_all | solution.py:310
  29.7 2.3 %attend.1 = bf16[16,64,128]{2,1,0:T(8,128)(2,1)} custom-call(bf16[16,4,48,128]{3,2,1,0:T(8,128)(2,1)S(1)} %all-to-all-done.recv_ref), custom_call_target="tpu_custom_call" | custom-call | flops 536870912 | bytes 1048576 | tf_op jit(solution)/shard_map/attend/pallas_call | solution.py:129
  32.0 5.9 %all-to-all-start.1 = ((bf16[16,64,128]{2,1,0:T(8,128)(2,1)}), bf16[16,64,128]{2,1,0:T(8,128)(2,1)S(1)}, u32[]{:S(2)}, u32[]{:S(2)}) async-start(bf16[16,64,128]{2,1,0:T(8,128)(2,1)} %attend.1), calls=%async_computation.1 | async-start | bytes 524288 | tf_op jit(solution)/shard_map/all_to_all | solution.py:310
  38.0 0.1 pad_add_fusion.where_ref
  38.0 0.0 collective-permute-done.1.chip_ref
  38.0 0.0 collective-permute-done.core_ref
  38.0 0.0 copy-done
  38.0 0.0 copy-done.1
  38.1 0.0 copy-done.2
  38.1 10.2 %video.1 = bf16[512,16,128]{2,1,0:T(8,128)(2,1)} custom-call(s32[4,4]{1,0:T(4,128)S(1)} %copy-done.1, s32[4]{0:T(128)S(1)} %copy-done.2, s32[3]{0:T(128)S(1)} %pad_add_fusion.where_ref, bf16[512,16,128]{2,1,0:T(8,128)(2,1)S(1)} %copy-done, bf16[16,128,128]{2,1,0:T(8,128)(2,1)S(1)} %get-tuple-element.7.own_ref, ...), custom_call_target="tpu_custom_call" | custom-call | flops 536870912 | bytes 33554432 | tf_op jit(solution)/shard_map/video/pallas_call | solution.py:269
  48.3 0.0 all-to-all-done.1.by_head_ref
  48.3 0.8 %collect.1 = bf16[64,16,128]{2,1,0:T(8,128)(2,1)} custom-call(bf16[16,64,128]{2,1,0:T(8,128)(2,1)S(1)} %all-to-all-done.1.by_head_ref), custom_call_target="tpu_custom_call" | custom-call | tf_op jit(solution)/shard_map/collect/pallas_call | solution.py:203
Async XLA Ops:
  2.7 35.4 %copy-start = (bf16[512,16,128]{2,1,0:T(8,128)(2,1)S(1)}, bf16[512,16,128]{2,1,0:T(8,128)(2,1)}, u32[]{:S(2)}) copy-start(bf16[512,16,128]{2,1,0:T(8,128)(2,1)} %video_ref.1) | copy-start | bytes 6291460
  2.7 35.4 %copy-start.1 = (s32[4,4]{1,0:T(4,128)S(1)}, s32[4,4]{1,0:T(4,128)}, u32[]{:S(2)}) copy-start(s32[4,4]{1,0:T(4,128)} %pairs_ref.1) | copy-start | bytes 196
  2.7 35.4 %copy-start.2 = (s32[4]{0:T(128)S(1)}, s32[4]{0:T(128)}, u32[]{:S(2)}) copy-start(s32[4]{0:T(128)} %counts_ref.1) | copy-start | bytes 52
  2.7 27.0 %all-to-all-start = ((bf16[16,4,48,128]{3,2,1,0:T(8,128)(2,1)}), bf16[16,4,48,128]{3,2,1,0:T(8,128)(2,1)S(1)}, u32[]{:S(2)}, u32[]{:S(2)}) async-start(bf16[16,4,48,128]{3,2,1,0:T(8,128)(2,1)} %get-tuple-element.6), calls=%async_computation | async-start | bytes 1572864 | tf_op jit(solution)/shard_map/all_to_all | solution.py:310
  11.8 26.2 %collective-permute-start.1 = (bf16[16,128,128]{2,1,0:T(8,128)(2,1)S(1)}, bf16[16,128,128]{2,1,0:T(8,128)(2,1)}, u32[]{:S(2)}, u32[]{:S(2)}) collective-permute-start(bf16[16,128,128]{2,1,0:T(8,128)(2,1)S(1)} %get-tuple-element.7.own_ref), channel_id=1, source_target_pairs={{1,2},{2,1},{3,4},{4,3},{5,6},{6,5},{7,8},{8,7},{9,10},{10,9},{11,... | collective-permute-start | bytes 1572872 | tf_op jit(solution)/shard_map/ppermute | solution.py:305
  13.3 24.8 %collective-permute-start = (bf16[16,128,128]{2,1,0:T(8,128)(2,1)S(1)}, bf16[16,128,128]{2,1,0:T(8,128)(2,1)}, u32[]{:S(2)}, u32[]{:S(2)}) collective-permute-start(bf16[16,128,128]{2,1,0:T(8,128)(2,1)S(1)} %get-tuple-element.7.own_ref), channel_id=1, source_target_pairs={{0,1},{1,0},{2,3},{3,2},{4,5},{5,4},{6,7},{7,6},{8,9},{9,8},{10,11... | collective-permute-start | bytes 1572872 | tf_op jit(solution)/shard_map/ppermute | solution.py:314
  32.0 16.3 %all-to-all-start.1 = ((bf16[16,64,128]{2,1,0:T(8,128)(2,1)}), bf16[16,64,128]{2,1,0:T(8,128)(2,1)S(1)}, u32[]{:S(2)}, u32[]{:S(2)}) async-start(bf16[16,64,128]{2,1,0:T(8,128)(2,1)} %attend.1), calls=%async_computation.1 | async-start | bytes 524288 | tf_op jit(solution)/shard_map/all_to_all | solution.py:310

commit v12 on v11

--- a/solution.py
+++ b/solution.py
@@ -16,10 +16,6 @@
 
 def params():
     return pltpu.CompilerParams(vmem_limit_bytes=VMEM_LIMIT)
-
-
-def whole(shape):
-    return pl.BlockSpec(shape, lambda *unused: (0,) * len(shape))
 
 
 PIECE = 16
@@ -215,75 +211,76 @@
 
 
 def video_kernel(
-    rows, slots, scale, group, pairs_ref, counts_ref, where_ref,
-    video_ref, own_ref, core_ref, chip_ref, out_ref,
-    near_keys, near_values, keys_ref, values_ref, queries_ref, result_ref, identity_ref,
+    scale, group, pairs_ref, counts_ref, where_ref, video_ref, own_ref, core_ref, chip_ref, out_ref,
+    near_keys, near_values, keys_ref, values_ref, queries_ref, result_ref, turned, sems,
 ):
-    block = pl.program_id(0)
-    heads, unused, size = own_ref.shape
-
-    @pl.when(block == 0)
-    def _():
-        for ref, place in ((own_ref, rows), (core_ref, where_ref[1]), (chip_ref, where_ref[2])):
-            at = pl.ds(pl.multiple_of(place, rows), rows)
-            near_keys[:, at] = ref[:, :rows]
-            near_values[:, at] = ref[:, rows:]
-        row = lax.broadcasted_iota(jnp.int32, (VBLK, VBLK), 0)
-        column = lax.broadcasted_iota(jnp.int32, (VBLK, VBLK), 1)
-        identity_ref[...] = jnp.where(row == column, 1.0, 0.0).astype(jnp.bfloat16)
-
-    queries_ref[...] = jnp.swapaxes(video_ref[...], 0, 1)
-    for slot in range(slots):
-        start = pl.multiple_of((pairs_ref[block, slot] - where_ref[0]) * ABLK, ABLK)
-        here = slice(slot * ABLK, (slot + 1) * ABLK)
-        keys_ref[:, here] = near_keys[:, pl.ds(start, ABLK)]
-        values_ref[:, here] = near_values[:, pl.ds(start, ABLK)]
-    key_row = lax.broadcasted_iota(jnp.int32, (slots * ABLK, VBLK), 0)
-    live = key_row < counts_ref[block] * ABLK
+    heads, both, size = own_ref.shape
+    rows = both // 2
+    blocks, slots = pairs_ref.shape
+    for ref, place in ((own_ref, rows), (core_ref, where_ref[1]), (chip_ref, where_ref[2])):
+        at = pl.ds(pl.multiple_of(place, rows), rows)
+        near_keys[:, at] = ref[:, :rows]
+        near_values[:, at] = ref[:, rows:]
+    values_ref[:, :, size:] = jnp.ones((heads, slots * ABLK, size), jnp.bfloat16)
+    column = lax.broadcasted_iota(jnp.int32, (VBLK, slots * ABLK), 1)
     factor = scale * LOG2E
-    for first in range(0, heads, group):
-        members = range(first, first + group)
-        scores = [scores_of(keys_ref[head], queries_ref[head]) for head in members]
-        scores = jnp.stack([jnp.where(live, one, LOWEST) for one in scores])
-        top = jnp.max(scores, axis=1, keepdims=True)
-        exact = jnp.exp2((scores - top) * factor)
-        share = 1.0 / jnp.sum(exact, axis=1, keepdims=True)
-        weights = (exact * share).astype(jnp.bfloat16)
-        turned = [
-            scores_of(identity_ref[...], weights[i]).astype(jnp.bfloat16) for i in range(group)
-        ]
-        for i, head in enumerate(members):
-            result_ref[head] = jnp.dot(
-                turned[i], values_ref[head], preferred_element_type=jnp.float32
-            ).astype(jnp.bfloat16)
-    out_ref[...] = jnp.swapaxes(result_ref[...], 0, 1)
+
+    def departure(block):
+        at = pl.ds(pl.multiple_of(block * VBLK, VBLK), VBLK)
+        return pltpu.make_async_copy(turned.at[block], out_ref.at[at], sems.at[block])
+
+    def one_block(block, carried):
+        at = pl.ds(pl.multiple_of(block * VBLK, VBLK), VBLK)
+        queries_ref[...] = jnp.swapaxes(video_ref[at], 0, 1)
+        for slot in range(slots):
+            start = pl.multiple_of((pairs_ref[block, slot] - where_ref[0]) * ABLK, ABLK)
+            here = slice(slot * ABLK, (slot + 1) * ABLK)
+            keys_ref[:, here] = near_keys[:, pl.ds(start, ABLK)]
+            values_ref[:, here, :size] = near_values[:, pl.ds(start, ABLK)]
+        live = column < counts_ref[block] * ABLK
+        for first in range(0, heads, group):
+            members = range(first, first + group)
+            scores = [scores_of(queries_ref[head], keys_ref[head]) for head in members]
+            scores = jnp.stack([jnp.where(live, one, LOWEST) for one in scores])
+            top = jnp.max(scores, axis=2, keepdims=True)
+            weights = jnp.exp2((scores - top) * factor).astype(jnp.bfloat16)
+            summed = [
+                jnp.dot(weights[i], values_ref[head], preferred_element_type=jnp.float32)
+                for i, head in enumerate(members)
+            ]
+            for i, head in enumerate(members):
+                result_ref[head] = (summed[i][:, :size] / summed[i][:, size:]).astype(jnp.bfloat16)
+        turned[block] = jnp.swapaxes(result_ref[...], 0, 1)
+        departure(block).start()
+        return carried
+
+    lax.fori_loop(0, blocks, one_block, 0)
+    for block in range(blocks):
+        departure(block).wait()
 
 
 def video(video_q, own, core, chip, pairs, counts, where, scale):
     total, heads, size = video_q.shape
     rows = own.shape[1] // 2
-    slots = pairs.shape[1]
-    blocks = total // VBLK
-    block_spec = pl.BlockSpec((VBLK, heads, size), lambda i, *unused: (i, 0, 0))
+    blocks, slots = pairs.shape
     work = total * heads * slots * ABLK
-    return pl.pallas_call(
-        functools.partial(video_kernel, rows, slots, scale, 4),
-        grid_spec=pltpu.PrefetchScalarGridSpec(
-            num_scalar_prefetch=3,
-            grid=(blocks,),
-            in_specs=[block_spec] + [whole(own.shape)] * 3,
-            out_specs=block_spec,
-            scratch_shapes=[
-                pltpu.VMEM((heads, 3 * rows, size), jnp.bfloat16),
-                pltpu.VMEM((heads, 3 * rows, size), jnp.bfloat16),
-                pltpu.VMEM((heads, slots * ABLK, size), jnp.bfloat16),
-                pltpu.VMEM((heads, slots * ABLK, size), jnp.bfloat16),
-                pltpu.VMEM((heads, VBLK, size), jnp.bfloat16),
-                pltpu.VMEM((heads, VBLK, size), jnp.bfloat16),
-                pltpu.VMEM((VBLK, VBLK), jnp.bfloat16),
-            ],
-        ),
-        out_shape=jax.ShapeDtypeStruct(video_q.shape, jnp.bfloat16),
+    in_smem = pl.BlockSpec(memory_space=pltpu.SMEM)
+    in_vmem = pl.BlockSpec(memory_space=pltpu.VMEM)
+    return pl.pallas_call(
+        functools.partial(video_kernel, scale, 4),
+        in_specs=[in_smem] * 3 + [in_vmem] * 4,
+        out_specs=pl.BlockSpec(memory_space=pltpu.HBM),
+        out_shape=pltpu.HBM(video_q.shape, jnp.bfloat16),
+        scratch_shapes=[
+            pltpu.VMEM((heads, 3 * rows, size), jnp.bfloat16),
+            pltpu.VMEM((heads, 3 * rows, size), jnp.bfloat16),
+            pltpu.VMEM((heads, slots * ABLK, size), jnp.bfloat16),
+            pltpu.VMEM((heads, slots * ABLK, 2 * size), jnp.bfloat16),
+            pltpu.VMEM((heads, VBLK, size), jnp.bfloat16),
+            pltpu.VMEM((heads, VBLK, size), jnp.bfloat16),
+            pltpu.VMEM((blocks, VBLK, heads, size), jnp.bfloat16),
+            pltpu.SemaphoreType.DMA((blocks,)),
+        ],
         compiler_params=params(),
         cost_estimate=pl.CostEstimate(
             flops=4 * work * size, bytes_accessed=32 * total * heads * size, transcendentals=work

time: 49.4 us -> 47.6 us (0.964)
  Pallas kernels: 15.3 us -> 13.5 us
    pallas_call x1, Pallas kernels: 10.2 us -> 8.41 us  [video(): pl.pallas_call(functools.partial(video_kernel, scale, 4), in_specs=[in_sm...]
  transfers between devices with their start and end apart: 4 -> 4, of which waited for: 1 -> 1; matrix products, arithmetic and copies ran while one was open for 0% -> 0% of each run, Pallas kernels for 25% -> 23%
where the time goes in v12:
time: 47.6 us; the launch traced here: 47.2 us
  starting transfers between devices  17.7 us (37%)
  waiting for transfers between devices  15.3 us (32%)
  Pallas kernels  13.5 us (28%)
  between operations  0.71 us (1%)
    all_to_all x2, waiting for transfers between devices, exchange(): lax.all_to_all(value, 'seq', split_axis=0, concat_axis=0, tiled=True, axi...  15.3 us
    all_to_all x2, starting transfers between devices, exchange(): lax.all_to_all(value, 'seq', split_axis=0, concat_axis=0, tiled=True, axi...  15 us
    pallas_call x1, Pallas kernels, video(): pl.pallas_call(functools.partial(video_kernel, scale, 4), in_specs=[in_sm...  8.41 us
    pallas_call x1, Pallas kernels, attend(): pl.pallas_call(functools.partial(attend_kernel, scale), in_specs=[pl.Bloc...  2.28 us
    pallas_call x1, Pallas kernels, arrange(): pl.pallas_call(functools.partial(arrange_kernel, pieces), in_specs=[pl.Bl...  2.03 us
    ppermute x1, starting transfers between devices, local(): chip = lax.ppermute(kv, 'seq', chip_pairs)  1.44 us
    ppermute x1, starting transfers between devices, local(): core = lax.ppermute(kv, 'seq', core_pairs)  1.2 us
  transfers between devices with their start and end apart: 4, of which 1 were waited for; matrix products, arithmetic and copies ran while one was open for 0% of the time, Pallas kernels for 23%

profile of v12, /device:TPU:0, one launch (start us, length us, event | category | flops | bytes accessed | tf_op | source)
XLA Modules:
  0.0 47.2 jit_solution(10842418636512380016)
XLA Ops:
  0.6 2.0 %arrange.1 = (bf16[16,4,48,128]{3,2,1,0:T(8,128)(2,1)}, bf16[16,128,128]{2,1,0:T(8,128)(2,1)S(1)}) custom-call(bf16[64,3,16,128]{3,2,1,0:T(8,128)(2,1)} %qkv_ref.1), custom_call_target="tpu_custom_call" | custom-call | tf_op jit(solution)/shard_map/arrange/pallas_call | solution.py:56
  2.7 0.0 copy-start
  2.7 0.0 copy-start.1
  2.7 0.0 copy-start.2
  2.7 9.1 %all-to-all-start = ((bf16[16,4,48,128]{3,2,1,0:T(8,128)(2,1)}), bf16[16,4,48,128]{3,2,1,0:T(8,128)(2,1)S(1)}, u32[]{:S(2)}, u32[]{:S(2)}) async-start(bf16[16,4,48,128]{3,2,1,0:T(8,128)(2,1)} %get-tuple-element.6), calls=%async_computation | async-start | bytes 1572864 | tf_op jit(solution)/shard_map/all_to_all | solution.py:307
  11.8 1.4 %collective-permute-start.1 = (bf16[16,128,128]{2,1,0:T(8,128)(2,1)S(1)}, bf16[16,128,128]{2,1,0:T(8,128)(2,1)}, u32[]{:S(2)}, u32[]{:S(2)}) collective-permute-start(bf16[16,128,128]{2,1,0:T(8,128)(2,1)S(1)} %get-tuple-element.7.own_ref), channel_id=1, source_target_pairs={{1,2},{2,1},{3,4},{4,3},{5,6},{6,5},{7,8},{8,7},{9,10},{10,9},{11,... | collective-permute-start | bytes 1572872 | tf_op jit(solution)/shard_map/ppermute | solution.py:302
  13.3 1.2 %collective-permute-start = (bf16[16,128,128]{2,1,0:T(8,128)(2,1)S(1)}, bf16[16,128,128]{2,1,0:T(8,128)(2,1)}, u32[]{:S(2)}, u32[]{:S(2)}) collective-permute-start(bf16[16,128,128]{2,1,0:T(8,128)(2,1)S(1)} %get-tuple-element.7.own_ref), channel_id=1, source_target_pairs={{0,1},{1,0},{2,3},{3,2},{4,5},{5,4},{6,7},{7,6},{8,9},{9,8},{10,11... | collective-permute-start | bytes 1572872 | tf_op jit(solution)/shard_map/ppermute | solution.py:311
  14.5 15.3 %all-to-all-done.recv_ref = bf16[16,4,48,128]{3,2,1,0:T(8,128)(2,1)S(1)} async-done(((bf16[16,4,48,128]{3,2,1,0:T(8,128)(2,1)}), bf16[16,4,48,128]{3,2,1,0:T(8,128)(2,1)S(1)}, u32[]{:S(2)}, u32[]{:S(2)}) %all-to-all-start) | async-done | bytes 786464 | tf_op jit(solution)/shard_map/all_to_all | solution.py:307
  29.7 2.3 %attend.1 = bf16[16,64,128]{2,1,0:T(8,128)(2,1)} custom-call(bf16[16,4,48,128]{3,2,1,0:T(8,128)(2,1)S(1)} %all-to-all-done.recv_ref), custom_call_target="tpu_custom_call" | custom-call | flops 536870912 | bytes 1048576 | tf_op jit(solution)/shard_map/attend/pallas_call | solution.py:125
  32.0 5.9 %all-to-all-start.1 = ((bf16[16,64,128]{2,1,0:T(8,128)(2,1)}), bf16[16,64,128]{2,1,0:T(8,128)(2,1)S(1)}, u32[]{:S(2)}, u32[]{:S(2)}) async-start(bf16[16,64,128]{2,1,0:T(8,128)(2,1)} %attend.1), calls=%async_computation.1 | async-start | bytes 524288 | tf_op jit(solution)/shard_map/all_to_all | solution.py:307
  38.0 0.1 pad_add_fusion.where_ref
  38.0 0.0 collective-permute-done.1.chip_ref
  38.0 0.0 collective-permute-done.core_ref
  38.0 0.0 copy-done
  38.0 0.0 copy-done.1
  38.1 0.0 copy-done.2
  38.1 8.4 %video.1 = bf16[512,16,128]{2,1,0:T(8,128)(2,1)} custom-call(s32[4,4]{1,0:T(4,128)S(1)} %copy-done.1, s32[4]{0:T(128)S(1)} %copy-done.2, s32[3]{0:T(128)S(1)} %pad_add_fusion.where_ref, bf16[512,16,128]{2,1,0:T(8,128)(2,1)S(1)} %copy-done, bf16[16,128,128]{2,1,0:T(8,128)(2,1)S(1)} %get-tuple-element.7.own_ref, ...), custom_call_target="tpu_custom_call" | custom-call | flops 536870912 | bytes 33554432 | tf_op jit(solution)/shard_map/video/pallas_call | solution.py:269
  46.5 0.0 all-to-all-done.1.by_head_ref
  46.5 0.8 %collect.1 = bf16[64,16,128]{2,1,0:T(8,128)(2,1)} custom-call(bf16[16,64,128]{2,1,0:T(8,128)(2,1)S(1)} %all-to-all-done.1.by_head_ref), custom_call_target="tpu_custom_call" | custom-call | tf_op jit(solution)/shard_map/collect/pallas_call | solution.py:199
Async XLA Ops:
  2.7 35.4 %copy-start = (bf16[512,16,128]{2,1,0:T(8,128)(2,1)S(1)}, bf16[512,16,128]{2,1,0:T(8,128)(2,1)}, u32[]{:S(2)}) copy-start(bf16[512,16,128]{2,1,0:T(8,128)(2,1)} %video_ref.1) | copy-start | bytes 6291460
  2.7 35.4 %copy-start.1 = (s32[4,4]{1,0:T(4,128)S(1)}, s32[4,4]{1,0:T(4,128)}, u32[]{:S(2)}) copy-start(s32[4,4]{1,0:T(4,128)} %pairs_ref.1) | copy-start | bytes 196
  2.7 35.4 %copy-start.2 = (s32[4]{0:T(128)S(1)}, s32[4]{0:T(128)}, u32[]{:S(2)}) copy-start(s32[4]{0:T(128)} %counts_ref.1) | copy-start | bytes 52
  2.7 27.0 %all-to-all-start = ((bf16[16,4,48,128]{3,2,1,0:T(8,128)(2,1)}), bf16[16,4,48,128]{3,2,1,0:T(8,128)(2,1)S(1)}, u32[]{:S(2)}, u32[]{:S(2)}) async-start(bf16[16,4,48,128]{3,2,1,0:T(8,128)(2,1)} %get-tuple-element.6), calls=%async_computation | async-start | bytes 1572864 | tf_op jit(solution)/shard_map/all_to_all | solution.py:307
  11.8 26.2 %collective-permute-start.1 = (bf16[16,128,128]{2,1,0:T(8,128)(2,1)S(1)}, bf16[16,128,128]{2,1,0:T(8,128)(2,1)}, u32[]{:S(2)}, u32[]{:S(2)}) collective-permute-start(bf16[16,128,128]{2,1,0:T(8,128)(2,1)S(1)} %get-tuple-element.7.own_ref), channel_id=1, source_target_pairs={{1,2},{2,1},{3,4},{4,3},{5,6},{6,5},{7,8},{8,7},{9,10},{10,9},{11,... | collective-permute-start | bytes 1572872 | tf_op jit(solution)/shard_map/ppermute | solution.py:302
  13.3 24.8 %collective-permute-start = (bf16[16,128,128]{2,1,0:T(8,128)(2,1)S(1)}, bf16[16,128,128]{2,1,0:T(8,128)(2,1)}, u32[]{:S(2)}, u32[]{:S(2)}) collective-permute-start(bf16[16,128,128]{2,1,0:T(8,128)(2,1)S(1)} %get-tuple-element.7.own_ref), channel_id=1, source_target_pairs={{0,1},{1,0},{2,3},{3,2},{4,5},{5,4},{6,7},{7,6},{8,9},{9,8},{10,11... | collective-permute-start | bytes 1572872 | tf_op jit(solution)/shard_map/ppermute | solution.py:311
  32.0 14.5 %all-to-all-start.1 = ((bf16[16,64,128]{2,1,0:T(8,128)(2,1)}), bf16[16,64,128]{2,1,0:T(8,128)(2,1)S(1)}, u32[]{:S(2)}, u32[]{:S(2)}) async-start(bf16[16,64,128]{2,1,0:T(8,128)(2,1)} %attend.1), calls=%async_computation.1 | async-start | bytes 524288 | tf_op jit(solution)/shard_map/all_to_all | solution.py:307

commit v13 on v12

--- a/solution.py
+++ b/solution.py
@@ -221,40 +221,51 @@
         at = pl.ds(pl.multiple_of(place, rows), rows)
         near_keys[:, at] = ref[:, :rows]
         near_values[:, at] = ref[:, rows:]
-    values_ref[:, :, size:] = jnp.ones((heads, slots * ABLK, size), jnp.bfloat16)
+    values_ref[:, :, :, size:] = jnp.ones((blocks, heads, slots * ABLK, size), jnp.bfloat16)
     column = lax.broadcasted_iota(jnp.int32, (VBLK, slots * ABLK), 1)
     factor = scale * LOG2E
 
-    def departure(block):
-        at = pl.ds(pl.multiple_of(block * VBLK, VBLK), VBLK)
-        return pltpu.make_async_copy(turned.at[block], out_ref.at[at], sems.at[block])
-
-    def one_block(block, carried):
-        at = pl.ds(pl.multiple_of(block * VBLK, VBLK), VBLK)
-        queries_ref[...] = jnp.swapaxes(video_ref[at], 0, 1)
+    def prepare(block):
+        queries_ref[block] = jnp.swapaxes(video_ref[block * VBLK : (block + 1) * VBLK], 0, 1)
         for slot in range(slots):
             start = pl.multiple_of((pairs_ref[block, slot] - where_ref[0]) * ABLK, ABLK)
             here = slice(slot * ABLK, (slot + 1) * ABLK)
-            keys_ref[:, here] = near_keys[:, pl.ds(start, ABLK)]
-            values_ref[:, here, :size] = near_values[:, pl.ds(start, ABLK)]
-        live = column < counts_ref[block] * ABLK
-        for first in range(0, heads, group):
-            members = range(first, first + group)
-            scores = [scores_of(queries_ref[head], keys_ref[head]) for head in members]
-            scores = jnp.stack([jnp.where(live, one, LOWEST) for one in scores])
-            top = jnp.max(scores, axis=2, keepdims=True)
-            weights = jnp.exp2((scores - top) * factor).astype(jnp.bfloat16)
-            summed = [
-                jnp.dot(weights[i], values_ref[head], preferred_element_type=jnp.float32)
-                for i, head in enumerate(members)
+            keys_ref[block, :, here] = near_keys[:, pl.ds(start, ABLK)]
+            values_ref[block, :, here, :size] = near_values[:, pl.ds(start, ABLK)]
+
+    def departure(block):
+        at = pl.ds(block * VBLK, VBLK)
+        return pltpu.make_async_copy(turned.at[block], out_ref.at[at], sems.at[block])
+
+    units = [(block, first) for block in range(blocks) for first in range(0, heads, group)]
+    scores, weights = {}, {}
+    for step in range(len(units) + 2):
+        if step < len(units):
+            block, first = units[step]
+            if first == 0:
+                prepare(block)
+            live = column < counts_ref[block] * ABLK
+            scores[step] = [
+                jnp.where(live, scores_of(queries_ref[block, head], keys_ref[block, head]), LOWEST)
+                for head in range(first, first + group)
             ]
-            for i, head in enumerate(members):
-                result_ref[head] = (summed[i][:, :size] / summed[i][:, size:]).astype(jnp.bfloat16)
-        turned[block] = jnp.swapaxes(result_ref[...], 0, 1)
-        departure(block).start()
-        return carried
-
-    lax.fori_loop(0, blocks, one_block, 0)
+        if 1 <= step <= len(units):
+            now = jnp.stack(scores.pop(step - 1))
+            top = jnp.max(now, axis=2, keepdims=True)
+            weights[step - 1] = jnp.exp2((now - top) * factor).astype(jnp.bfloat16)
+        if step >= 2:
+            block, first = units[step - 2]
+            now = weights.pop(step - 2)
+            for i in range(group):
+                summed = jnp.dot(
+                    now[i], values_ref[block, first + i], preferred_element_type=jnp.float32
+                )
+                result_ref[block, first + i] = (summed[:, :size] / summed[:, size:]).astype(
+                    jnp.bfloat16
+                )
+            if first + group == heads:
+                turned[block] = jnp.swapaxes(result_ref[block], 0, 1)
+                departure(block).start()
     for block in range(blocks):
         departure(block).wait()
 
@@ -274,10 +285,10 @@
         scratch_shapes=[
             pltpu.VMEM((heads, 3 * rows, size), jnp.bfloat16),
             pltpu.VMEM((heads, 3 * rows, size), jnp.bfloat16),
-            pltpu.VMEM((heads, slots * ABLK, size), jnp.bfloat16),
-            pltpu.VMEM((heads, slots * ABLK, 2 * size), jnp.bfloat16),
-            pltpu.VMEM((heads, VBLK, size), jnp.bfloat16),
-            pltpu.VMEM((heads, VBLK, size), jnp.bfloat16),
+            pltpu.VMEM((blocks, heads, slots * ABLK, size), jnp.bfloat16),
+            pltpu.VMEM((blocks, heads, slots * ABLK, 2 * size), jnp.bfloat16),
+            pltpu.VMEM((blocks, heads, VBLK, size), jnp.bfloat16),
+            pltpu.VMEM((blocks, heads, VBLK, size), jnp.bfloat16),
             pltpu.VMEM((blocks, VBLK, heads, size), jnp.bfloat16),
             pltpu.SemaphoreType.DMA((blocks,)),
         ],

time: 47.6 us -> 46.2 us (0.971)
  Pallas kernels: 13.5 us -> 11.2 us
  waiting for transfers between devices: 15.3 us -> 16.1 us
    pallas_call x1, Pallas kernels: 8.41 us -> 6.16 us  [video(): pl.pallas_call(functools.partial(video_kernel, scale, 4), in_specs=[in_sm...]
    all_to_all x2, waiting for transfers between devices: 15.3 us -> 16.1 us  [exchange(): lax.all_to_all(value, 'seq', split_axis=0, concat_axis=0, tiled=True, axi...]
  transfers between devices with their start and end apart: 4 -> 4, of which waited for: 1 -> 2; matrix products, arithmetic and copies ran while one was open for 0% -> 0% of each run, Pallas kernels for 23% -> 18%
where the time goes in v13:
time: 46.2 us; the launch traced here: 45.8 us
  starting transfers between devices  17.7 us (38%)
  waiting for transfers between devices  16.1 us (35%)
  Pallas kernels  11.2 us (24%)
  between operations  0.7 us (2%)
    all_to_all x2, waiting for transfers between devices, exchange(): lax.all_to_all(value, 'seq', split_axis=0, concat_axis=0, tiled=True, axi...  16.1 us
    all_to_all x2, starting transfers between devices, exchange(): lax.all_to_all(value, 'seq', split_axis=0, concat_axis=0, tiled=True, axi...  15 us
    pallas_call x1, Pallas kernels, video(): pl.pallas_call(functools.partial(video_kernel, scale, 4), in_specs=[in_sm...  6.16 us
    pallas_call x1, Pallas kernels, attend(): pl.pallas_call(functools.partial(attend_kernel, scale), in_specs=[pl.Bloc...  2.28 us
    pallas_call x1, Pallas kernels, arrange(): pl.pallas_call(functools.partial(arrange_kernel, pieces), in_specs=[pl.Bl...  2.03 us
    ppermute x1, starting transfers between devices, local(): chip = lax.ppermute(kv, 'seq', chip_pairs)  1.44 us
    ppermute x1, starting transfers between devices, local(): core = lax.ppermute(kv, 'seq', core_pairs)  1.2 us
  transfers between devices with their start and end apart: 4, of which 2 were waited for; matrix products, arithmetic and copies ran while one was open for 0% of the time, Pallas kernels for 18%

profile of v13, /device:TPU:0, one launch (start us, length us, event | category | flops | bytes accessed | tf_op | source)
XLA Modules:
  0.0 45.8 jit_solution(7802644944319320511)
XLA Ops:
  0.6 2.0 %arrange.1 = (bf16[16,4,48,128]{3,2,1,0:T(8,128)(2,1)}, bf16[16,128,128]{2,1,0:T(8,128)(2,1)S(1)}) custom-call(bf16[64,3,16,128]{3,2,1,0:T(8,128)(2,1)} %qkv_ref.1), custom_call_target="tpu_custom_call" | custom-call | tf_op jit(solution)/shard_map/arrange/pallas_call | solution.py:56
  2.7 0.0 copy-start
  2.7 0.0 copy-start.1
  2.7 0.0 copy-start.2
  2.7 9.1 %all-to-all-start = ((bf16[16,4,48,128]{3,2,1,0:T(8,128)(2,1)}), bf16[16,4,48,128]{3,2,1,0:T(8,128)(2,1)S(1)}, u32[]{:S(2)}, u32[]{:S(2)}) async-start(bf16[16,4,48,128]{3,2,1,0:T(8,128)(2,1)} %get-tuple-element.6), calls=%async_computation | async-start | bytes 1572864 | tf_op jit(solution)/shard_map/all_to_all | solution.py:318
  11.8 1.4 %collective-permute-start.1 = (bf16[16,128,128]{2,1,0:T(8,128)(2,1)S(1)}, bf16[16,128,128]{2,1,0:T(8,128)(2,1)}, u32[]{:S(2)}, u32[]{:S(2)}) collective-permute-start(bf16[16,128,128]{2,1,0:T(8,128)(2,1)S(1)} %get-tuple-element.7.own_ref), channel_id=1, source_target_pairs={{1,2},{2,1},{3,4},{4,3},{5,6},{6,5},{7,8},{8,7},{9,10},{10,9},{11,... | collective-permute-start | bytes 1572872 | tf_op jit(solution)/shard_map/ppermute | solution.py:313
  13.3 1.2 %collective-permute-start = (bf16[16,128,128]{2,1,0:T(8,128)(2,1)S(1)}, bf16[16,128,128]{2,1,0:T(8,128)(2,1)}, u32[]{:S(2)}, u32[]{:S(2)}) collective-permute-start(bf16[16,128,128]{2,1,0:T(8,128)(2,1)S(1)} %get-tuple-element.7.own_ref), channel_id=1, source_target_pairs={{0,1},{1,0},{2,3},{3,2},{4,5},{5,4},{6,7},{7,6},{8,9},{9,8},{10,11... | collective-permute-start | bytes 1572872 | tf_op jit(solution)/shard_map/ppermute | solution.py:322
  14.5 15.3 %all-to-all-done.recv_ref = bf16[16,4,48,128]{3,2,1,0:T(8,128)(2,1)S(1)} async-done(((bf16[16,4,48,128]{3,2,1,0:T(8,128)(2,1)}), bf16[16,4,48,128]{3,2,1,0:T(8,128)(2,1)S(1)}, u32[]{:S(2)}, u32[]{:S(2)}) %all-to-all-start) | async-done | bytes 786464 | tf_op jit(solution)/shard_map/all_to_all | solution.py:318
  29.7 2.3 %attend.1 = bf16[16,64,128]{2,1,0:T(8,128)(2,1)} custom-call(bf16[16,4,48,128]{3,2,1,0:T(8,128)(2,1)S(1)} %all-to-all-done.recv_ref), custom_call_target="tpu_custom_call" | custom-call | flops 536870912 | bytes 1048576 | tf_op jit(solution)/shard_map/attend/pallas_call | solution.py:125
  32.0 5.9 %all-to-all-start.1 = ((bf16[16,64,128]{2,1,0:T(8,128)(2,1)}), bf16[16,64,128]{2,1,0:T(8,128)(2,1)S(1)}, u32[]{:S(2)}, u32[]{:S(2)}) async-start(bf16[16,64,128]{2,1,0:T(8,128)(2,1)} %attend.1), calls=%async_computation.1 | async-start | bytes 524288 | tf_op jit(solution)/shard_map/all_to_all | solution.py:318
  38.0 0.1 pad_add_fusion.where_ref
  38.0 0.0 collective-permute-done.1.chip_ref
  38.0 0.0 collective-permute-done.core_ref
  38.0 0.0 copy-done
  38.0 0.0 copy-done.1
  38.1 0.0 copy-done.2
  38.1 6.2 %video.1 = bf16[512,16,128]{2,1,0:T(8,128)(2,1)} custom-call(s32[4,4]{1,0:T(4,128)S(1)} %copy-done.1, s32[4]{0:T(128)S(1)} %copy-done.2, s32[3]{0:T(128)S(1)} %pad_add_fusion.where_ref, bf16[512,16,128]{2,1,0:T(8,128)(2,1)S(1)} %copy-done, bf16[16,128,128]{2,1,0:T(8,128)(2,1)S(1)} %get-tuple-element.7.own_ref, ...), custom_call_target="tpu_custom_call" | custom-call | flops 536870912 | bytes 33554432 | tf_op jit(solution)/shard_map/video/pallas_call | solution.py:280
  44.2 0.8 %all-to-all-done.1.by_head_ref = bf16[16,64,128]{2,1,0:T(8,128)(2,1)S(1)} async-done(((bf16[16,64,128]{2,1,0:T(8,128)(2,1)}), bf16[16,64,128]{2,1,0:T(8,128)(2,1)S(1)}, u32[]{:S(2)}, u32[]{:S(2)}) %all-to-all-start.1) | async-done | bytes 262176 | tf_op jit(solution)/shard_map/all_to_all | solution.py:318
  45.1 0.8 %collect.1 = bf16[64,16,128]{2,1,0:T(8,128)(2,1)} custom-call(bf16[16,64,128]{2,1,0:T(8,128)(2,1)S(1)} %all-to-all-done.1.by_head_ref), custom_call_target="tpu_custom_call" | custom-call | tf_op jit(solution)/shard_map/collect/pallas_call | solution.py:199
Async XLA Ops:
  2.7 35.4 %copy-start = (bf16[512,16,128]{2,1,0:T(8,128)(2,1)S(1)}, bf16[512,16,128]{2,1,0:T(8,128)(2,1)}, u32[]{:S(2)}) copy-start(bf16[512,16,128]{2,1,0:T(8,128)(2,1)} %video_ref.1) | copy-start | bytes 6291460
  2.7 35.4 %copy-start.1 = (s32[4,4]{1,0:T(4,128)S(1)}, s32[4,4]{1,0:T(4,128)}, u32[]{:S(2)}) copy-start(s32[4,4]{1,0:T(4,128)} %pairs_ref.1) | copy-start | bytes 196
  2.7 35.4 %copy-start.2 = (s32[4]{0:T(128)S(1)}, s32[4]{0:T(128)}, u32[]{:S(2)}) copy-start(s32[4]{0:T(128)} %counts_ref.1) | copy-start | bytes 52
  2.7 27.0 %all-to-all-start = ((bf16[16,4,48,128]{3,2,1,0:T(8,128)(2,1)}), bf16[16,4,48,128]{3,2,1,0:T(8,128)(2,1)S(1)}, u32[]{:S(2)}, u32[]{:S(2)}) async-start(bf16[16,4,48,128]{3,2,1,0:T(8,128)(2,1)} %get-tuple-element.6), calls=%async_computation | async-start | bytes 1572864 | tf_op jit(solution)/shard_map/all_to_all | solution.py:318
  11.8 26.2 %collective-permute-start.1 = (bf16[16,128,128]{2,1,0:T(8,128)(2,1)S(1)}, bf16[16,128,128]{2,1,0:T(8,128)(2,1)}, u32[]{:S(2)}, u32[]{:S(2)}) collective-permute-start(bf16[16,128,128]{2,1,0:T(8,128)(2,1)S(1)} %get-tuple-element.7.own_ref), channel_id=1, source_target_pairs={{1,2},{2,1},{3,4},{4,3},{5,6},{6,5},{7,8},{8,7},{9,10},{10,9},{11,... | collective-permute-start | bytes 1572872 | tf_op jit(solution)/shard_map/ppermute | solution.py:313
  13.3 24.8 %collective-permute-start = (bf16[16,128,128]{2,1,0:T(8,128)(2,1)S(1)}, bf16[16,128,128]{2,1,0:T(8,128)(2,1)}, u32[]{:S(2)}, u32[]{:S(2)}) collective-permute-start(bf16[16,128,128]{2,1,0:T(8,128)(2,1)S(1)} %get-tuple-element.7.own_ref), channel_id=1, source_target_pairs={{0,1},{1,0},{2,3},{3,2},{4,5},{5,4},{6,7},{7,6},{8,9},{9,8},{10,11... | collective-permute-start | bytes 1572872 | tf_op jit(solution)/shard_map/ppermute | solution.py:322
  32.0 13.0 %all-to-all-start.1 = ((bf16[16,64,128]{2,1,0:T(8,128)(2,1)}), bf16[16,64,128]{2,1,0:T(8,128)(2,1)S(1)}, u32[]{:S(2)}, u32[]{:S(2)}) async-start(bf16[16,64,128]{2,1,0:T(8,128)(2,1)} %attend.1), calls=%async_computation.1 | async-start | bytes 524288 | tf_op jit(solution)/shard_map/all_to_all | solution.py:318

commit v14 on v13

--- a/solution.py
+++ b/solution.py
@@ -23,28 +23,38 @@
 
 def arrange_kernel(pieces, qkv_ref, send_ref, kv_ref, came, turned, in_sems, out_sems):
     rows = pieces * PIECE
-    arrivals = [
-        pltpu.make_async_copy(
-            qkv_ref.at[pl.ds(piece * PIECE, PIECE)], came.at[piece], in_sems.at[piece]
-        )
-        for piece in range(pieces)
-    ]
+    heads = turned.shape[1]
+    halves = 2
+    arrivals = []
+    for piece in range(pieces):
+        for half in range(halves):
+            count = PIECE // halves
+            arrivals.append(
+                pltpu.make_async_copy(
+                    qkv_ref.at[pl.ds(piece * PIECE + half * count, count)],
+                    came.at[piece, pl.ds(half * count, count)],
+                    in_sems.at[piece, half],
+                )
+            )
     for arrival in arrivals:
         arrival.start()
     departures = []
-    for piece, arrival in enumerate(arrivals):
-        arrival.wait()
+    for piece in range(pieces):
+        for half in range(halves):
+            arrivals[piece * halves + half].wait()
         for part in range(3):
             by_head = jnp.swapaxes(came[piece, :, part], 0, 1)
             turned[piece, :, part * PIECE : (part + 1) * PIECE] = by_head
             if part:
                 at = (part - 1) * rows + piece * PIECE
                 kv_ref[:, at : at + PIECE] = by_head
-        departure = pltpu.make_async_copy(
-            turned.at[piece], send_ref.at[:, piece], out_sems.at[piece]
-        )
-        departure.start()
-        departures.append(departure)
+        for half in range(halves):
+            at = pl.ds(half * (heads // halves), heads // halves)
+            departure = pltpu.make_async_copy(
+                turned.at[piece, at], send_ref.at[at, piece], out_sems.at[piece, half]
+            )
+            departure.start()
+            departures.append(departure)
     for departure in departures:
         departure.wait()
 
@@ -67,8 +77,8 @@
         scratch_shapes=[
             pltpu.VMEM((pieces, PIECE, parts, heads, size), dtype),
             pltpu.VMEM((pieces, heads, parts * PIECE, size), dtype),
-            pltpu.SemaphoreType.DMA((pieces,)),
-            pltpu.SemaphoreType.DMA((pieces,)),
+            pltpu.SemaphoreType.DMA((pieces, 2)),
+            pltpu.SemaphoreType.DMA((pieces, 2)),
         ],
         compiler_params=params(),
         name="arrange",
@@ -129,7 +139,7 @@
         out_shape=pltpu.HBM((sources, rows, size), jnp.bfloat16),
         scratch_shapes=[
             pltpu.VMEM((sources, rows, size), jnp.bfloat16),
-            pltpu.SemaphoreType.DMA((total // 128,)),
+            pltpu.SemaphoreType.DMA((total // 256,)),
         ],
         compiler_params=params(),
         cost_estimate=pl.CostEstimate(

time: 46.2 us -> 46.3 us (level)
  no operation moved by 1% of the time
where the time goes in v14:
time: 46.3 us; the launch traced here: 45.9 us
  starting transfers between devices  17.7 us (38%)
  waiting for transfers between devices  16.1 us (35%)
  Pallas kernels  11.3 us (24%)
  between operations  0.7 us (2%)
    all_to_all x2, waiting for transfers between devices, exchange(): lax.all_to_all(value, 'seq', split_axis=0, concat_axis=0, tiled=True, axi...  16.1 us
    all_to_all x2, starting transfers between devices, exchange(): lax.all_to_all(value, 'seq', split_axis=0, concat_axis=0, tiled=True, axi...  15 us
    pallas_call x1, Pallas kernels, video(): pl.pallas_call(functools.partial(video_kernel, scale, 4), in_specs=[in_sm...  6.17 us
    pallas_call x1, Pallas kernels, attend(): pl.pallas_call(functools.partial(attend_kernel, scale), in_specs=[pl.Bloc...  2.29 us
    pallas_call x1, Pallas kernels, arrange(): pl.pallas_call(functools.partial(arrange_kernel, pieces), in_specs=[pl.Bl...  2.09 us
    ppermute x1, starting transfers between devices, local(): chip = lax.ppermute(kv, 'seq', chip_pairs)  1.44 us
    ppermute x1, starting transfers between devices, local(): core = lax.ppermute(kv, 'seq', core_pairs)  1.2 us
  transfers between devices with their start and end apart: 4, of which 2 were waited for; matrix products, arithmetic and copies ran while one was open for 0% of the time, Pallas kernels for 18%

profile of v14, /device:TPU:0, one launch (start us, length us, event | category | flops | bytes accessed | tf_op | source)
XLA Modules:
  0.0 45.9 jit_solution(5875760249227048717)
XLA Ops:
  0.6 2.1 %arrange.1 = (bf16[16,4,48,128]{3,2,1,0:T(8,128)(2,1)}, bf16[16,128,128]{2,1,0:T(8,128)(2,1)S(1)}) custom-call(bf16[64,3,16,128]{3,2,1,0:T(8,128)(2,1)} %qkv_ref.1), custom_call_target="tpu_custom_call" | custom-call | tf_op jit(solution)/shard_map/arrange/pallas_call | solution.py:66
  2.7 0.0 copy-start
  2.7 0.0 copy-start.1
  2.8 0.0 copy-start.2
  2.8 9.1 %all-to-all-start = ((bf16[16,4,48,128]{3,2,1,0:T(8,128)(2,1)}), bf16[16,4,48,128]{3,2,1,0:T(8,128)(2,1)S(1)}, u32[]{:S(2)}, u32[]{:S(2)}) async-start(bf16[16,4,48,128]{3,2,1,0:T(8,128)(2,1)} %get-tuple-element.6), calls=%async_computation | async-start | bytes 1572864 | tf_op jit(solution)/shard_map/all_to_all | solution.py:328
  11.9 1.4 %collective-permute-start.1 = (bf16[16,128,128]{2,1,0:T(8,128)(2,1)S(1)}, bf16[16,128,128]{2,1,0:T(8,128)(2,1)}, u32[]{:S(2)}, u32[]{:S(2)}) collective-permute-start(bf16[16,128,128]{2,1,0:T(8,128)(2,1)S(1)} %get-tuple-element.7.own_ref), channel_id=1, source_target_pairs={{1,2},{2,1},{3,4},{4,3},{5,6},{6,5},{7,8},{8,7},{9,10},{10,9},{11,... | collective-permute-start | bytes 1572872 | tf_op jit(solution)/shard_map/ppermute | solution.py:323
  13.3 1.2 %collective-permute-start = (bf16[16,128,128]{2,1,0:T(8,128)(2,1)S(1)}, bf16[16,128,128]{2,1,0:T(8,128)(2,1)}, u32[]{:S(2)}, u32[]{:S(2)}) collective-permute-start(bf16[16,128,128]{2,1,0:T(8,128)(2,1)S(1)} %get-tuple-element.7.own_ref), channel_id=1, source_target_pairs={{0,1},{1,0},{2,3},{3,2},{4,5},{5,4},{6,7},{7,6},{8,9},{9,8},{10,11... | collective-permute-start | bytes 1572872 | tf_op jit(solution)/shard_map/ppermute | solution.py:332
  14.5 15.3 %all-to-all-done.recv_ref = bf16[16,4,48,128]{3,2,1,0:T(8,128)(2,1)S(1)} async-done(((bf16[16,4,48,128]{3,2,1,0:T(8,128)(2,1)}), bf16[16,4,48,128]{3,2,1,0:T(8,128)(2,1)S(1)}, u32[]{:S(2)}, u32[]{:S(2)}) %all-to-all-start) | async-done | bytes 786464 | tf_op jit(solution)/shard_map/all_to_all | solution.py:328
  29.8 2.3 %attend.1 = bf16[16,64,128]{2,1,0:T(8,128)(2,1)} custom-call(bf16[16,4,48,128]{3,2,1,0:T(8,128)(2,1)S(1)} %all-to-all-done.recv_ref), custom_call_target="tpu_custom_call" | custom-call | flops 536870912 | bytes 1048576 | tf_op jit(solution)/shard_map/attend/pallas_call | solution.py:135
  32.1 5.9 %all-to-all-start.1 = ((bf16[16,64,128]{2,1,0:T(8,128)(2,1)}), bf16[16,64,128]{2,1,0:T(8,128)(2,1)S(1)}, u32[]{:S(2)}, u32[]{:S(2)}) async-start(bf16[16,64,128]{2,1,0:T(8,128)(2,1)} %attend.1), calls=%async_computation.1 | async-start | bytes 524288 | tf_op jit(solution)/shard_map/all_to_all | solution.py:328
  38.0 0.1 pad_add_fusion.where_ref
  38.1 0.0 collective-permute-done.1.chip_ref
  38.1 0.0 collective-permute-done.core_ref
  38.1 0.0 copy-done
  38.1 0.0 copy-done.1
  38.1 0.0 copy-done.2
  38.1 6.2 %video.1 = bf16[512,16,128]{2,1,0:T(8,128)(2,1)} custom-call(s32[4,4]{1,0:T(4,128)S(1)} %copy-done.1, s32[4]{0:T(128)S(1)} %copy-done.2, s32[3]{0:T(128)S(1)} %pad_add_fusion.where_ref, bf16[512,16,128]{2,1,0:T(8,128)(2,1)S(1)} %copy-done, bf16[16,128,128]{2,1,0:T(8,128)(2,1)S(1)} %get-tuple-element.7.own_ref, ...), custom_call_target="tpu_custom_call" | custom-call | flops 536870912 | bytes 33554432 | tf_op jit(solution)/shard_map/video/pallas_call | solution.py:290
  44.3 0.8 %all-to-all-done.1.by_head_ref = bf16[16,64,128]{2,1,0:T(8,128)(2,1)S(1)} async-done(((bf16[16,64,128]{2,1,0:T(8,128)(2,1)}), bf16[16,64,128]{2,1,0:T(8,128)(2,1)S(1)}, u32[]{:S(2)}, u32[]{:S(2)}) %all-to-all-start.1) | async-done | bytes 262176 | tf_op jit(solution)/shard_map/all_to_all | solution.py:328
  45.1 0.8 %collect.1 = bf16[64,16,128]{2,1,0:T(8,128)(2,1)} custom-call(bf16[16,64,128]{2,1,0:T(8,128)(2,1)S(1)} %all-to-all-done.1.by_head_ref), custom_call_target="tpu_custom_call" | custom-call | tf_op jit(solution)/shard_map/collect/pallas_call | solution.py:209
Async XLA Ops:
  2.7 35.4 %copy-start = (bf16[512,16,128]{2,1,0:T(8,128)(2,1)S(1)}, bf16[512,16,128]{2,1,0:T(8,128)(2,1)}, u32[]{:S(2)}) copy-start(bf16[512,16,128]{2,1,0:T(8,128)(2,1)} %video_ref.1) | copy-start | bytes 6291460
  2.7 35.4 %copy-start.1 = (s32[4,4]{1,0:T(4,128)S(1)}, s32[4,4]{1,0:T(4,128)}, u32[]{:S(2)}) copy-start(s32[4,4]{1,0:T(4,128)} %pairs_ref.1) | copy-start | bytes 196
  2.8 35.4 %copy-start.2 = (s32[4]{0:T(128)S(1)}, s32[4]{0:T(128)}, u32[]{:S(2)}) copy-start(s32[4]{0:T(128)} %counts_ref.1) | copy-start | bytes 52
  2.8 27.0 %all-to-all-start = ((bf16[16,4,48,128]{3,2,1,0:T(8,128)(2,1)}), bf16[16,4,48,128]{3,2,1,0:T(8,128)(2,1)S(1)}, u32[]{:S(2)}, u32[]{:S(2)}) async-start(bf16[16,4,48,128]{3,2,1,0:T(8,128)(2,1)} %get-tuple-element.6), calls=%async_computation | async-start | bytes 1572864 | tf_op jit(solution)/shard_map/all_to_all | solution.py:328
  11.9 26.2 %collective-permute-start.1 = (bf16[16,128,128]{2,1,0:T(8,128)(2,1)S(1)}, bf16[16,128,128]{2,1,0:T(8,128)(2,1)}, u32[]{:S(2)}, u32[]{:S(2)}) collective-permute-start(bf16[16,128,128]{2,1,0:T(8,128)(2,1)S(1)} %get-tuple-element.7.own_ref), channel_id=1, source_target_pairs={{1,2},{2,1},{3,4},{4,3},{5,6},{6,5},{7,8},{8,7},{9,10},{10,9},{11,... | collective-permute-start | bytes 1572872 | tf_op jit(solution)/shard_map/ppermute | solution.py:323
  13.3 24.8 %collective-permute-start = (bf16[16,128,128]{2,1,0:T(8,128)(2,1)S(1)}, bf16[16,128,128]{2,1,0:T(8,128)(2,1)}, u32[]{:S(2)}, u32[]{:S(2)}) collective-permute-start(bf16[16,128,128]{2,1,0:T(8,128)(2,1)S(1)} %get-tuple-element.7.own_ref), channel_id=1, source_target_pairs={{0,1},{1,0},{2,3},{3,2},{4,5},{5,4},{6,7},{7,6},{8,9},{9,8},{10,11... | collective-permute-start | bytes 1572872 | tf_op jit(solution)/shard_map/ppermute | solution.py:332
  32.1 13.0 %all-to-all-start.1 = ((bf16[16,64,128]{2,1,0:T(8,128)(2,1)}), bf16[16,64,128]{2,1,0:T(8,128)(2,1)S(1)}, u32[]{:S(2)}, u32[]{:S(2)}) async-start(bf16[16,64,128]{2,1,0:T(8,128)(2,1)} %attend.1), calls=%async_computation.1 | async-start | bytes 524288 | tf_op jit(solution)/shard_map/all_to_all | solution.py:328

commit v15 on v13

--- a/solution.py
+++ b/solution.py
@@ -312,7 +312,7 @@
 
     chip = lax.ppermute(kv, "seq", chip_pairs)
 
-    order = list(range(devices))[::-1]
+    order = [(devices - 1 - devices // 4 - p) % devices for p in range(devices)]
 
     def exchange(value):
         return lax.all_to_all(

time: 46.2 us -> 44.6 us (0.965)
  waiting for transfers between devices: 16.1 us -> 15 us
  starting transfers between devices: 17.7 us -> 17 us
    all_to_all x2, waiting for transfers between devices: 16.1 us -> 15 us  [exchange(): lax.all_to_all(value, 'seq', split_axis=0, concat_axis=0, tiled=True, axi...]
    all_to_all x2, starting transfers between devices: 15 us -> 14.4 us  [exchange(): lax.all_to_all(value, 'seq', split_axis=0, concat_axis=0, tiled=True, axi...]
  transfers between devices with their start and end apart: 4 -> 4, of which waited for: 2 -> 1; matrix products, arithmetic and copies ran while one was open for 0% -> 0% of each run, Pallas kernels for 18% -> 19%
where the time goes in v15:
time: 44.6 us; the launch traced here: 44.1 us
  starting transfers between devices  17 us (38%)
  waiting for transfers between devices  15 us (34%)
  Pallas kernels  11.2 us (25%)
  between operations  0.71 us (2%)
    all_to_all x2, waiting for transfers between devices, exchange(): lax.all_to_all(value, 'seq', split_axis=0, concat_axis=0, tiled=True, axi...  15 us
    all_to_all x2, starting transfers between devices, exchange(): lax.all_to_all(value, 'seq', split_axis=0, concat_axis=0, tiled=True, axi...  14.4 us
    pallas_call x1, Pallas kernels, video(): pl.pallas_call(functools.partial(video_kernel, scale, 4), in_specs=[in_sm...  6.18 us
    pallas_call x1, Pallas kernels, attend(): pl.pallas_call(functools.partial(attend_kernel, scale), in_specs=[pl.Bloc...  2.28 us
    pallas_call x1, Pallas kernels, arrange(): pl.pallas_call(functools.partial(arrange_kernel, pieces), in_specs=[pl.Bl...  2.03 us
    ppermute x1, starting transfers between devices, local(): chip = lax.ppermute(kv, 'seq', chip_pairs)  1.44 us
    ppermute x1, starting transfers between devices, local(): core = lax.ppermute(kv, 'seq', core_pairs)  1.2 us
  transfers between devices with their start and end apart: 4, of which 1 were waited for; matrix products, arithmetic and copies ran while one was open for 0% of the time, Pallas kernels for 19%

profile of v15, /device:TPU:0, one launch (start us, length us, event | category | flops | bytes accessed | tf_op | source)
XLA Modules:
  0.0 44.1 jit_solution(2748235789077324467)
XLA Ops:
  0.6 2.0 %arrange.1 = (bf16[16,4,48,128]{3,2,1,0:T(8,128)(2,1)}, bf16[16,128,128]{2,1,0:T(8,128)(2,1)S(1)}) custom-call(bf16[64,3,16,128]{3,2,1,0:T(8,128)(2,1)} %qkv_ref.1), custom_call_target="tpu_custom_call" | custom-call | tf_op jit(solution)/shard_map/arrange/pallas_call | solution.py:56
  2.7 0.0 copy-start
  2.7 0.0 copy-start.1
  2.7 0.0 copy-start.2
  2.7 8.1 %all-to-all-start = ((bf16[16,4,48,128]{3,2,1,0:T(8,128)(2,1)}), bf16[16,4,48,128]{3,2,1,0:T(8,128)(2,1)S(1)}, u32[]{:S(2)}, u32[]{:S(2)}) async-start(bf16[16,4,48,128]{3,2,1,0:T(8,128)(2,1)} %get-tuple-element.6), calls=%async_computation | async-start | bytes 1572864 | tf_op jit(solution)/shard_map/all_to_all | solution.py:318
  10.8 1.4 %collective-permute-start.1 = (bf16[16,128,128]{2,1,0:T(8,128)(2,1)S(1)}, bf16[16,128,128]{2,1,0:T(8,128)(2,1)}, u32[]{:S(2)}, u32[]{:S(2)}) collective-permute-start(bf16[16,128,128]{2,1,0:T(8,128)(2,1)S(1)} %get-tuple-element.7.own_ref), channel_id=1, source_target_pairs={{1,2},{2,1},{3,4},{4,3},{5,6},{6,5},{7,8},{8,7},{9,10},{10,9},{11,... | collective-permute-start | bytes 1572872 | tf_op jit(solution)/shard_map/ppermute | solution.py:313
  12.2 1.2 %collective-permute-start = (bf16[16,128,128]{2,1,0:T(8,128)(2,1)S(1)}, bf16[16,128,128]{2,1,0:T(8,128)(2,1)}, u32[]{:S(2)}, u32[]{:S(2)}) collective-permute-start(bf16[16,128,128]{2,1,0:T(8,128)(2,1)S(1)} %get-tuple-element.7.own_ref), channel_id=1, source_target_pairs={{0,1},{1,0},{2,3},{3,2},{4,5},{5,4},{6,7},{7,6},{8,9},{9,8},{10,11... | collective-permute-start | bytes 1572872 | tf_op jit(solution)/shard_map/ppermute | solution.py:322
  13.4 15.0 %all-to-all-done.recv_ref = bf16[16,4,48,128]{3,2,1,0:T(8,128)(2,1)S(1)} async-done(((bf16[16,4,48,128]{3,2,1,0:T(8,128)(2,1)}), bf16[16,4,48,128]{3,2,1,0:T(8,128)(2,1)S(1)}, u32[]{:S(2)}, u32[]{:S(2)}) %all-to-all-start) | async-done | bytes 786464 | tf_op jit(solution)/shard_map/all_to_all | solution.py:318
  28.4 2.3 %attend.1 = bf16[16,64,128]{2,1,0:T(8,128)(2,1)} custom-call(bf16[16,4,48,128]{3,2,1,0:T(8,128)(2,1)S(1)} %all-to-all-done.recv_ref), custom_call_target="tpu_custom_call" | custom-call | flops 536870912 | bytes 1048576 | tf_op jit(solution)/shard_map/attend/pallas_call | solution.py:125
  30.7 6.3 %all-to-all-start.1 = ((bf16[16,64,128]{2,1,0:T(8,128)(2,1)}), bf16[16,64,128]{2,1,0:T(8,128)(2,1)S(1)}, u32[]{:S(2)}, u32[]{:S(2)}) async-start(bf16[16,64,128]{2,1,0:T(8,128)(2,1)} %attend.1), calls=%async_computation.1 | async-start | bytes 524288 | tf_op jit(solution)/shard_map/all_to_all | solution.py:318
  37.0 0.1 pad_add_fusion.where_ref
  37.1 0.0 collective-permute-done.1.chip_ref
  37.1 0.0 collective-permute-done.core_ref
  37.1 0.0 copy-done
  37.1 0.0 copy-done.1
  37.1 0.0 copy-done.2
  37.1 6.2 %video.1 = bf16[512,16,128]{2,1,0:T(8,128)(2,1)} custom-call(s32[4,4]{1,0:T(4,128)S(1)} %copy-done.1, s32[4]{0:T(128)S(1)} %copy-done.2, s32[3]{0:T(128)S(1)} %pad_add_fusion.where_ref, bf16[512,16,128]{2,1,0:T(8,128)(2,1)S(1)} %copy-done, bf16[16,128,128]{2,1,0:T(8,128)(2,1)S(1)} %get-tuple-element.7.own_ref, ...), custom_call_target="tpu_custom_call" | custom-call | flops 536870912 | bytes 33554432 | tf_op jit(solution)/shard_map/video/pallas_call | solution.py:280
  43.3 0.0 all-to-all-done.1.by_head_ref
  43.3 0.8 %collect.1 = bf16[64,16,128]{2,1,0:T(8,128)(2,1)} custom-call(bf16[16,64,128]{2,1,0:T(8,128)(2,1)S(1)} %all-to-all-done.1.by_head_ref), custom_call_target="tpu_custom_call" | custom-call | tf_op jit(solution)/shard_map/collect/pallas_call | solution.py:199
Async XLA Ops:
  2.7 34.4 %copy-start = (bf16[512,16,128]{2,1,0:T(8,128)(2,1)S(1)}, bf16[512,16,128]{2,1,0:T(8,128)(2,1)}, u32[]{:S(2)}) copy-start(bf16[512,16,128]{2,1,0:T(8,128)(2,1)} %video_ref.1) | copy-start | bytes 6291460
  2.7 34.4 %copy-start.1 = (s32[4,4]{1,0:T(4,128)S(1)}, s32[4,4]{1,0:T(4,128)}, u32[]{:S(2)}) copy-start(s32[4,4]{1,0:T(4,128)} %pairs_ref.1) | copy-start | bytes 196
  2.7 34.4 %copy-start.2 = (s32[4]{0:T(128)S(1)}, s32[4]{0:T(128)}, u32[]{:S(2)}) copy-start(s32[4]{0:T(128)} %counts_ref.1) | copy-start | bytes 52
  2.7 25.7 %all-to-all-start = ((bf16[16,4,48,128]{3,2,1,0:T(8,128)(2,1)}), bf16[16,4,48,128]{3,2,1,0:T(8,128)(2,1)S(1)}, u32[]{:S(2)}, u32[]{:S(2)}) async-start(bf16[16,4,48,128]{3,2,1,0:T(8,128)(2,1)} %get-tuple-element.6), calls=%async_computation | async-start | bytes 1572864 | tf_op jit(solution)/shard_map/all_to_all | solution.py:318
  10.8 26.3 %collective-permute-start.1 = (bf16[16,128,128]{2,1,0:T(8,128)(2,1)S(1)}, bf16[16,128,128]{2,1,0:T(8,128)(2,1)}, u32[]{:S(2)}, u32[]{:S(2)}) collective-permute-start(bf16[16,128,128]{2,1,0:T(8,128)(2,1)S(1)} %get-tuple-element.7.own_ref), channel_id=1, source_target_pairs={{1,2},{2,1},{3,4},{4,3},{5,6},{6,5},{7,8},{8,7},{9,10},{10,9},{11,... | collective-permute-start | bytes 1572872 | tf_op jit(solution)/shard_map/ppermute | solution.py:313
  12.2 24.9 %collective-permute-start = (bf16[16,128,128]{2,1,0:T(8,128)(2,1)S(1)}, bf16[16,128,128]{2,1,0:T(8,128)(2,1)}, u32[]{:S(2)}, u32[]{:S(2)}) collective-permute-start(bf16[16,128,128]{2,1,0:T(8,128)(2,1)S(1)} %get-tuple-element.7.own_ref), channel_id=1, source_target_pairs={{0,1},{1,0},{2,3},{3,2},{4,5},{5,4},{6,7},{7,6},{8,9},{9,8},{10,11... | collective-permute-start | bytes 1572872 | tf_op jit(solution)/shard_map/ppermute | solution.py:322
  30.7 12.6 %all-to-all-start.1 = ((bf16[16,64,128]{2,1,0:T(8,128)(2,1)}), bf16[16,64,128]{2,1,0:T(8,128)(2,1)S(1)}, u32[]{:S(2)}, u32[]{:S(2)}) async-start(bf16[16,64,128]{2,1,0:T(8,128)(2,1)} %attend.1), calls=%async_computation.1 | async-start | bytes 524288 | tf_op jit(solution)/shard_map/all_to_all | solution.py:318

commit v16 on v15

--- a/solution.py
+++ b/solution.py
@@ -312,7 +312,7 @@
 
     chip = lax.ppermute(kv, "seq", chip_pairs)
 
-    order = [(devices - 1 - devices // 4 - p) % devices for p in range(devices)]
+    order = [(devices - 1 - devices // 2 - p) % devices for p in range(devices)]
 
     def exchange(value):
         return lax.all_to_all(

time: 44.6 us -> 44.7 us (level)
  starting transfers between devices: 17 us -> 14.7 us
  waiting for transfers between devices: 15 us -> 17.1 us
    all_to_all x2, starting transfers between devices: 14.4 us -> 12.1 us  [exchange(): lax.all_to_all(value, 'seq', split_axis=0, concat_axis=0, tiled=True, axi...]
    all_to_all x2, waiting for transfers between devices: 15 us -> 17.1 us  [exchange(): lax.all_to_all(value, 'seq', split_axis=0, concat_axis=0, tiled=True, axi...]
  transfers between devices with their start and end apart: 4 -> 4, of which waited for: 1 -> 2; matrix products, arithmetic and copies ran while one was open for 0% -> 0% of each run, Pallas kernels for 19% -> 19%
where the time goes in v16:
time: 44.7 us; the launch traced here: 43.9 us
  waiting for transfers between devices  17.1 us (38%)
  starting transfers between devices  14.7 us (33%)
  Pallas kernels  11.2 us (25%)
  between operations  0.7 us (2%)
    all_to_all x2, waiting for transfers between devices, exchange(): lax.all_to_all(value, 'seq', split_axis=0, concat_axis=0, tiled=True, axi...  17.1 us
    all_to_all x2, starting transfers between devices, exchange(): lax.all_to_all(value, 'seq', split_axis=0, concat_axis=0, tiled=True, axi...  12.1 us
    pallas_call x1, Pallas kernels, video(): pl.pallas_call(functools.partial(video_kernel, scale, 4), in_specs=[in_sm...  6.18 us
    pallas_call x1, Pallas kernels, attend(): pl.pallas_call(functools.partial(attend_kernel, scale), in_specs=[pl.Bloc...  2.28 us
    pallas_call x1, Pallas kernels, arrange(): pl.pallas_call(functools.partial(arrange_kernel, pieces), in_specs=[pl.Bl...  2.03 us
    ppermute x1, starting transfers between devices, local(): chip = lax.ppermute(kv, 'seq', chip_pairs)  1.44 us
    ppermute x1, starting transfers between devices, local(): core = lax.ppermute(kv, 'seq', core_pairs)  1.21 us
  transfers between devices with their start and end apart: 4, of which 2 were waited for; matrix products, arithmetic and copies ran while one was open for 0% of the time, Pallas kernels for 19%

profile of v16, /device:TPU:0, one launch (start us, length us, event | category | flops | bytes accessed | tf_op | source)
XLA Modules:
  0.0 43.9 jit_solution(12350312998720257285)
XLA Ops:
  0.6 2.0 %arrange.1 = (bf16[16,4,48,128]{3,2,1,0:T(8,128)(2,1)}, bf16[16,128,128]{2,1,0:T(8,128)(2,1)S(1)}) custom-call(bf16[64,3,16,128]{3,2,1,0:T(8,128)(2,1)} %qkv_ref.1), custom_call_target="tpu_custom_call" | custom-call | tf_op jit(solution)/shard_map/arrange/pallas_call | solution.py:56
  2.7 0.0 copy-start
  2.7 0.0 copy-start.1
  2.7 0.0 copy-start.2
  2.7 7.8 %all-to-all-start = ((bf16[16,4,48,128]{3,2,1,0:T(8,128)(2,1)}), bf16[16,4,48,128]{3,2,1,0:T(8,128)(2,1)S(1)}, u32[]{:S(2)}, u32[]{:S(2)}) async-start(bf16[16,4,48,128]{3,2,1,0:T(8,128)(2,1)} %get-tuple-element.6), calls=%async_computation | async-start | bytes 1572864 | tf_op jit(solution)/shard_map/all_to_all | solution.py:318
  10.5 1.4 %collective-permute-start.1 = (bf16[16,128,128]{2,1,0:T(8,128)(2,1)S(1)}, bf16[16,128,128]{2,1,0:T(8,128)(2,1)}, u32[]{:S(2)}, u32[]{:S(2)}) collective-permute-start(bf16[16,128,128]{2,1,0:T(8,128)(2,1)S(1)} %get-tuple-element.7.own_ref), channel_id=1, source_target_pairs={{1,2},{2,1},{3,4},{4,3},{5,6},{6,5},{7,8},{8,7},{9,10},{10,9},{11,... | collective-permute-start | bytes 1572872 | tf_op jit(solution)/shard_map/ppermute | solution.py:313
  11.9 1.2 %collective-permute-start = (bf16[16,128,128]{2,1,0:T(8,128)(2,1)S(1)}, bf16[16,128,128]{2,1,0:T(8,128)(2,1)}, u32[]{:S(2)}, u32[]{:S(2)}) collective-permute-start(bf16[16,128,128]{2,1,0:T(8,128)(2,1)S(1)} %get-tuple-element.7.own_ref), channel_id=1, source_target_pairs={{0,1},{1,0},{2,3},{3,2},{4,5},{5,4},{6,7},{7,6},{8,9},{9,8},{10,11... | collective-permute-start | bytes 1572872 | tf_op jit(solution)/shard_map/ppermute | solution.py:322
  13.1 16.2 %all-to-all-done.recv_ref = bf16[16,4,48,128]{3,2,1,0:T(8,128)(2,1)S(1)} async-done(((bf16[16,4,48,128]{3,2,1,0:T(8,128)(2,1)}), bf16[16,4,48,128]{3,2,1,0:T(8,128)(2,1)S(1)}, u32[]{:S(2)}, u32[]{:S(2)}) %all-to-all-start) | async-done | bytes 786464 | tf_op jit(solution)/shard_map/all_to_all | solution.py:318
  29.4 2.3 %attend.1 = bf16[16,64,128]{2,1,0:T(8,128)(2,1)} custom-call(bf16[16,4,48,128]{3,2,1,0:T(8,128)(2,1)S(1)} %all-to-all-done.recv_ref), custom_call_target="tpu_custom_call" | custom-call | flops 536870912 | bytes 1048576 | tf_op jit(solution)/shard_map/attend/pallas_call | solution.py:125
  31.6 4.3 %all-to-all-start.1 = ((bf16[16,64,128]{2,1,0:T(8,128)(2,1)}), bf16[16,64,128]{2,1,0:T(8,128)(2,1)S(1)}, u32[]{:S(2)}, u32[]{:S(2)}) async-start(bf16[16,64,128]{2,1,0:T(8,128)(2,1)} %attend.1), calls=%async_computation.1 | async-start | bytes 524288 | tf_op jit(solution)/shard_map/all_to_all | solution.py:318
  36.0 0.1 pad_add_fusion.where_ref
  36.1 0.0 collective-permute-done.1.chip_ref
  36.1 0.0 collective-permute-done.core_ref
  36.1 0.0 copy-done
  36.1 0.0 copy-done.1
  36.1 0.0 copy-done.2
  36.1 6.2 %video.1 = bf16[512,16,128]{2,1,0:T(8,128)(2,1)} custom-call(s32[4,4]{1,0:T(4,128)S(1)} %copy-done.1, s32[4]{0:T(128)S(1)} %copy-done.2, s32[3]{0:T(128)S(1)} %pad_add_fusion.where_ref, bf16[512,16,128]{2,1,0:T(8,128)(2,1)S(1)} %copy-done, bf16[16,128,128]{2,1,0:T(8,128)(2,1)S(1)} %get-tuple-element.7.own_ref, ...), custom_call_target="tpu_custom_call" | custom-call | flops 536870912 | bytes 33554432 | tf_op jit(solution)/shard_map/video/pallas_call | solution.py:280
  42.3 0.9 %all-to-all-done.1.by_head_ref = bf16[16,64,128]{2,1,0:T(8,128)(2,1)S(1)} async-done(((bf16[16,64,128]{2,1,0:T(8,128)(2,1)}), bf16[16,64,128]{2,1,0:T(8,128)(2,1)S(1)}, u32[]{:S(2)}, u32[]{:S(2)}) %all-to-all-start.1) | async-done | bytes 262176 | tf_op jit(solution)/shard_map/all_to_all | solution.py:318
  43.1 0.8 %collect.1 = bf16[64,16,128]{2,1,0:T(8,128)(2,1)} custom-call(bf16[16,64,128]{2,1,0:T(8,128)(2,1)S(1)} %all-to-all-done.1.by_head_ref), custom_call_target="tpu_custom_call" | custom-call | tf_op jit(solution)/shard_map/collect/pallas_call | solution.py:199
Async XLA Ops:
  2.7 33.4 %copy-start = (bf16[512,16,128]{2,1,0:T(8,128)(2,1)S(1)}, bf16[512,16,128]{2,1,0:T(8,128)(2,1)}, u32[]{:S(2)}) copy-start(bf16[512,16,128]{2,1,0:T(8,128)(2,1)} %video_ref.1) | copy-start | bytes 6291460
  2.7 33.4 %copy-start.1 = (s32[4,4]{1,0:T(4,128)S(1)}, s32[4,4]{1,0:T(4,128)}, u32[]{:S(2)}) copy-start(s32[4,4]{1,0:T(4,128)} %pairs_ref.1) | copy-start | bytes 196
  2.7 33.4 %copy-start.2 = (s32[4]{0:T(128)S(1)}, s32[4]{0:T(128)}, u32[]{:S(2)}) copy-start(s32[4]{0:T(128)} %counts_ref.1) | copy-start | bytes 52
  2.7 26.7 %all-to-all-start = ((bf16[16,4,48,128]{3,2,1,0:T(8,128)(2,1)}), bf16[16,4,48,128]{3,2,1,0:T(8,128)(2,1)S(1)}, u32[]{:S(2)}, u32[]{:S(2)}) async-start(bf16[16,4,48,128]{3,2,1,0:T(8,128)(2,1)} %get-tuple-element.6), calls=%async_computation | async-start | bytes 1572864 | tf_op jit(solution)/shard_map/all_to_all | solution.py:318
  10.5 25.6 %collective-permute-start.1 = (bf16[16,128,128]{2,1,0:T(8,128)(2,1)S(1)}, bf16[16,128,128]{2,1,0:T(8,128)(2,1)}, u32[]{:S(2)}, u32[]{:S(2)}) collective-permute-start(bf16[16,128,128]{2,1,0:T(8,128)(2,1)S(1)} %get-tuple-element.7.own_ref), channel_id=1, source_target_pairs={{1,2},{2,1},{3,4},{4,3},{5,6},{6,5},{7,8},{8,7},{9,10},{10,9},{11,... | collective-permute-start | bytes 1572872 | tf_op jit(solution)/shard_map/ppermute | solution.py:313
  11.9 24.2 %collective-permute-start = (bf16[16,128,128]{2,1,0:T(8,128)(2,1)S(1)}, bf16[16,128,128]{2,1,0:T(8,128)(2,1)}, u32[]{:S(2)}, u32[]{:S(2)}) collective-permute-start(bf16[16,128,128]{2,1,0:T(8,128)(2,1)S(1)} %get-tuple-element.7.own_ref), channel_id=1, source_target_pairs={{0,1},{1,0},{2,3},{3,2},{4,5},{5,4},{6,7},{7,6},{8,9},{9,8},{10,11... | collective-permute-start | bytes 1572872 | tf_op jit(solution)/shard_map/ppermute | solution.py:322
  31.6 11.5 %all-to-all-start.1 = ((bf16[16,64,128]{2,1,0:T(8,128)(2,1)}), bf16[16,64,128]{2,1,0:T(8,128)(2,1)S(1)}, u32[]{:S(2)}, u32[]{:S(2)}) async-start(bf16[16,64,128]{2,1,0:T(8,128)(2,1)} %attend.1), calls=%async_computation.1 | async-start | bytes 524288 | tf_op jit(solution)/shard_map/all_to_all | solution.py:318

commit v17 on v16

--- a/solution.py
+++ b/solution.py
@@ -312,7 +312,7 @@
 
     chip = lax.ppermute(kv, "seq", chip_pairs)
 
-    order = [(devices - 1 - devices // 2 - p) % devices for p in range(devices)]
+    order = [(devices // 2 + p) % devices for p in range(devices)]
 
     def exchange(value):
         return lax.all_to_all(

time: 44.7 us -> 46.8 us (1.047)
  starting transfers between devices: 14.7 us -> 20 us
  waiting for transfers between devices: 17.1 us -> 14.4 us
    all_to_all x2, starting transfers between devices: 12.1 us -> 16.4 us  [exchange(): lax.all_to_all(value, 'seq', split_axis=0, concat_axis=0, tiled=True, axi...]
    all_to_all x2, waiting for transfers between devices: 17.1 us -> 14.4 us  [exchange(): lax.all_to_all(value, 'seq', split_axis=0, concat_axis=0, tiled=True, axi...]
    ppermute x1, starting transfers between devices: 1.21 us -> 2.11 us  [local(): core = lax.ppermute(kv, 'seq', core_pairs)]
  transfers between devices with their start and end apart: 4 -> 4, of which waited for: 2 -> 2; matrix products, arithmetic and copies ran while one was open for 0% -> 0% of each run, Pallas kernels for 19% -> 18%
where the time goes in v17:
time: 46.8 us; the launch traced here: 46.4 us
  starting transfers between devices  20 us (43%)
  waiting for transfers between devices  14.4 us (31%)
  Pallas kernels  11.2 us (24%)
  between operations  0.7 us (1%)
    all_to_all x2, starting transfers between devices, exchange(): lax.all_to_all(value, 'seq', split_axis=0, concat_axis=0, tiled=True, axi...  16.4 us
    all_to_all x2, waiting for transfers between devices, exchange(): lax.all_to_all(value, 'seq', split_axis=0, concat_axis=0, tiled=True, axi...  14.4 us
    pallas_call x1, Pallas kernels, video(): pl.pallas_call(functools.partial(video_kernel, scale, 4), in_specs=[in_sm...  6.18 us
    pallas_call x1, Pallas kernels, attend(): pl.pallas_call(functools.partial(attend_kernel, scale), in_specs=[pl.Bloc...  2.28 us
    ppermute x1, starting transfers between devices, local(): core = lax.ppermute(kv, 'seq', core_pairs)  2.11 us
    pallas_call x1, Pallas kernels, arrange(): pl.pallas_call(functools.partial(arrange_kernel, pieces), in_specs=[pl.Bl...  2.03 us
    ppermute x1, starting transfers between devices, local(): chip = lax.ppermute(kv, 'seq', chip_pairs)  1.44 us
  transfers between devices with their start and end apart: 4, of which 2 were waited for; matrix products, arithmetic and copies ran while one was open for 0% of the time, Pallas kernels for 18%

profile of v17, /device:TPU:0, one launch (start us, length us, event | category | flops | bytes accessed | tf_op | source)
XLA Modules:
  0.0 46.4 jit_solution(10973797867472995703)
XLA Ops:
  0.6 2.0 %arrange.1 = (bf16[16,4,48,128]{3,2,1,0:T(8,128)(2,1)}, bf16[16,128,128]{2,1,0:T(8,128)(2,1)S(1)}) custom-call(bf16[64,3,16,128]{3,2,1,0:T(8,128)(2,1)} %qkv_ref.1), custom_call_target="tpu_custom_call" | custom-call | tf_op jit(solution)/shard_map/arrange/pallas_call | solution.py:56
  2.7 0.0 copy-start
  2.7 0.0 copy-start.1
  2.7 0.0 copy-start.2
  2.7 8.0 %all-to-all-start = ((bf16[16,4,48,128]{3,2,1,0:T(8,128)(2,1)}), bf16[16,4,48,128]{3,2,1,0:T(8,128)(2,1)S(1)}, u32[]{:S(2)}, u32[]{:S(2)}) async-start(bf16[16,4,48,128]{3,2,1,0:T(8,128)(2,1)} %get-tuple-element.6), calls=%async_computation | async-start | bytes 1572864 | tf_op jit(solution)/shard_map/all_to_all | solution.py:318
  10.7 1.4 %collective-permute-start.1 = (bf16[16,128,128]{2,1,0:T(8,128)(2,1)S(1)}, bf16[16,128,128]{2,1,0:T(8,128)(2,1)}, u32[]{:S(2)}, u32[]{:S(2)}) collective-permute-start(bf16[16,128,128]{2,1,0:T(8,128)(2,1)S(1)} %get-tuple-element.7.own_ref), channel_id=1, source_target_pairs={{1,2},{2,1},{3,4},{4,3},{5,6},{6,5},{7,8},{8,7},{9,10},{10,9},{11,... | collective-permute-start | bytes 1572872 | tf_op jit(solution)/shard_map/ppermute | solution.py:313
  12.1 2.1 %collective-permute-start = (bf16[16,128,128]{2,1,0:T(8,128)(2,1)S(1)}, bf16[16,128,128]{2,1,0:T(8,128)(2,1)}, u32[]{:S(2)}, u32[]{:S(2)}) collective-permute-start(bf16[16,128,128]{2,1,0:T(8,128)(2,1)S(1)} %get-tuple-element.7.own_ref), channel_id=1, source_target_pairs={{0,1},{1,0},{2,3},{3,2},{4,5},{5,4},{6,7},{7,6},{8,9},{9,8},{10,11... | collective-permute-start | bytes 1572872 | tf_op jit(solution)/shard_map/ppermute | solution.py:322
  14.3 12.9 %all-to-all-done.recv_ref = bf16[16,4,48,128]{3,2,1,0:T(8,128)(2,1)S(1)} async-done(((bf16[16,4,48,128]{3,2,1,0:T(8,128)(2,1)}), bf16[16,4,48,128]{3,2,1,0:T(8,128)(2,1)S(1)}, u32[]{:S(2)}, u32[]{:S(2)}) %all-to-all-start) | async-done | bytes 786464 | tf_op jit(solution)/shard_map/all_to_all | solution.py:318
  27.2 2.3 %attend.1 = bf16[16,64,128]{2,1,0:T(8,128)(2,1)} custom-call(bf16[16,4,48,128]{3,2,1,0:T(8,128)(2,1)S(1)} %all-to-all-done.recv_ref), custom_call_target="tpu_custom_call" | custom-call | flops 536870912 | bytes 1048576 | tf_op jit(solution)/shard_map/attend/pallas_call | solution.py:125
  29.4 8.4 %all-to-all-start.1 = ((bf16[16,64,128]{2,1,0:T(8,128)(2,1)}), bf16[16,64,128]{2,1,0:T(8,128)(2,1)S(1)}, u32[]{:S(2)}, u32[]{:S(2)}) async-start(bf16[16,64,128]{2,1,0:T(8,128)(2,1)} %attend.1), calls=%async_computation.1 | async-start | bytes 524288 | tf_op jit(solution)/shard_map/all_to_all | solution.py:318
  37.9 0.1 pad_add_fusion.where_ref
  38.0 0.0 collective-permute-done.1.chip_ref
  38.0 0.0 collective-permute-done.core_ref
  38.0 0.0 copy-done
  38.0 0.0 copy-done.1
  38.0 0.0 copy-done.2
  38.0 6.2 %video.1 = bf16[512,16,128]{2,1,0:T(8,128)(2,1)} custom-call(s32[4,4]{1,0:T(4,128)S(1)} %copy-done.1, s32[4]{0:T(128)S(1)} %copy-done.2, s32[3]{0:T(128)S(1)} %pad_add_fusion.where_ref, bf16[512,16,128]{2,1,0:T(8,128)(2,1)S(1)} %copy-done, bf16[16,128,128]{2,1,0:T(8,128)(2,1)S(1)} %get-tuple-element.7.own_ref, ...), custom_call_target="tpu_custom_call" | custom-call | flops 536870912 | bytes 33554432 | tf_op jit(solution)/shard_map/video/pallas_call | solution.py:280
  44.2 1.5 %all-to-all-done.1.by_head_ref = bf16[16,64,128]{2,1,0:T(8,128)(2,1)S(1)} async-done(((bf16[16,64,128]{2,1,0:T(8,128)(2,1)}), bf16[16,64,128]{2,1,0:T(8,128)(2,1)S(1)}, u32[]{:S(2)}, u32[]{:S(2)}) %all-to-all-start.1) | async-done | bytes 262176 | tf_op jit(solution)/shard_map/all_to_all | solution.py:318
  45.6 0.8 %collect.1 = bf16[64,16,128]{2,1,0:T(8,128)(2,1)} custom-call(bf16[16,64,128]{2,1,0:T(8,128)(2,1)S(1)} %all-to-all-done.1.by_head_ref), custom_call_target="tpu_custom_call" | custom-call | tf_op jit(solution)/shard_map/collect/pallas_call | solution.py:199
Async XLA Ops:
  2.7 35.3 %copy-start = (bf16[512,16,128]{2,1,0:T(8,128)(2,1)S(1)}, bf16[512,16,128]{2,1,0:T(8,128)(2,1)}, u32[]{:S(2)}) copy-start(bf16[512,16,128]{2,1,0:T(8,128)(2,1)} %video_ref.1) | copy-start | bytes 6291460
  2.7 35.3 %copy-start.1 = (s32[4,4]{1,0:T(4,128)S(1)}, s32[4,4]{1,0:T(4,128)}, u32[]{:S(2)}) copy-start(s32[4,4]{1,0:T(4,128)} %pairs_ref.1) | copy-start | bytes 196
  2.7 35.3 %copy-start.2 = (s32[4]{0:T(128)S(1)}, s32[4]{0:T(128)}, u32[]{:S(2)}) copy-start(s32[4]{0:T(128)} %counts_ref.1) | copy-start | bytes 52
  2.7 24.4 %all-to-all-start = ((bf16[16,4,48,128]{3,2,1,0:T(8,128)(2,1)}), bf16[16,4,48,128]{3,2,1,0:T(8,128)(2,1)S(1)}, u32[]{:S(2)}, u32[]{:S(2)}) async-start(bf16[16,4,48,128]{3,2,1,0:T(8,128)(2,1)} %get-tuple-element.6), calls=%async_computation | async-start | bytes 1572864 | tf_op jit(solution)/shard_map/all_to_all | solution.py:318
  10.7 27.2 %collective-permute-start.1 = (bf16[16,128,128]{2,1,0:T(8,128)(2,1)S(1)}, bf16[16,128,128]{2,1,0:T(8,128)(2,1)}, u32[]{:S(2)}, u32[]{:S(2)}) collective-permute-start(bf16[16,128,128]{2,1,0:T(8,128)(2,1)S(1)} %get-tuple-element.7.own_ref), channel_id=1, source_target_pairs={{1,2},{2,1},{3,4},{4,3},{5,6},{6,5},{7,8},{8,7},{9,10},{10,9},{11,... | collective-permute-start | bytes 1572872 | tf_op jit(solution)/shard_map/ppermute | solution.py:313
  12.1 25.8 %collective-permute-start = (bf16[16,128,128]{2,1,0:T(8,128)(2,1)S(1)}, bf16[16,128,128]{2,1,0:T(8,128)(2,1)}, u32[]{:S(2)}, u32[]{:S(2)}) collective-permute-start(bf16[16,128,128]{2,1,0:T(8,128)(2,1)S(1)} %get-tuple-element.7.own_ref), channel_id=1, source_target_pairs={{0,1},{1,0},{2,3},{3,2},{4,5},{5,4},{6,7},{7,6},{8,9},{9,8},{10,11... | collective-permute-start | bytes 1572872 | tf_op jit(solution)/shard_map/ppermute | solution.py:322
  29.4 16.2 %all-to-all-start.1 = ((bf16[16,64,128]{2,1,0:T(8,128)(2,1)}), bf16[16,64,128]{2,1,0:T(8,128)(2,1)S(1)}, u32[]{:S(2)}, u32[]{:S(2)}) async-start(bf16[16,64,128]{2,1,0:T(8,128)(2,1)} %attend.1), calls=%async_computation.1 | async-start | bytes 524288 | tf_op jit(solution)/shard_map/all_to_all | solution.py:318

commit v18 on v17

--- a/solution.py
+++ b/solution.py
@@ -312,7 +312,8 @@
 
     chip = lax.ppermute(kv, "seq", chip_pairs)
 
-    order = [(devices // 2 + p) % devices for p in range(devices)]
+    plane = devices // 4
+    order = [z * plane + plane - 1 - r for z in (1, 3, 0, 2) for r in range(plane)]
 
     def exchange(value):
         return lax.all_to_all(

time: 46.8 us -> 44.9 us (0.959)
  starting transfers between devices: 20 us -> 14.9 us
  waiting for transfers between devices: 14.4 us -> 17.3 us
    all_to_all x2, starting transfers between devices: 16.4 us -> 12.3 us  [exchange(): lax.all_to_all(value, 'seq', split_axis=0, concat_axis=0, tiled=True, axi...]
    all_to_all x2, waiting for transfers between devices: 14.4 us -> 17.3 us  [exchange(): lax.all_to_all(value, 'seq', split_axis=0, concat_axis=0, tiled=True, axi...]
    ppermute x1, starting transfers between devices: 2.11 us -> 1.21 us  [local(): core = lax.ppermute(kv, 'seq', core_pairs)]
  transfers between devices with their start and end apart: 4 -> 4, of which waited for: 2 -> 2; matrix products, arithmetic and copies ran while one was open for 0% -> 0% of each run, Pallas kernels for 18% -> 19%
where the time goes in v18:
time: 44.9 us; the launch traced here: 44.2 us
  waiting for transfers between devices  17.3 us (39%)
  starting transfers between devices  14.9 us (33%)
  Pallas kernels  11.3 us (25%)
  between operations  0.7 us (2%)
    all_to_all x2, waiting for transfers between devices, exchange(): lax.all_to_all(value, 'seq', split_axis=0, concat_axis=0, tiled=True, axi...  17.3 us
    all_to_all x2, starting transfers between devices, exchange(): lax.all_to_all(value, 'seq', split_axis=0, concat_axis=0, tiled=True, axi...  12.3 us
    pallas_call x1, Pallas kernels, video(): pl.pallas_call(functools.partial(video_kernel, scale, 4), in_specs=[in_sm...  6.18 us
    pallas_call x1, Pallas kernels, attend(): pl.pallas_call(functools.partial(attend_kernel, scale), in_specs=[pl.Bloc...  2.28 us
    pallas_call x1, Pallas kernels, arrange(): pl.pallas_call(functools.partial(arrange_kernel, pieces), in_specs=[pl.Bl...  2.03 us
    ppermute x1, starting transfers between devices, local(): chip = lax.ppermute(kv, 'seq', chip_pairs)  1.44 us
    ppermute x1, starting transfers between devices, local(): core = lax.ppermute(kv, 'seq', core_pairs)  1.21 us
  transfers between devices with their start and end apart: 4, of which 2 were waited for; matrix products, arithmetic and copies ran while one was open for 0% of the time, Pallas kernels for 19%

profile of v18, /device:TPU:0, one launch (start us, length us, event | category | flops | bytes accessed | tf_op | source)
XLA Modules:
  0.0 44.2 jit_solution(18133881672562633235)
XLA Ops:
  0.6 2.0 %arrange.1 = (bf16[16,4,48,128]{3,2,1,0:T(8,128)(2,1)}, bf16[16,128,128]{2,1,0:T(8,128)(2,1)S(1)}) custom-call(bf16[64,3,16,128]{3,2,1,0:T(8,128)(2,1)} %qkv_ref.1), custom_call_target="tpu_custom_call" | custom-call | tf_op jit(solution)/shard_map/arrange/pallas_call | solution.py:56
  2.7 0.0 copy-start
  2.7 0.0 copy-start.1
  2.7 0.0 copy-start.2
  2.7 7.8 %all-to-all-start = ((bf16[16,4,48,128]{3,2,1,0:T(8,128)(2,1)}), bf16[16,4,48,128]{3,2,1,0:T(8,128)(2,1)S(1)}, u32[]{:S(2)}, u32[]{:S(2)}) async-start(bf16[16,4,48,128]{3,2,1,0:T(8,128)(2,1)} %get-tuple-element.6), calls=%async_computation | async-start | bytes 1572864 | tf_op jit(solution)/shard_map/all_to_all | solution.py:319
  10.5 1.4 %collective-permute-start.1 = (bf16[16,128,128]{2,1,0:T(8,128)(2,1)S(1)}, bf16[16,128,128]{2,1,0:T(8,128)(2,1)}, u32[]{:S(2)}, u32[]{:S(2)}) collective-permute-start(bf16[16,128,128]{2,1,0:T(8,128)(2,1)S(1)} %get-tuple-element.7.own_ref), channel_id=1, source_target_pairs={{1,2},{2,1},{3,4},{4,3},{5,6},{6,5},{7,8},{8,7},{9,10},{10,9},{11,... | collective-permute-start | bytes 1572872 | tf_op jit(solution)/shard_map/ppermute | solution.py:313
  11.9 1.2 %collective-permute-start = (bf16[16,128,128]{2,1,0:T(8,128)(2,1)S(1)}, bf16[16,128,128]{2,1,0:T(8,128)(2,1)}, u32[]{:S(2)}, u32[]{:S(2)}) collective-permute-start(bf16[16,128,128]{2,1,0:T(8,128)(2,1)S(1)} %get-tuple-element.7.own_ref), channel_id=1, source_target_pairs={{0,1},{1,0},{2,3},{3,2},{4,5},{5,4},{6,7},{7,6},{8,9},{9,8},{10,11... | collective-permute-start | bytes 1572872 | tf_op jit(solution)/shard_map/ppermute | solution.py:323
  13.1 16.2 %all-to-all-done.recv_ref = bf16[16,4,48,128]{3,2,1,0:T(8,128)(2,1)S(1)} async-done(((bf16[16,4,48,128]{3,2,1,0:T(8,128)(2,1)}), bf16[16,4,48,128]{3,2,1,0:T(8,128)(2,1)S(1)}, u32[]{:S(2)}, u32[]{:S(2)}) %all-to-all-start) | async-done | bytes 786464 | tf_op jit(solution)/shard_map/all_to_all | solution.py:319
  29.4 2.3 %attend.1 = bf16[16,64,128]{2,1,0:T(8,128)(2,1)} custom-call(bf16[16,4,48,128]{3,2,1,0:T(8,128)(2,1)S(1)} %all-to-all-done.recv_ref), custom_call_target="tpu_custom_call" | custom-call | flops 536870912 | bytes 1048576 | tf_op jit(solution)/shard_map/attend/pallas_call | solution.py:125
  31.6 4.5 %all-to-all-start.1 = ((bf16[16,64,128]{2,1,0:T(8,128)(2,1)}), bf16[16,64,128]{2,1,0:T(8,128)(2,1)S(1)}, u32[]{:S(2)}, u32[]{:S(2)}) async-start(bf16[16,64,128]{2,1,0:T(8,128)(2,1)} %attend.1), calls=%async_computation.1 | async-start | bytes 524288 | tf_op jit(solution)/shard_map/all_to_all | solution.py:319
  36.2 0.1 pad_add_fusion.where_ref
  36.3 0.0 collective-permute-done.1.chip_ref
  36.3 0.0 collective-permute-done.core_ref
  36.3 0.0 copy-done
  36.3 0.0 copy-done.1
  36.3 0.0 copy-done.2
  36.3 6.2 %video.1 = bf16[512,16,128]{2,1,0:T(8,128)(2,1)} custom-call(s32[4,4]{1,0:T(4,128)S(1)} %copy-done.1, s32[4]{0:T(128)S(1)} %copy-done.2, s32[3]{0:T(128)S(1)} %pad_add_fusion.where_ref, bf16[512,16,128]{2,1,0:T(8,128)(2,1)S(1)} %copy-done, bf16[16,128,128]{2,1,0:T(8,128)(2,1)S(1)} %get-tuple-element.7.own_ref, ...), custom_call_target="tpu_custom_call" | custom-call | flops 536870912 | bytes 33554432 | tf_op jit(solution)/shard_map/video/pallas_call | solution.py:280
  42.5 1.0 %all-to-all-done.1.by_head_ref = bf16[16,64,128]{2,1,0:T(8,128)(2,1)S(1)} async-done(((bf16[16,64,128]{2,1,0:T(8,128)(2,1)}), bf16[16,64,128]{2,1,0:T(8,128)(2,1)S(1)}, u32[]{:S(2)}, u32[]{:S(2)}) %all-to-all-start.1) | async-done | bytes 262176 | tf_op jit(solution)/shard_map/all_to_all | solution.py:319
  43.5 0.8 %collect.1 = bf16[64,16,128]{2,1,0:T(8,128)(2,1)} custom-call(bf16[16,64,128]{2,1,0:T(8,128)(2,1)S(1)} %all-to-all-done.1.by_head_ref), custom_call_target="tpu_custom_call" | custom-call | tf_op jit(solution)/shard_map/collect/pallas_call | solution.py:199
Async XLA Ops:
  2.7 33.6 %copy-start = (bf16[512,16,128]{2,1,0:T(8,128)(2,1)S(1)}, bf16[512,16,128]{2,1,0:T(8,128)(2,1)}, u32[]{:S(2)}) copy-start(bf16[512,16,128]{2,1,0:T(8,128)(2,1)} %video_ref.1) | copy-start | bytes 6291460
  2.7 33.6 %copy-start.1 = (s32[4,4]{1,0:T(4,128)S(1)}, s32[4,4]{1,0:T(4,128)}, u32[]{:S(2)}) copy-start(s32[4,4]{1,0:T(4,128)} %pairs_ref.1) | copy-start | bytes 196
  2.7 33.6 %copy-start.2 = (s32[4]{0:T(128)S(1)}, s32[4]{0:T(128)}, u32[]{:S(2)}) copy-start(s32[4]{0:T(128)} %counts_ref.1) | copy-start | bytes 52
  2.7 26.7 %all-to-all-start = ((bf16[16,4,48,128]{3,2,1,0:T(8,128)(2,1)}), bf16[16,4,48,128]{3,2,1,0:T(8,128)(2,1)S(1)}, u32[]{:S(2)}, u32[]{:S(2)}) async-start(bf16[16,4,48,128]{3,2,1,0:T(8,128)(2,1)} %get-tuple-element.6), calls=%async_computation | async-start | bytes 1572864 | tf_op jit(solution)/shard_map/all_to_all | solution.py:319
  10.5 25.8 %collective-permute-start.1 = (bf16[16,128,128]{2,1,0:T(8,128)(2,1)S(1)}, bf16[16,128,128]{2,1,0:T(8,128)(2,1)}, u32[]{:S(2)}, u32[]{:S(2)}) collective-permute-start(bf16[16,128,128]{2,1,0:T(8,128)(2,1)S(1)} %get-tuple-element.7.own_ref), channel_id=1, source_target_pairs={{1,2},{2,1},{3,4},{4,3},{5,6},{6,5},{7,8},{8,7},{9,10},{10,9},{11,... | collective-permute-start | bytes 1572872 | tf_op jit(solution)/shard_map/ppermute | solution.py:313
  11.9 24.4 %collective-permute-start = (bf16[16,128,128]{2,1,0:T(8,128)(2,1)S(1)}, bf16[16,128,128]{2,1,0:T(8,128)(2,1)}, u32[]{:S(2)}, u32[]{:S(2)}) collective-permute-start(bf16[16,128,128]{2,1,0:T(8,128)(2,1)S(1)} %get-tuple-element.7.own_ref), channel_id=1, source_target_pairs={{0,1},{1,0},{2,3},{3,2},{4,5},{5,4},{6,7},{7,6},{8,9},{9,8},{10,11... | collective-permute-start | bytes 1572872 | tf_op jit(solution)/shard_map/ppermute | solution.py:323
  31.6 11.8 %all-to-all-start.1 = ((bf16[16,64,128]{2,1,0:T(8,128)(2,1)}), bf16[16,64,128]{2,1,0:T(8,128)(2,1)S(1)}, u32[]{:S(2)}, u32[]{:S(2)}) async-start(bf16[16,64,128]{2,1,0:T(8,128)(2,1)} %attend.1), calls=%async_computation.1 | async-start | bytes 524288 | tf_op jit(solution)/shard_map/all_to_all | solution.py:319

commit v19 on v18

--- a/solution.py
+++ b/solution.py
@@ -313,7 +313,7 @@
     chip = lax.ppermute(kv, "seq", chip_pairs)
 
     plane = devices // 4
-    order = [z * plane + plane - 1 - r for z in (1, 3, 0, 2) for r in range(plane)]
+    order = [z * plane + plane - 1 - r for r in range(plane) for z in (1, 0, 3, 2)]
 
     def exchange(value):
         return lax.all_to_all(

time: 44.9 us -> 45.6 us (1.016)
  starting transfers between devices: 14.9 us -> 15.6 us
    all_to_all x2, starting transfers between devices: 12.3 us -> 12.9 us  [exchange(): lax.all_to_all(value, 'seq', split_axis=0, concat_axis=0, tiled=True, axi...]
where the time goes in v19:
time: 45.6 us; the launch traced here: 45.2 us
  waiting for transfers between devices  17.6 us (39%)
  starting transfers between devices  15.6 us (34%)
  Pallas kernels  11.2 us (25%)
  between operations  0.7 us (2%)
    all_to_all x2, waiting for transfers between devices, exchange(): lax.all_to_all(value, 'seq', split_axis=0, concat_axis=0, tiled=True, axi...  17.6 us
    all_to_all x2, starting transfers between devices, exchange(): lax.all_to_all(value, 'seq', split_axis=0, concat_axis=0, tiled=True, axi...  12.9 us
    pallas_call x1, Pallas kernels, video(): pl.pallas_call(functools.partial(video_kernel, scale, 4), in_specs=[in_sm...  6.16 us
    pallas_call x1, Pallas kernels, attend(): pl.pallas_call(functools.partial(attend_kernel, scale), in_specs=[pl.Bloc...  2.28 us
    pallas_call x1, Pallas kernels, arrange(): pl.pallas_call(functools.partial(arrange_kernel, pieces), in_specs=[pl.Bl...  2.03 us
    ppermute x1, starting transfers between devices, local(): chip = lax.ppermute(kv, 'seq', chip_pairs)  1.44 us
    ppermute x1, starting transfers between devices, local(): core = lax.ppermute(kv, 'seq', core_pairs)  1.21 us
  transfers between devices with their start and end apart: 4, of which 2 were waited for; matrix products, arithmetic and copies ran while one was open for 0% of the time, Pallas kernels for 19%

profile of v19, /device:TPU:0, one launch (start us, length us, event | category | flops | bytes accessed | tf_op | source)
XLA Modules:
  0.0 45.2 jit_solution(10447437232509221786)
XLA Ops:
  0.6 2.0 %arrange.1 = (bf16[16,4,48,128]{3,2,1,0:T(8,128)(2,1)}, bf16[16,128,128]{2,1,0:T(8,128)(2,1)S(1)}) custom-call(bf16[64,3,16,128]{3,2,1,0:T(8,128)(2,1)} %qkv_ref.1), custom_call_target="tpu_custom_call" | custom-call | tf_op jit(solution)/shard_map/arrange/pallas_call | solution.py:56
  2.7 0.0 copy-start
  2.7 0.0 copy-start.1
  2.7 0.0 copy-start.2
  2.7 7.8 %all-to-all-start = ((bf16[16,4,48,128]{3,2,1,0:T(8,128)(2,1)}), bf16[16,4,48,128]{3,2,1,0:T(8,128)(2,1)S(1)}, u32[]{:S(2)}, u32[]{:S(2)}) async-start(bf16[16,4,48,128]{3,2,1,0:T(8,128)(2,1)} %get-tuple-element.6), calls=%async_computation | async-start | bytes 1572864 | tf_op jit(solution)/shard_map/all_to_all | solution.py:319
  10.5 1.4 %collective-permute-start.1 = (bf16[16,128,128]{2,1,0:T(8,128)(2,1)S(1)}, bf16[16,128,128]{2,1,0:T(8,128)(2,1)}, u32[]{:S(2)}, u32[]{:S(2)}) collective-permute-start(bf16[16,128,128]{2,1,0:T(8,128)(2,1)S(1)} %get-tuple-element.7.own_ref), channel_id=1, source_target_pairs={{1,2},{2,1},{3,4},{4,3},{5,6},{6,5},{7,8},{8,7},{9,10},{10,9},{11,... | collective-permute-start | bytes 1572872 | tf_op jit(solution)/shard_map/ppermute | solution.py:313
  11.9 1.2 %collective-permute-start = (bf16[16,128,128]{2,1,0:T(8,128)(2,1)S(1)}, bf16[16,128,128]{2,1,0:T(8,128)(2,1)}, u32[]{:S(2)}, u32[]{:S(2)}) collective-permute-start(bf16[16,128,128]{2,1,0:T(8,128)(2,1)S(1)} %get-tuple-element.7.own_ref), channel_id=1, source_target_pairs={{0,1},{1,0},{2,3},{3,2},{4,5},{5,4},{6,7},{7,6},{8,9},{9,8},{10,11... | collective-permute-start | bytes 1572872 | tf_op jit(solution)/shard_map/ppermute | solution.py:323
  13.1 16.3 %all-to-all-done.recv_ref = bf16[16,4,48,128]{3,2,1,0:T(8,128)(2,1)S(1)} async-done(((bf16[16,4,48,128]{3,2,1,0:T(8,128)(2,1)}), bf16[16,4,48,128]{3,2,1,0:T(8,128)(2,1)S(1)}, u32[]{:S(2)}, u32[]{:S(2)}) %all-to-all-start) | async-done | bytes 786464 | tf_op jit(solution)/shard_map/all_to_all | solution.py:319
  29.4 2.3 %attend.1 = bf16[16,64,128]{2,1,0:T(8,128)(2,1)} custom-call(bf16[16,4,48,128]{3,2,1,0:T(8,128)(2,1)S(1)} %all-to-all-done.recv_ref), custom_call_target="tpu_custom_call" | custom-call | flops 536870912 | bytes 1048576 | tf_op jit(solution)/shard_map/attend/pallas_call | solution.py:125
  31.7 5.2 %all-to-all-start.1 = ((bf16[16,64,128]{2,1,0:T(8,128)(2,1)}), bf16[16,64,128]{2,1,0:T(8,128)(2,1)S(1)}, u32[]{:S(2)}, u32[]{:S(2)}) async-start(bf16[16,64,128]{2,1,0:T(8,128)(2,1)} %attend.1), calls=%async_computation.1 | async-start | bytes 524288 | tf_op jit(solution)/shard_map/all_to_all | solution.py:319
  36.9 0.1 pad_add_fusion.where_ref
  37.0 0.0 collective-permute-done.1.chip_ref
  37.0 0.0 collective-permute-done.core_ref
  37.0 0.0 copy-done
  37.0 0.0 copy-done.1
  37.0 0.0 copy-done.2
  37.0 6.2 %video.1 = bf16[512,16,128]{2,1,0:T(8,128)(2,1)} custom-call(s32[4,4]{1,0:T(4,128)S(1)} %copy-done.1, s32[4]{0:T(128)S(1)} %copy-done.2, s32[3]{0:T(128)S(1)} %pad_add_fusion.where_ref, bf16[512,16,128]{2,1,0:T(8,128)(2,1)S(1)} %copy-done, bf16[16,128,128]{2,1,0:T(8,128)(2,1)S(1)} %get-tuple-element.7.own_ref, ...), custom_call_target="tpu_custom_call" | custom-call | flops 536870912 | bytes 33554432 | tf_op jit(solution)/shard_map/video/pallas_call | solution.py:280
  43.2 1.3 %all-to-all-done.1.by_head_ref = bf16[16,64,128]{2,1,0:T(8,128)(2,1)S(1)} async-done(((bf16[16,64,128]{2,1,0:T(8,128)(2,1)}), bf16[16,64,128]{2,1,0:T(8,128)(2,1)S(1)}, u32[]{:S(2)}, u32[]{:S(2)}) %all-to-all-start.1) | async-done | bytes 262176 | tf_op jit(solution)/shard_map/all_to_all | solution.py:319
  44.4 0.8 %collect.1 = bf16[64,16,128]{2,1,0:T(8,128)(2,1)} custom-call(bf16[16,64,128]{2,1,0:T(8,128)(2,1)S(1)} %all-to-all-done.1.by_head_ref), custom_call_target="tpu_custom_call" | custom-call | tf_op jit(solution)/shard_map/collect/pallas_call | solution.py:199
Async XLA Ops:
  2.7 34.3 %copy-start = (bf16[512,16,128]{2,1,0:T(8,128)(2,1)S(1)}, bf16[512,16,128]{2,1,0:T(8,128)(2,1)}, u32[]{:S(2)}) copy-start(bf16[512,16,128]{2,1,0:T(8,128)(2,1)} %video_ref.1) | copy-start | bytes 6291460
  2.7 34.3 %copy-start.1 = (s32[4,4]{1,0:T(4,128)S(1)}, s32[4,4]{1,0:T(4,128)}, u32[]{:S(2)}) copy-start(s32[4,4]{1,0:T(4,128)} %pairs_ref.1) | copy-start | bytes 196
  2.7 34.3 %copy-start.2 = (s32[4]{0:T(128)S(1)}, s32[4]{0:T(128)}, u32[]{:S(2)}) copy-start(s32[4]{0:T(128)} %counts_ref.1) | copy-start | bytes 52
  2.7 26.7 %all-to-all-start = ((bf16[16,4,48,128]{3,2,1,0:T(8,128)(2,1)}), bf16[16,4,48,128]{3,2,1,0:T(8,128)(2,1)S(1)}, u32[]{:S(2)}, u32[]{:S(2)}) async-start(bf16[16,4,48,128]{3,2,1,0:T(8,128)(2,1)} %get-tuple-element.6), calls=%async_computation | async-start | bytes 1572864 | tf_op jit(solution)/shard_map/all_to_all | solution.py:319
  10.5 26.5 %collective-permute-start.1 = (bf16[16,128,128]{2,1,0:T(8,128)(2,1)S(1)}, bf16[16,128,128]{2,1,0:T(8,128)(2,1)}, u32[]{:S(2)}, u32[]{:S(2)}) collective-permute-start(bf16[16,128,128]{2,1,0:T(8,128)(2,1)S(1)} %get-tuple-element.7.own_ref), channel_id=1, source_target_pairs={{1,2},{2,1},{3,4},{4,3},{5,6},{6,5},{7,8},{8,7},{9,10},{10,9},{11,... | collective-permute-start | bytes 1572872 | tf_op jit(solution)/shard_map/ppermute | solution.py:313
  11.9 25.1 %collective-permute-start = (bf16[16,128,128]{2,1,0:T(8,128)(2,1)S(1)}, bf16[16,128,128]{2,1,0:T(8,128)(2,1)}, u32[]{:S(2)}, u32[]{:S(2)}) collective-permute-start(bf16[16,128,128]{2,1,0:T(8,128)(2,1)S(1)} %get-tuple-element.7.own_ref), channel_id=1, source_target_pairs={{0,1},{1,0},{2,3},{3,2},{4,5},{5,4},{6,7},{7,6},{8,9},{9,8},{10,11... | collective-permute-start | bytes 1572872 | tf_op jit(solution)/shard_map/ppermute | solution.py:323
  31.7 12.7 %all-to-all-start.1 = ((bf16[16,64,128]{2,1,0:T(8,128)(2,1)}), bf16[16,64,128]{2,1,0:T(8,128)(2,1)S(1)}, u32[]{:S(2)}, u32[]{:S(2)}) async-start(bf16[16,64,128]{2,1,0:T(8,128)(2,1)} %attend.1), calls=%async_computation.1 | async-start | bytes 524288 | tf_op jit(solution)/shard_map/all_to_all | solution.py:319

commit v20 on v16

--- a/solution.py
+++ b/solution.py
@@ -81,16 +81,17 @@
     )
 
 
-def attend_kernel(scale, recv_ref, out_ref, held, sems):
+def attend_kernel(scale, recv_ref, out_ref, held, values_ref, sems):
     sources, pieces, unused, size = recv_ref.shape
     total = sources * pieces * PIECE
     chunk = total // sems.shape[0]
     group = chunk // (pieces * PIECE)
     factor = scale * LOG2E
     keys = recv_ref[:, :, PIECE : 2 * PIECE].reshape(total, size)
-    values = recv_ref[:, :, 2 * PIECE :].reshape(total, size)
+    values_ref[:, :size] = recv_ref[:, :, 2 * PIECE :].reshape(total, size)
+    values_ref[:, size:] = jnp.ones((total, size), jnp.bfloat16)
     chunks = total // chunk
-    scores, weights, sums, departures = {}, {}, {}, []
+    scores, weights, departures = {}, {}, []
     for step in range(chunks + 2):
         if step < chunks:
             first = step * group
@@ -99,14 +100,12 @@
         if 0 <= step - 1 < chunks:
             now = scores.pop(step - 1)
             top = jnp.max(now, axis=1, keepdims=True)
-            exact = jnp.exp2((now - top) * factor)
-            sums[step - 1] = jnp.sum(exact, axis=1, keepdims=True)
-            weights[step - 1] = exact.astype(jnp.bfloat16)
+            weights[step - 1] = jnp.exp2((now - top) * factor).astype(jnp.bfloat16)
         if step >= 2:
             summed = jnp.dot(
-                weights.pop(step - 2), values, preferred_element_type=jnp.float32
+                weights.pop(step - 2), values_ref[...], preferred_element_type=jnp.float32
             )
-            result = (summed / sums.pop(step - 2)).astype(jnp.bfloat16)
+            result = (summed[:, :size] / summed[:, size:]).astype(jnp.bfloat16)
             at = (step - 2) * group
             held[at : at + group] = result.reshape(group, pieces * PIECE, size)
             departure = pltpu.make_async_copy(
@@ -129,6 +128,7 @@
         out_shape=pltpu.HBM((sources, rows, size), jnp.bfloat16),
         scratch_shapes=[
             pltpu.VMEM((sources, rows, size), jnp.bfloat16),
+            pltpu.VMEM((total, 2 * size), jnp.bfloat16),
             pltpu.SemaphoreType.DMA((total // 128,)),
         ],
         compiler_params=params(),

time: 44.7 us -> 44.9 us (level)
  transfers between devices with their start and end apart: 4 -> 4, of which waited for: 2 -> 2; matrix products, arithmetic and copies ran while one was open for 0% -> 0% of each run, Pallas kernels for 19% -> 20%
where the time goes in v20:
time: 44.9 us; the launch traced here: 44.1 us
  waiting for transfers between devices  17.1 us (38%)
  starting transfers between devices  14.7 us (33%)
  Pallas kernels  11.4 us (25%)
  between operations  0.7 us (2%)
    all_to_all x2, waiting for transfers between devices, exchange(): lax.all_to_all(value, 'seq', split_axis=0, concat_axis=0, tiled=True, axi...  17.1 us
    all_to_all x2, starting transfers between devices, exchange(): lax.all_to_all(value, 'seq', split_axis=0, concat_axis=0, tiled=True, axi...  12.1 us
    pallas_call x1, Pallas kernels, video(): pl.pallas_call(functools.partial(video_kernel, scale, 4), in_specs=[in_sm...  6.17 us
    pallas_call x1, Pallas kernels, attend(): pl.pallas_call(functools.partial(attend_kernel, scale), in_specs=[pl.Bloc...  2.44 us
    pallas_call x1, Pallas kernels, arrange(): pl.pallas_call(functools.partial(arrange_kernel, pieces), in_specs=[pl.Bl...  2.03 us
    ppermute x1, starting transfers between devices, local(): chip = lax.ppermute(kv, 'seq', chip_pairs)  1.44 us
    ppermute x1, starting transfers between devices, local(): core = lax.ppermute(kv, 'seq', core_pairs)  1.21 us
  transfers between devices with their start and end apart: 4, of which 2 were waited for; matrix products, arithmetic and copies ran while one was open for 0% of the time, Pallas kernels for 20%

profile of v20, /device:TPU:0, one launch (start us, length us, event | category | flops | bytes accessed | tf_op | source)
XLA Modules:
  0.0 44.1 jit_solution(17850428929624882013)
XLA Ops:
  0.6 2.0 %arrange.1 = (bf16[16,4,48,128]{3,2,1,0:T(8,128)(2,1)}, bf16[16,128,128]{2,1,0:T(8,128)(2,1)S(1)}) custom-call(bf16[64,3,16,128]{3,2,1,0:T(8,128)(2,1)} %qkv_ref.1), custom_call_target="tpu_custom_call" | custom-call | tf_op jit(solution)/shard_map/arrange/pallas_call | solution.py:56
  2.7 0.0 copy-start
  2.7 0.0 copy-start.1
  2.7 0.0 copy-start.2
  2.7 7.8 %all-to-all-start = ((bf16[16,4,48,128]{3,2,1,0:T(8,128)(2,1)}), bf16[16,4,48,128]{3,2,1,0:T(8,128)(2,1)S(1)}, u32[]{:S(2)}, u32[]{:S(2)}) async-start(bf16[16,4,48,128]{3,2,1,0:T(8,128)(2,1)} %get-tuple-element.6), calls=%async_computation | async-start | bytes 1572864 | tf_op jit(solution)/shard_map/all_to_all | solution.py:318
  10.5 1.4 %collective-permute-start.1 = (bf16[16,128,128]{2,1,0:T(8,128)(2,1)S(1)}, bf16[16,128,128]{2,1,0:T(8,128)(2,1)}, u32[]{:S(2)}, u32[]{:S(2)}) collective-permute-start(bf16[16,128,128]{2,1,0:T(8,128)(2,1)S(1)} %get-tuple-element.7.own_ref), channel_id=1, source_target_pairs={{1,2},{2,1},{3,4},{4,3},{5,6},{6,5},{7,8},{8,7},{9,10},{10,9},{11,... | collective-permute-start | bytes 1572872 | tf_op jit(solution)/shard_map/ppermute | solution.py:313
  11.9 1.2 %collective-permute-start = (bf16[16,128,128]{2,1,0:T(8,128)(2,1)S(1)}, bf16[16,128,128]{2,1,0:T(8,128)(2,1)}, u32[]{:S(2)}, u32[]{:S(2)}) collective-permute-start(bf16[16,128,128]{2,1,0:T(8,128)(2,1)S(1)} %get-tuple-element.7.own_ref), channel_id=1, source_target_pairs={{0,1},{1,0},{2,3},{3,2},{4,5},{5,4},{6,7},{7,6},{8,9},{9,8},{10,11... | collective-permute-start | bytes 1572872 | tf_op jit(solution)/shard_map/ppermute | solution.py:322
  13.1 16.2 %all-to-all-done.recv_ref = bf16[16,4,48,128]{3,2,1,0:T(8,128)(2,1)S(1)} async-done(((bf16[16,4,48,128]{3,2,1,0:T(8,128)(2,1)}), bf16[16,4,48,128]{3,2,1,0:T(8,128)(2,1)S(1)}, u32[]{:S(2)}, u32[]{:S(2)}) %all-to-all-start) | async-done | bytes 786464 | tf_op jit(solution)/shard_map/all_to_all | solution.py:318
  29.4 2.4 %attend.1 = bf16[16,64,128]{2,1,0:T(8,128)(2,1)} custom-call(bf16[16,4,48,128]{3,2,1,0:T(8,128)(2,1)S(1)} %all-to-all-done.recv_ref), custom_call_target="tpu_custom_call" | custom-call | flops 536870912 | bytes 1048576 | tf_op jit(solution)/shard_map/attend/pallas_call | solution.py:124
  31.8 4.3 %all-to-all-start.1 = ((bf16[16,64,128]{2,1,0:T(8,128)(2,1)}), bf16[16,64,128]{2,1,0:T(8,128)(2,1)S(1)}, u32[]{:S(2)}, u32[]{:S(2)}) async-start(bf16[16,64,128]{2,1,0:T(8,128)(2,1)} %attend.1), calls=%async_computation.1 | async-start | bytes 524288 | tf_op jit(solution)/shard_map/all_to_all | solution.py:318
  36.1 0.1 pad_add_fusion.where_ref
  36.2 0.0 collective-permute-done.1.chip_ref
  36.2 0.0 collective-permute-done.core_ref
  36.2 0.0 copy-done
  36.2 0.0 copy-done.1
  36.2 0.0 copy-done.2
  36.2 6.2 %video.1 = bf16[512,16,128]{2,1,0:T(8,128)(2,1)} custom-call(s32[4,4]{1,0:T(4,128)S(1)} %copy-done.1, s32[4]{0:T(128)S(1)} %copy-done.2, s32[3]{0:T(128)S(1)} %pad_add_fusion.where_ref, bf16[512,16,128]{2,1,0:T(8,128)(2,1)S(1)} %copy-done, bf16[16,128,128]{2,1,0:T(8,128)(2,1)S(1)} %get-tuple-element.7.own_ref, ...), custom_call_target="tpu_custom_call" | custom-call | flops 536870912 | bytes 33554432 | tf_op jit(solution)/shard_map/video/pallas_call | solution.py:280
  42.4 0.9 %all-to-all-done.1.by_head_ref = bf16[16,64,128]{2,1,0:T(8,128)(2,1)S(1)} async-done(((bf16[16,64,128]{2,1,0:T(8,128)(2,1)}), bf16[16,64,128]{2,1,0:T(8,128)(2,1)S(1)}, u32[]{:S(2)}, u32[]{:S(2)}) %all-to-all-start.1) | async-done | bytes 262176 | tf_op jit(solution)/shard_map/all_to_all | solution.py:318
  43.3 0.8 %collect.1 = bf16[64,16,128]{2,1,0:T(8,128)(2,1)} custom-call(bf16[16,64,128]{2,1,0:T(8,128)(2,1)S(1)} %all-to-all-done.1.by_head_ref), custom_call_target="tpu_custom_call" | custom-call | tf_op jit(solution)/shard_map/collect/pallas_call | solution.py:199
Async XLA Ops:
  2.7 33.6 %copy-start = (bf16[512,16,128]{2,1,0:T(8,128)(2,1)S(1)}, bf16[512,16,128]{2,1,0:T(8,128)(2,1)}, u32[]{:S(2)}) copy-start(bf16[512,16,128]{2,1,0:T(8,128)(2,1)} %video_ref.1) | copy-start | bytes 6291460
  2.7 33.5 %copy-start.1 = (s32[4,4]{1,0:T(4,128)S(1)}, s32[4,4]{1,0:T(4,128)}, u32[]{:S(2)}) copy-start(s32[4,4]{1,0:T(4,128)} %pairs_ref.1) | copy-start | bytes 196
  2.7 33.5 %copy-start.2 = (s32[4]{0:T(128)S(1)}, s32[4]{0:T(128)}, u32[]{:S(2)}) copy-start(s32[4]{0:T(128)} %counts_ref.1) | copy-start | bytes 52
  2.7 26.7 %all-to-all-start = ((bf16[16,4,48,128]{3,2,1,0:T(8,128)(2,1)}), bf16[16,4,48,128]{3,2,1,0:T(8,128)(2,1)S(1)}, u32[]{:S(2)}, u32[]{:S(2)}) async-start(bf16[16,4,48,128]{3,2,1,0:T(8,128)(2,1)} %get-tuple-element.6), calls=%async_computation | async-start | bytes 1572864 | tf_op jit(solution)/shard_map/all_to_all | solution.py:318
  10.5 25.8 %collective-permute-start.1 = (bf16[16,128,128]{2,1,0:T(8,128)(2,1)S(1)}, bf16[16,128,128]{2,1,0:T(8,128)(2,1)}, u32[]{:S(2)}, u32[]{:S(2)}) collective-permute-start(bf16[16,128,128]{2,1,0:T(8,128)(2,1)S(1)} %get-tuple-element.7.own_ref), channel_id=1, source_target_pairs={{1,2},{2,1},{3,4},{4,3},{5,6},{6,5},{7,8},{8,7},{9,10},{10,9},{11,... | collective-permute-start | bytes 1572872 | tf_op jit(solution)/shard_map/ppermute | solution.py:313
  11.9 24.3 %collective-permute-start = (bf16[16,128,128]{2,1,0:T(8,128)(2,1)S(1)}, bf16[16,128,128]{2,1,0:T(8,128)(2,1)}, u32[]{:S(2)}, u32[]{:S(2)}) collective-permute-start(bf16[16,128,128]{2,1,0:T(8,128)(2,1)S(1)} %get-tuple-element.7.own_ref), channel_id=1, source_target_pairs={{0,1},{1,0},{2,3},{3,2},{4,5},{5,4},{6,7},{7,6},{8,9},{9,8},{10,11... | collective-permute-start | bytes 1572872 | tf_op jit(solution)/shard_map/ppermute | solution.py:322
  31.8 11.5 %all-to-all-start.1 = ((bf16[16,64,128]{2,1,0:T(8,128)(2,1)}), bf16[16,64,128]{2,1,0:T(8,128)(2,1)S(1)}, u32[]{:S(2)}, u32[]{:S(2)}) async-start(bf16[16,64,128]{2,1,0:T(8,128)(2,1)} %attend.1), calls=%async_computation.1 | async-start | bytes 524288 | tf_op jit(solution)/shard_map/all_to_all | solution.py:318

commit v21 on v17

--- a/solution.py
+++ b/solution.py
@@ -312,7 +312,7 @@
 
     chip = lax.ppermute(kv, "seq", chip_pairs)
 
-    order = [(devices // 2 + p) % devices for p in range(devices)]
+    order = [(devices // 4 + 1 - p) % devices for p in range(devices)]
 
     def exchange(value):
         return lax.all_to_all(

time: 46.8 us -> 45.4 us (0.970)
  starting transfers between devices: 20 us -> 14.7 us
  waiting for transfers between devices: 14.4 us -> 18.1 us
    all_to_all x2, starting transfers between devices: 16.4 us -> 11.2 us  [exchange(): lax.all_to_all(value, 'seq', split_axis=0, concat_axis=0, tiled=True, axi...]
    all_to_all x2, waiting for transfers between devices: 14.4 us -> 18.1 us  [exchange(): lax.all_to_all(value, 'seq', split_axis=0, concat_axis=0, tiled=True, axi...]
  transfers between devices with their start and end apart: 4 -> 4, of which waited for: 2 -> 2; matrix products, arithmetic and copies ran while one was open for 0% -> 0% of each run, Pallas kernels for 18% -> 19%
where the time goes in v21:
time: 45.4 us; the launch traced here: 44.9 us
  waiting for transfers between devices  18.1 us (40%)
  starting transfers between devices  14.7 us (32%)
  Pallas kernels  11.3 us (25%)
  between operations  0.72 us (2%)
    all_to_all x2, waiting for transfers between devices, exchange(): lax.all_to_all(value, 'seq', split_axis=0, concat_axis=0, tiled=True, axi...  18.1 us
    all_to_all x2, starting transfers between devices, exchange(): lax.all_to_all(value, 'seq', split_axis=0, concat_axis=0, tiled=True, axi...  11.2 us
    pallas_call x1, Pallas kernels, video(): pl.pallas_call(functools.partial(video_kernel, scale, 4), in_specs=[in_sm...  6.18 us
    pallas_call x1, Pallas kernels, attend(): pl.pallas_call(functools.partial(attend_kernel, scale), in_specs=[pl.Bloc...  2.28 us
    ppermute x1, starting transfers between devices, local(): core = lax.ppermute(kv, 'seq', core_pairs)  2.11 us
    pallas_call x1, Pallas kernels, arrange(): pl.pallas_call(functools.partial(arrange_kernel, pieces), in_specs=[pl.Bl...  2.03 us
    ppermute x1, starting transfers between devices, local(): chip = lax.ppermute(kv, 'seq', chip_pairs)  1.44 us
  transfers between devices with their start and end apart: 4, of which 2 were waited for; matrix products, arithmetic and copies ran while one was open for 0% of the time, Pallas kernels for 19%

profile of v21, /device:TPU:0, one launch (start us, length us, event | category | flops | bytes accessed | tf_op | source)
XLA Modules:
  0.0 44.9 jit_solution(1667526255940212096)
XLA Ops:
  0.6 2.0 %arrange.1 = (bf16[16,4,48,128]{3,2,1,0:T(8,128)(2,1)}, bf16[16,128,128]{2,1,0:T(8,128)(2,1)S(1)}) custom-call(bf16[64,3,16,128]{3,2,1,0:T(8,128)(2,1)} %qkv_ref.1), custom_call_target="tpu_custom_call" | custom-call | tf_op jit(solution)/shard_map/arrange/pallas_call | solution.py:56
  2.7 0.0 copy-start
  2.7 0.0 copy-start.1
  2.7 0.0 copy-start.2
  2.7 7.8 %all-to-all-start = ((bf16[16,4,48,128]{3,2,1,0:T(8,128)(2,1)}), bf16[16,4,48,128]{3,2,1,0:T(8,128)(2,1)S(1)}, u32[]{:S(2)}, u32[]{:S(2)}) async-start(bf16[16,4,48,128]{3,2,1,0:T(8,128)(2,1)} %get-tuple-element.6), calls=%async_computation | async-start | bytes 1572864 | tf_op jit(solution)/shard_map/all_to_all | solution.py:318
  10.5 1.4 %collective-permute-start.1 = (bf16[16,128,128]{2,1,0:T(8,128)(2,1)S(1)}, bf16[16,128,128]{2,1,0:T(8,128)(2,1)}, u32[]{:S(2)}, u32[]{:S(2)}) collective-permute-start(bf16[16,128,128]{2,1,0:T(8,128)(2,1)S(1)} %get-tuple-element.7.own_ref), channel_id=1, source_target_pairs={{1,2},{2,1},{3,4},{4,3},{5,6},{6,5},{7,8},{8,7},{9,10},{10,9},{11,... | collective-permute-start | bytes 1572872 | tf_op jit(solution)/shard_map/ppermute | solution.py:313
  11.9 2.1 %collective-permute-start = (bf16[16,128,128]{2,1,0:T(8,128)(2,1)S(1)}, bf16[16,128,128]{2,1,0:T(8,128)(2,1)}, u32[]{:S(2)}, u32[]{:S(2)}) collective-permute-start(bf16[16,128,128]{2,1,0:T(8,128)(2,1)S(1)} %get-tuple-element.7.own_ref), channel_id=1, source_target_pairs={{0,1},{1,0},{2,3},{3,2},{4,5},{5,4},{6,7},{7,6},{8,9},{9,8},{10,11... | collective-permute-start | bytes 1572872 | tf_op jit(solution)/shard_map/ppermute | solution.py:322
  14.0 16.2 %all-to-all-done.recv_ref = bf16[16,4,48,128]{3,2,1,0:T(8,128)(2,1)S(1)} async-done(((bf16[16,4,48,128]{3,2,1,0:T(8,128)(2,1)}), bf16[16,4,48,128]{3,2,1,0:T(8,128)(2,1)S(1)}, u32[]{:S(2)}, u32[]{:S(2)}) %all-to-all-start) | async-done | bytes 786464 | tf_op jit(solution)/shard_map/all_to_all | solution.py:318
  30.3 2.3 %attend.1 = bf16[16,64,128]{2,1,0:T(8,128)(2,1)} custom-call(bf16[16,4,48,128]{3,2,1,0:T(8,128)(2,1)S(1)} %all-to-all-done.recv_ref), custom_call_target="tpu_custom_call" | custom-call | flops 536870912 | bytes 1048576 | tf_op jit(solution)/shard_map/attend/pallas_call | solution.py:125
  32.5 3.4 %all-to-all-start.1 = ((bf16[16,64,128]{2,1,0:T(8,128)(2,1)}), bf16[16,64,128]{2,1,0:T(8,128)(2,1)S(1)}, u32[]{:S(2)}, u32[]{:S(2)}) async-start(bf16[16,64,128]{2,1,0:T(8,128)(2,1)} %attend.1), calls=%async_computation.1 | async-start | bytes 524288 | tf_op jit(solution)/shard_map/all_to_all | solution.py:318
  36.0 0.1 pad_add_fusion.where_ref
  36.1 0.0 collective-permute-done.1.chip_ref
  36.1 0.0 collective-permute-done.core_ref
  36.1 0.0 copy-done
  36.1 0.0 copy-done.1
  36.1 0.0 copy-done.2
  36.1 6.2 %video.1 = bf16[512,16,128]{2,1,0:T(8,128)(2,1)} custom-call(s32[4,4]{1,0:T(4,128)S(1)} %copy-done.1, s32[4]{0:T(128)S(1)} %copy-done.2, s32[3]{0:T(128)S(1)} %pad_add_fusion.where_ref, bf16[512,16,128]{2,1,0:T(8,128)(2,1)S(1)} %copy-done, bf16[16,128,128]{2,1,0:T(8,128)(2,1)S(1)} %get-tuple-element.7.own_ref, ...), custom_call_target="tpu_custom_call" | custom-call | flops 536870912 | bytes 33554432 | tf_op jit(solution)/shard_map/video/pallas_call | solution.py:280
  42.3 1.8 %all-to-all-done.1.by_head_ref = bf16[16,64,128]{2,1,0:T(8,128)(2,1)S(1)} async-done(((bf16[16,64,128]{2,1,0:T(8,128)(2,1)}), bf16[16,64,128]{2,1,0:T(8,128)(2,1)S(1)}, u32[]{:S(2)}, u32[]{:S(2)}) %all-to-all-start.1) | async-done | bytes 262176 | tf_op jit(solution)/shard_map/all_to_all | solution.py:318
  44.1 0.8 %collect.1 = bf16[64,16,128]{2,1,0:T(8,128)(2,1)} custom-call(bf16[16,64,128]{2,1,0:T(8,128)(2,1)S(1)} %all-to-all-done.1.by_head_ref), custom_call_target="tpu_custom_call" | custom-call | tf_op jit(solution)/shard_map/collect/pallas_call | solution.py:199
Async XLA Ops:
  2.7 33.4 %copy-start = (bf16[512,16,128]{2,1,0:T(8,128)(2,1)S(1)}, bf16[512,16,128]{2,1,0:T(8,128)(2,1)}, u32[]{:S(2)}) copy-start(bf16[512,16,128]{2,1,0:T(8,128)(2,1)} %video_ref.1) | copy-start | bytes 6291460
  2.7 33.4 %copy-start.1 = (s32[4,4]{1,0:T(4,128)S(1)}, s32[4,4]{1,0:T(4,128)}, u32[]{:S(2)}) copy-start(s32[4,4]{1,0:T(4,128)} %pairs_ref.1) | copy-start | bytes 196
  2.7 33.4 %copy-start.2 = (s32[4]{0:T(128)S(1)}, s32[4]{0:T(128)}, u32[]{:S(2)}) copy-start(s32[4]{0:T(128)} %counts_ref.1) | copy-start | bytes 52
  2.7 27.6 %all-to-all-start = ((bf16[16,4,48,128]{3,2,1,0:T(8,128)(2,1)}), bf16[16,4,48,128]{3,2,1,0:T(8,128)(2,1)S(1)}, u32[]{:S(2)}, u32[]{:S(2)}) async-start(bf16[16,4,48,128]{3,2,1,0:T(8,128)(2,1)} %get-tuple-element.6), calls=%async_computation | async-start | bytes 1572864 | tf_op jit(solution)/shard_map/all_to_all | solution.py:318
  10.5 25.6 %collective-permute-start.1 = (bf16[16,128,128]{2,1,0:T(8,128)(2,1)S(1)}, bf16[16,128,128]{2,1,0:T(8,128)(2,1)}, u32[]{:S(2)}, u32[]{:S(2)}) collective-permute-start(bf16[16,128,128]{2,1,0:T(8,128)(2,1)S(1)} %get-tuple-element.7.own_ref), channel_id=1, source_target_pairs={{1,2},{2,1},{3,4},{4,3},{5,6},{6,5},{7,8},{8,7},{9,10},{10,9},{11,... | collective-permute-start | bytes 1572872 | tf_op jit(solution)/shard_map/ppermute | solution.py:313
  11.9 24.2 %collective-permute-start = (bf16[16,128,128]{2,1,0:T(8,128)(2,1)S(1)}, bf16[16,128,128]{2,1,0:T(8,128)(2,1)}, u32[]{:S(2)}, u32[]{:S(2)}) collective-permute-start(bf16[16,128,128]{2,1,0:T(8,128)(2,1)S(1)} %get-tuple-element.7.own_ref), channel_id=1, source_target_pairs={{0,1},{1,0},{2,3},{3,2},{4,5},{5,4},{6,7},{7,6},{8,9},{9,8},{10,11... | collective-permute-start | bytes 1572872 | tf_op jit(solution)/shard_map/ppermute | solution.py:322
  32.5 11.6 %all-to-all-start.1 = ((bf16[16,64,128]{2,1,0:T(8,128)(2,1)}), bf16[16,64,128]{2,1,0:T(8,128)(2,1)S(1)}, u32[]{:S(2)}, u32[]{:S(2)}) async-start(bf16[16,64,128]{2,1,0:T(8,128)(2,1)} %attend.1), calls=%async_computation.1 | async-start | bytes 524288 | tf_op jit(solution)/shard_map/all_to_all | solution.py:318

commit v22 on v21

--- a/solution.py
+++ b/solution.py
@@ -312,7 +312,7 @@
 
     chip = lax.ppermute(kv, "seq", chip_pairs)
 
-    order = [(devices // 4 + 1 - p) % devices for p in range(devices)]
+    order = [(devices // 2 + 1 - p) % devices for p in range(devices)]
 
     def exchange(value):
         return lax.all_to_all(

time: 45.4 us -> 46.3 us (1.020)
  starting transfers between devices: 14.7 us -> 17.2 us
  waiting for transfers between devices: 18.1 us -> 16.2 us
    all_to_all x2, starting transfers between devices: 11.2 us -> 13.6 us  [exchange(): lax.all_to_all(value, 'seq', split_axis=0, concat_axis=0, tiled=True, axi...]
    all_to_all x2, waiting for transfers between devices: 18.1 us -> 16.2 us  [exchange(): lax.all_to_all(value, 'seq', split_axis=0, concat_axis=0, tiled=True, axi...]
where the time goes in v22:
time: 46.3 us; the launch traced here: 45.5 us
  starting transfers between devices  17.2 us (37%)
  waiting for transfers between devices  16.2 us (35%)
  Pallas kernels  11.2 us (24%)
  between operations  0.7 us (2%)
    all_to_all x2, waiting for transfers between devices, exchange(): lax.all_to_all(value, 'seq', split_axis=0, concat_axis=0, tiled=True, axi...  16.2 us
    all_to_all x2, starting transfers between devices, exchange(): lax.all_to_all(value, 'seq', split_axis=0, concat_axis=0, tiled=True, axi...  13.6 us
    pallas_call x1, Pallas kernels, video(): pl.pallas_call(functools.partial(video_kernel, scale, 4), in_specs=[in_sm...  6.17 us
    pallas_call x1, Pallas kernels, attend(): pl.pallas_call(functools.partial(attend_kernel, scale), in_specs=[pl.Bloc...  2.28 us
    ppermute x1, starting transfers between devices, local(): core = lax.ppermute(kv, 'seq', core_pairs)  2.11 us
    pallas_call x1, Pallas kernels, arrange(): pl.pallas_call(functools.partial(arrange_kernel, pieces), in_specs=[pl.Bl...  2.03 us
    ppermute x1, starting transfers between devices, local(): chip = lax.ppermute(kv, 'seq', chip_pairs)  1.44 us
  transfers between devices with their start and end apart: 4, of which 2 were waited for; matrix products, arithmetic and copies ran while one was open for 0% of the time, Pallas kernels for 19%

profile of v22, /device:TPU:0, one launch (start us, length us, event | category | flops | bytes accessed | tf_op | source)
XLA Modules:
  0.0 45.5 jit_solution(6896295234751885217)
XLA Ops:
  0.6 2.0 %arrange.1 = (bf16[16,4,48,128]{3,2,1,0:T(8,128)(2,1)}, bf16[16,128,128]{2,1,0:T(8,128)(2,1)S(1)}) custom-call(bf16[64,3,16,128]{3,2,1,0:T(8,128)(2,1)} %qkv_ref.1), custom_call_target="tpu_custom_call" | custom-call | tf_op jit(solution)/shard_map/arrange/pallas_call | solution.py:56
  2.7 0.0 copy-start
  2.7 0.0 copy-start.1
  2.7 0.0 copy-start.2
  2.7 7.8 %all-to-all-start = ((bf16[16,4,48,128]{3,2,1,0:T(8,128)(2,1)}), bf16[16,4,48,128]{3,2,1,0:T(8,128)(2,1)S(1)}, u32[]{:S(2)}, u32[]{:S(2)}) async-start(bf16[16,4,48,128]{3,2,1,0:T(8,128)(2,1)} %get-tuple-element.6), calls=%async_computation | async-start | bytes 1572864 | tf_op jit(solution)/shard_map/all_to_all | solution.py:318
  10.5 1.4 %collective-permute-start.1 = (bf16[16,128,128]{2,1,0:T(8,128)(2,1)S(1)}, bf16[16,128,128]{2,1,0:T(8,128)(2,1)}, u32[]{:S(2)}, u32[]{:S(2)}) collective-permute-start(bf16[16,128,128]{2,1,0:T(8,128)(2,1)S(1)} %get-tuple-element.7.own_ref), channel_id=1, source_target_pairs={{1,2},{2,1},{3,4},{4,3},{5,6},{6,5},{7,8},{8,7},{9,10},{10,9},{11,... | collective-permute-start | bytes 1572872 | tf_op jit(solution)/shard_map/ppermute | solution.py:313
  11.9 2.1 %collective-permute-start = (bf16[16,128,128]{2,1,0:T(8,128)(2,1)S(1)}, bf16[16,128,128]{2,1,0:T(8,128)(2,1)}, u32[]{:S(2)}, u32[]{:S(2)}) collective-permute-start(bf16[16,128,128]{2,1,0:T(8,128)(2,1)S(1)} %get-tuple-element.7.own_ref), channel_id=1, source_target_pairs={{0,1},{1,0},{2,3},{3,2},{4,5},{5,4},{6,7},{7,6},{8,9},{9,8},{10,11... | collective-permute-start | bytes 1572872 | tf_op jit(solution)/shard_map/ppermute | solution.py:322
  14.0 15.3 %all-to-all-done.recv_ref = bf16[16,4,48,128]{3,2,1,0:T(8,128)(2,1)S(1)} async-done(((bf16[16,4,48,128]{3,2,1,0:T(8,128)(2,1)}), bf16[16,4,48,128]{3,2,1,0:T(8,128)(2,1)S(1)}, u32[]{:S(2)}, u32[]{:S(2)}) %all-to-all-start) | async-done | bytes 786464 | tf_op jit(solution)/shard_map/all_to_all | solution.py:318
  29.4 2.3 %attend.1 = bf16[16,64,128]{2,1,0:T(8,128)(2,1)} custom-call(bf16[16,4,48,128]{3,2,1,0:T(8,128)(2,1)S(1)} %all-to-all-done.recv_ref), custom_call_target="tpu_custom_call" | custom-call | flops 536870912 | bytes 1048576 | tf_op jit(solution)/shard_map/attend/pallas_call | solution.py:125
  31.6 5.9 %all-to-all-start.1 = ((bf16[16,64,128]{2,1,0:T(8,128)(2,1)}), bf16[16,64,128]{2,1,0:T(8,128)(2,1)S(1)}, u32[]{:S(2)}, u32[]{:S(2)}) async-start(bf16[16,64,128]{2,1,0:T(8,128)(2,1)} %attend.1), calls=%async_computation.1 | async-start | bytes 524288 | tf_op jit(solution)/shard_map/all_to_all | solution.py:318
  37.5 0.1 pad_add_fusion.where_ref
  37.6 0.0 collective-permute-done.1.chip_ref
  37.6 0.0 collective-permute-done.core_ref
  37.6 0.0 copy-done
  37.6 0.0 copy-done.1
  37.6 0.0 copy-done.2
  37.6 6.2 %video.1 = bf16[512,16,128]{2,1,0:T(8,128)(2,1)} custom-call(s32[4,4]{1,0:T(4,128)S(1)} %copy-done.1, s32[4]{0:T(128)S(1)} %copy-done.2, s32[3]{0:T(128)S(1)} %pad_add_fusion.where_ref, bf16[512,16,128]{2,1,0:T(8,128)(2,1)S(1)} %copy-done, bf16[16,128,128]{2,1,0:T(8,128)(2,1)S(1)} %get-tuple-element.7.own_ref, ...), custom_call_target="tpu_custom_call" | custom-call | flops 536870912 | bytes 33554432 | tf_op jit(solution)/shard_map/video/pallas_call | solution.py:280
  43.8 0.9 %all-to-all-done.1.by_head_ref = bf16[16,64,128]{2,1,0:T(8,128)(2,1)S(1)} async-done(((bf16[16,64,128]{2,1,0:T(8,128)(2,1)}), bf16[16,64,128]{2,1,0:T(8,128)(2,1)S(1)}, u32[]{:S(2)}, u32[]{:S(2)}) %all-to-all-start.1) | async-done | bytes 262176 | tf_op jit(solution)/shard_map/all_to_all | solution.py:318
  44.7 0.8 %collect.1 = bf16[64,16,128]{2,1,0:T(8,128)(2,1)} custom-call(bf16[16,64,128]{2,1,0:T(8,128)(2,1)S(1)} %all-to-all-done.1.by_head_ref), custom_call_target="tpu_custom_call" | custom-call | tf_op jit(solution)/shard_map/collect/pallas_call | solution.py:199
Async XLA Ops:
  2.7 35.0 %copy-start = (bf16[512,16,128]{2,1,0:T(8,128)(2,1)S(1)}, bf16[512,16,128]{2,1,0:T(8,128)(2,1)}, u32[]{:S(2)}) copy-start(bf16[512,16,128]{2,1,0:T(8,128)(2,1)} %video_ref.1) | copy-start | bytes 6291460
  2.7 35.0 %copy-start.1 = (s32[4,4]{1,0:T(4,128)S(1)}, s32[4,4]{1,0:T(4,128)}, u32[]{:S(2)}) copy-start(s32[4,4]{1,0:T(4,128)} %pairs_ref.1) | copy-start | bytes 196
  2.7 34.9 %copy-start.2 = (s32[4]{0:T(128)S(1)}, s32[4]{0:T(128)}, u32[]{:S(2)}) copy-start(s32[4]{0:T(128)} %counts_ref.1) | copy-start | bytes 52
  2.7 26.7 %all-to-all-start = ((bf16[16,4,48,128]{3,2,1,0:T(8,128)(2,1)}), bf16[16,4,48,128]{3,2,1,0:T(8,128)(2,1)S(1)}, u32[]{:S(2)}, u32[]{:S(2)}) async-start(bf16[16,4,48,128]{3,2,1,0:T(8,128)(2,1)} %get-tuple-element.6), calls=%async_computation | async-start | bytes 1572864 | tf_op jit(solution)/shard_map/all_to_all | solution.py:318
  10.5 27.2 %collective-permute-start.1 = (bf16[16,128,128]{2,1,0:T(8,128)(2,1)S(1)}, bf16[16,128,128]{2,1,0:T(8,128)(2,1)}, u32[]{:S(2)}, u32[]{:S(2)}) collective-permute-start(bf16[16,128,128]{2,1,0:T(8,128)(2,1)S(1)} %get-tuple-element.7.own_ref), channel_id=1, source_target_pairs={{1,2},{2,1},{3,4},{4,3},{5,6},{6,5},{7,8},{8,7},{9,10},{10,9},{11,... | collective-permute-start | bytes 1572872 | tf_op jit(solution)/shard_map/ppermute | solution.py:313
  11.9 25.7 %collective-permute-start = (bf16[16,128,128]{2,1,0:T(8,128)(2,1)S(1)}, bf16[16,128,128]{2,1,0:T(8,128)(2,1)}, u32[]{:S(2)}, u32[]{:S(2)}) collective-permute-start(bf16[16,128,128]{2,1,0:T(8,128)(2,1)S(1)} %get-tuple-element.7.own_ref), channel_id=1, source_target_pairs={{0,1},{1,0},{2,3},{3,2},{4,5},{5,4},{6,7},{7,6},{8,9},{9,8},{10,11... | collective-permute-start | bytes 1572872 | tf_op jit(solution)/shard_map/ppermute | solution.py:322
  31.6 13.1 %all-to-all-start.1 = ((bf16[16,64,128]{2,1,0:T(8,128)(2,1)}), bf16[16,64,128]{2,1,0:T(8,128)(2,1)S(1)}, u32[]{:S(2)}, u32[]{:S(2)}) async-start(bf16[16,64,128]{2,1,0:T(8,128)(2,1)} %attend.1), calls=%async_computation.1 | async-start | bytes 524288 | tf_op jit(solution)/shard_map/all_to_all | solution.py:318

commit v23 on v16

--- a/solution.py
+++ b/solution.py
@@ -37,14 +37,16 @@
         for part in range(3):
             by_head = jnp.swapaxes(came[piece, :, part], 0, 1)
             turned[piece, :, part * PIECE : (part + 1) * PIECE] = by_head
-            if part:
-                at = (part - 1) * rows + piece * PIECE
-                kv_ref[:, at : at + PIECE] = by_head
         departure = pltpu.make_async_copy(
             turned.at[piece], send_ref.at[:, piece], out_sems.at[piece]
         )
         departure.start()
         departures.append(departure)
+    for piece in range(pieces):
+        for half in range(2):
+            at = half * rows + piece * PIECE
+            part = (half + 1) * PIECE
+            kv_ref[:, at : at + PIECE] = turned[piece, :, part : part + PIECE]
     for departure in departures:
         departure.wait()
 

time: 44.7 us -> 44.8 us (level)
  no operation moved by 1% of the time
where the time goes in v23:
time: 44.8 us; the launch traced here: 43.9 us
  waiting for transfers between devices  17.1 us (38%)
  starting transfers between devices  14.7 us (33%)
  Pallas kernels  11.3 us (25%)
  between operations  0.7 us (2%)
    all_to_all x2, waiting for transfers between devices, exchange(): lax.all_to_all(value, 'seq', split_axis=0, concat_axis=0, tiled=True, axi...  17.1 us
    all_to_all x2, starting transfers between devices, exchange(): lax.all_to_all(value, 'seq', split_axis=0, concat_axis=0, tiled=True, axi...  12.1 us
    pallas_call x1, Pallas kernels, video(): pl.pallas_call(functools.partial(video_kernel, scale, 4), in_specs=[in_sm...  6.17 us
    pallas_call x1, Pallas kernels, attend(): pl.pallas_call(functools.partial(attend_kernel, scale), in_specs=[pl.Bloc...  2.28 us
    pallas_call x1, Pallas kernels, arrange(): pl.pallas_call(functools.partial(arrange_kernel, pieces), in_specs=[pl.Bl...  2.07 us
    ppermute x1, starting transfers between devices, local(): chip = lax.ppermute(kv, 'seq', chip_pairs)  1.44 us
    ppermute x1, starting transfers between devices, local(): core = lax.ppermute(kv, 'seq', core_pairs)  1.21 us
  transfers between devices with their start and end apart: 4, of which 2 were waited for; matrix products, arithmetic and copies ran while one was open for 0% of the time, Pallas kernels for 19%

profile of v23, /device:TPU:0, one launch (start us, length us, event | category | flops | bytes accessed | tf_op | source)
XLA Modules:
  0.0 43.9 jit_solution(12110215668973306960)
XLA Ops:
  0.6 2.1 %arrange.1 = (bf16[16,4,48,128]{3,2,1,0:T(8,128)(2,1)}, bf16[16,128,128]{2,1,0:T(8,128)(2,1)S(1)}) custom-call(bf16[64,3,16,128]{3,2,1,0:T(8,128)(2,1)} %qkv_ref.1), custom_call_target="tpu_custom_call" | custom-call | tf_op jit(solution)/shard_map/arrange/pallas_call | solution.py:58
  2.7 0.0 copy-start
  2.7 0.0 copy-start.1
  2.7 0.0 copy-start.2
  2.7 7.8 %all-to-all-start = ((bf16[16,4,48,128]{3,2,1,0:T(8,128)(2,1)}), bf16[16,4,48,128]{3,2,1,0:T(8,128)(2,1)S(1)}, u32[]{:S(2)}, u32[]{:S(2)}) async-start(bf16[16,4,48,128]{3,2,1,0:T(8,128)(2,1)} %get-tuple-element.6), calls=%async_computation | async-start | bytes 1572864 | tf_op jit(solution)/shard_map/all_to_all | solution.py:320
  10.5 1.4 %collective-permute-start.1 = (bf16[16,128,128]{2,1,0:T(8,128)(2,1)S(1)}, bf16[16,128,128]{2,1,0:T(8,128)(2,1)}, u32[]{:S(2)}, u32[]{:S(2)}) collective-permute-start(bf16[16,128,128]{2,1,0:T(8,128)(2,1)S(1)} %get-tuple-element.7.own_ref), channel_id=1, source_target_pairs={{1,2},{2,1},{3,4},{4,3},{5,6},{6,5},{7,8},{8,7},{9,10},{10,9},{11,... | collective-permute-start | bytes 1572872 | tf_op jit(solution)/shard_map/ppermute | solution.py:315
  11.9 1.2 %collective-permute-start = (bf16[16,128,128]{2,1,0:T(8,128)(2,1)S(1)}, bf16[16,128,128]{2,1,0:T(8,128)(2,1)}, u32[]{:S(2)}, u32[]{:S(2)}) collective-permute-start(bf16[16,128,128]{2,1,0:T(8,128)(2,1)S(1)} %get-tuple-element.7.own_ref), channel_id=1, source_target_pairs={{0,1},{1,0},{2,3},{3,2},{4,5},{5,4},{6,7},{7,6},{8,9},{9,8},{10,11... | collective-permute-start | bytes 1572872 | tf_op jit(solution)/shard_map/ppermute | solution.py:324
  13.1 16.2 %all-to-all-done.recv_ref = bf16[16,4,48,128]{3,2,1,0:T(8,128)(2,1)S(1)} async-done(((bf16[16,4,48,128]{3,2,1,0:T(8,128)(2,1)}), bf16[16,4,48,128]{3,2,1,0:T(8,128)(2,1)S(1)}, u32[]{:S(2)}, u32[]{:S(2)}) %all-to-all-start) | async-done | bytes 786464 | tf_op jit(solution)/shard_map/all_to_all | solution.py:320
  29.4 2.3 %attend.1 = bf16[16,64,128]{2,1,0:T(8,128)(2,1)} custom-call(bf16[16,4,48,128]{3,2,1,0:T(8,128)(2,1)S(1)} %all-to-all-done.recv_ref), custom_call_target="tpu_custom_call" | custom-call | flops 536870912 | bytes 1048576 | tf_op jit(solution)/shard_map/attend/pallas_call | solution.py:127
  31.7 4.3 %all-to-all-start.1 = ((bf16[16,64,128]{2,1,0:T(8,128)(2,1)}), bf16[16,64,128]{2,1,0:T(8,128)(2,1)S(1)}, u32[]{:S(2)}, u32[]{:S(2)}) async-start(bf16[16,64,128]{2,1,0:T(8,128)(2,1)} %attend.1), calls=%async_computation.1 | async-start | bytes 524288 | tf_op jit(solution)/shard_map/all_to_all | solution.py:320
  36.0 0.1 pad_add_fusion.where_ref
  36.1 0.0 collective-permute-done.1.chip_ref
  36.1 0.0 collective-permute-done.core_ref
  36.1 0.0 copy-done
  36.1 0.0 copy-done.1
  36.1 0.0 copy-done.2
  36.1 6.2 %video.1 = bf16[512,16,128]{2,1,0:T(8,128)(2,1)} custom-call(s32[4,4]{1,0:T(4,128)S(1)} %copy-done.1, s32[4]{0:T(128)S(1)} %copy-done.2, s32[3]{0:T(128)S(1)} %pad_add_fusion.where_ref, bf16[512,16,128]{2,1,0:T(8,128)(2,1)S(1)} %copy-done, bf16[16,128,128]{2,1,0:T(8,128)(2,1)S(1)} %get-tuple-element.7.own_ref, ...), custom_call_target="tpu_custom_call" | custom-call | flops 536870912 | bytes 33554432 | tf_op jit(solution)/shard_map/video/pallas_call | solution.py:282
  42.3 0.9 %all-to-all-done.1.by_head_ref = bf16[16,64,128]{2,1,0:T(8,128)(2,1)S(1)} async-done(((bf16[16,64,128]{2,1,0:T(8,128)(2,1)}), bf16[16,64,128]{2,1,0:T(8,128)(2,1)S(1)}, u32[]{:S(2)}, u32[]{:S(2)}) %all-to-all-start.1) | async-done | bytes 262176 | tf_op jit(solution)/shard_map/all_to_all | solution.py:320
  43.2 0.8 %collect.1 = bf16[64,16,128]{2,1,0:T(8,128)(2,1)} custom-call(bf16[16,64,128]{2,1,0:T(8,128)(2,1)S(1)} %all-to-all-done.1.by_head_ref), custom_call_target="tpu_custom_call" | custom-call | tf_op jit(solution)/shard_map/collect/pallas_call | solution.py:201
Async XLA Ops:
  2.7 33.4 %copy-start = (bf16[512,16,128]{2,1,0:T(8,128)(2,1)S(1)}, bf16[512,16,128]{2,1,0:T(8,128)(2,1)}, u32[]{:S(2)}) copy-start(bf16[512,16,128]{2,1,0:T(8,128)(2,1)} %video_ref.1) | copy-start | bytes 6291460
  2.7 33.4 %copy-start.1 = (s32[4,4]{1,0:T(4,128)S(1)}, s32[4,4]{1,0:T(4,128)}, u32[]{:S(2)}) copy-start(s32[4,4]{1,0:T(4,128)} %pairs_ref.1) | copy-start | bytes 196
  2.7 33.4 %copy-start.2 = (s32[4]{0:T(128)S(1)}, s32[4]{0:T(128)}, u32[]{:S(2)}) copy-start(s32[4]{0:T(128)} %counts_ref.1) | copy-start | bytes 52
  2.7 26.7 %all-to-all-start = ((bf16[16,4,48,128]{3,2,1,0:T(8,128)(2,1)}), bf16[16,4,48,128]{3,2,1,0:T(8,128)(2,1)S(1)}, u32[]{:S(2)}, u32[]{:S(2)}) async-start(bf16[16,4,48,128]{3,2,1,0:T(8,128)(2,1)} %get-tuple-element.6), calls=%async_computation | async-start | bytes 1572864 | tf_op jit(solution)/shard_map/all_to_all | solution.py:320
  10.5 25.6 %collective-permute-start.1 = (bf16[16,128,128]{2,1,0:T(8,128)(2,1)S(1)}, bf16[16,128,128]{2,1,0:T(8,128)(2,1)}, u32[]{:S(2)}, u32[]{:S(2)}) collective-permute-start(bf16[16,128,128]{2,1,0:T(8,128)(2,1)S(1)} %get-tuple-element.7.own_ref), channel_id=1, source_target_pairs={{1,2},{2,1},{3,4},{4,3},{5,6},{6,5},{7,8},{8,7},{9,10},{10,9},{11,... | collective-permute-start | bytes 1572872 | tf_op jit(solution)/shard_map/ppermute | solution.py:315
  11.9 24.2 %collective-permute-start = (bf16[16,128,128]{2,1,0:T(8,128)(2,1)S(1)}, bf16[16,128,128]{2,1,0:T(8,128)(2,1)}, u32[]{:S(2)}, u32[]{:S(2)}) collective-permute-start(bf16[16,128,128]{2,1,0:T(8,128)(2,1)S(1)} %get-tuple-element.7.own_ref), channel_id=1, source_target_pairs={{0,1},{1,0},{2,3},{3,2},{4,5},{5,4},{6,7},{7,6},{8,9},{9,8},{10,11... | collective-permute-start | bytes 1572872 | tf_op jit(solution)/shard_map/ppermute | solution.py:324
  31.7 11.5 %all-to-all-start.1 = ((bf16[16,64,128]{2,1,0:T(8,128)(2,1)}), bf16[16,64,128]{2,1,0:T(8,128)(2,1)S(1)}, u32[]{:S(2)}, u32[]{:S(2)}) async-start(bf16[16,64,128]{2,1,0:T(8,128)(2,1)} %attend.1), calls=%async_computation.1 | async-start | bytes 524288 | tf_op jit(solution)/shard_map/all_to_all | solution.py:320

commit v24 on v19

--- a/solution.py
+++ b/solution.py
@@ -313,7 +313,8 @@
     chip = lax.ppermute(kv, "seq", chip_pairs)
 
     plane = devices // 4
-    order = [z * plane + plane - 1 - r for r in range(plane) for z in (1, 0, 3, 2)]
+    within = list(range(1, plane, 2))[::-1] + list(range(0, plane, 2))[::-1]
+    order = [z * plane + r for z in (1, 0, 3, 2) for r in within]
 
     def exchange(value):
         return lax.all_to_all(

time: 45.6 us -> 46.4 us (1.018)
  waiting for transfers between devices: 17.6 us -> 18.1 us
    all_to_all x2, waiting for transfers between devices: 17.6 us -> 18.1 us  [exchange(): lax.all_to_all(value, 'seq', split_axis=0, concat_axis=0, tiled=True, axi...]
  transfers between devices with their start and end apart: 4 -> 4, of which waited for: 2 -> 2; matrix products, arithmetic and copies ran while one was open for 0% -> 0% of each run, Pallas kernels for 19% -> 18%
where the time goes in v24:
time: 46.4 us; the launch traced here: 46 us
  waiting for transfers between devices  18.1 us (39%)
  starting transfers between devices  15.8 us (34%)
  Pallas kernels  11.3 us (24%)
  between operations  0.7 us (2%)
    all_to_all x2, waiting for transfers between devices, exchange(): lax.all_to_all(value, 'seq', split_axis=0, concat_axis=0, tiled=True, axi...  18.1 us
    all_to_all x2, starting transfers between devices, exchange(): lax.all_to_all(value, 'seq', split_axis=0, concat_axis=0, tiled=True, axi...  13.2 us
    pallas_call x1, Pallas kernels, video(): pl.pallas_call(functools.partial(video_kernel, scale, 4), in_specs=[in_sm...  6.18 us
    pallas_call x1, Pallas kernels, attend(): pl.pallas_call(functools.partial(attend_kernel, scale), in_specs=[pl.Bloc...  2.28 us
    pallas_call x1, Pallas kernels, arrange(): pl.pallas_call(functools.partial(arrange_kernel, pieces), in_specs=[pl.Bl...  2.03 us
    ppermute x1, starting transfers between devices, local(): chip = lax.ppermute(kv, 'seq', chip_pairs)  1.44 us
    ppermute x1, starting transfers between devices, local(): core = lax.ppermute(kv, 'seq', core_pairs)  1.21 us
  transfers between devices with their start and end apart: 4, of which 2 were waited for; matrix products, arithmetic and copies ran while one was open for 0% of the time, Pallas kernels for 18%

profile of v24, /device:TPU:0, one launch (start us, length us, event | category | flops | bytes accessed | tf_op | source)
XLA Modules:
  0.0 46.0 jit_solution(11385278034226176967)
XLA Ops:
  0.6 2.0 %arrange.1 = (bf16[16,4,48,128]{3,2,1,0:T(8,128)(2,1)}, bf16[16,128,128]{2,1,0:T(8,128)(2,1)S(1)}) custom-call(bf16[64,3,16,128]{3,2,1,0:T(8,128)(2,1)} %qkv_ref.1), custom_call_target="tpu_custom_call" | custom-call | tf_op jit(solution)/shard_map/arrange/pallas_call | solution.py:56
  2.7 0.0 copy-start
  2.7 0.0 copy-start.1
  2.7 0.0 copy-start.2
  2.7 7.8 %all-to-all-start = ((bf16[16,4,48,128]{3,2,1,0:T(8,128)(2,1)}), bf16[16,4,48,128]{3,2,1,0:T(8,128)(2,1)S(1)}, u32[]{:S(2)}, u32[]{:S(2)}) async-start(bf16[16,4,48,128]{3,2,1,0:T(8,128)(2,1)} %get-tuple-element.6), calls=%async_computation | async-start | bytes 1572864 | tf_op jit(solution)/shard_map/all_to_all | solution.py:320
  10.5 1.4 %collective-permute-start.1 = (bf16[16,128,128]{2,1,0:T(8,128)(2,1)S(1)}, bf16[16,128,128]{2,1,0:T(8,128)(2,1)}, u32[]{:S(2)}, u32[]{:S(2)}) collective-permute-start(bf16[16,128,128]{2,1,0:T(8,128)(2,1)S(1)} %get-tuple-element.7.own_ref), channel_id=1, source_target_pairs={{1,2},{2,1},{3,4},{4,3},{5,6},{6,5},{7,8},{8,7},{9,10},{10,9},{11,... | collective-permute-start | bytes 1572872 | tf_op jit(solution)/shard_map/ppermute | solution.py:313
  11.9 1.2 %collective-permute-start = (bf16[16,128,128]{2,1,0:T(8,128)(2,1)S(1)}, bf16[16,128,128]{2,1,0:T(8,128)(2,1)}, u32[]{:S(2)}, u32[]{:S(2)}) collective-permute-start(bf16[16,128,128]{2,1,0:T(8,128)(2,1)S(1)} %get-tuple-element.7.own_ref), channel_id=1, source_target_pairs={{0,1},{1,0},{2,3},{3,2},{4,5},{5,4},{6,7},{7,6},{8,9},{9,8},{10,11... | collective-permute-start | bytes 1572872 | tf_op jit(solution)/shard_map/ppermute | solution.py:324
  13.1 16.4 %all-to-all-done.recv_ref = bf16[16,4,48,128]{3,2,1,0:T(8,128)(2,1)S(1)} async-done(((bf16[16,4,48,128]{3,2,1,0:T(8,128)(2,1)}), bf16[16,4,48,128]{3,2,1,0:T(8,128)(2,1)S(1)}, u32[]{:S(2)}, u32[]{:S(2)}) %all-to-all-start) | async-done | bytes 786464 | tf_op jit(solution)/shard_map/all_to_all | solution.py:320
  29.5 2.3 %attend.1 = bf16[16,64,128]{2,1,0:T(8,128)(2,1)} custom-call(bf16[16,4,48,128]{3,2,1,0:T(8,128)(2,1)S(1)} %all-to-all-done.recv_ref), custom_call_target="tpu_custom_call" | custom-call | flops 536870912 | bytes 1048576 | tf_op jit(solution)/shard_map/attend/pallas_call | solution.py:125
  31.8 5.4 %all-to-all-start.1 = ((bf16[16,64,128]{2,1,0:T(8,128)(2,1)}), bf16[16,64,128]{2,1,0:T(8,128)(2,1)S(1)}, u32[]{:S(2)}, u32[]{:S(2)}) async-start(bf16[16,64,128]{2,1,0:T(8,128)(2,1)} %attend.1), calls=%async_computation.1 | async-start | bytes 524288 | tf_op jit(solution)/shard_map/all_to_all | solution.py:320
  37.2 0.1 pad_add_fusion.where_ref
  37.3 0.0 collective-permute-done.1.chip_ref
  37.3 0.0 collective-permute-done.core_ref
  37.3 0.0 copy-done
  37.3 0.0 copy-done.1
  37.3 0.0 copy-done.2
  37.3 6.2 %video.1 = bf16[512,16,128]{2,1,0:T(8,128)(2,1)} custom-call(s32[4,4]{1,0:T(4,128)S(1)} %copy-done.1, s32[4]{0:T(128)S(1)} %copy-done.2, s32[3]{0:T(128)S(1)} %pad_add_fusion.where_ref, bf16[512,16,128]{2,1,0:T(8,128)(2,1)S(1)} %copy-done, bf16[16,128,128]{2,1,0:T(8,128)(2,1)S(1)} %get-tuple-element.7.own_ref, ...), custom_call_target="tpu_custom_call" | custom-call | flops 536870912 | bytes 33554432 | tf_op jit(solution)/shard_map/video/pallas_call | solution.py:280
  43.5 1.7 %all-to-all-done.1.by_head_ref = bf16[16,64,128]{2,1,0:T(8,128)(2,1)S(1)} async-done(((bf16[16,64,128]{2,1,0:T(8,128)(2,1)}), bf16[16,64,128]{2,1,0:T(8,128)(2,1)S(1)}, u32[]{:S(2)}, u32[]{:S(2)}) %all-to-all-start.1) | async-done | bytes 262176 | tf_op jit(solution)/shard_map/all_to_all | solution.py:320
  45.2 0.8 %collect.1 = bf16[64,16,128]{2,1,0:T(8,128)(2,1)} custom-call(bf16[16,64,128]{2,1,0:T(8,128)(2,1)S(1)} %all-to-all-done.1.by_head_ref), custom_call_target="tpu_custom_call" | custom-call | tf_op jit(solution)/shard_map/collect/pallas_call | solution.py:199
Async XLA Ops:
  2.7 34.6 %copy-start = (bf16[512,16,128]{2,1,0:T(8,128)(2,1)S(1)}, bf16[512,16,128]{2,1,0:T(8,128)(2,1)}, u32[]{:S(2)}) copy-start(bf16[512,16,128]{2,1,0:T(8,128)(2,1)} %video_ref.1) | copy-start | bytes 6291460
  2.7 34.6 %copy-start.1 = (s32[4,4]{1,0:T(4,128)S(1)}, s32[4,4]{1,0:T(4,128)}, u32[]{:S(2)}) copy-start(s32[4,4]{1,0:T(4,128)} %pairs_ref.1) | copy-start | bytes 196
  2.7 34.6 %copy-start.2 = (s32[4]{0:T(128)S(1)}, s32[4]{0:T(128)}, u32[]{:S(2)}) copy-start(s32[4]{0:T(128)} %counts_ref.1) | copy-start | bytes 52
  2.7 26.8 %all-to-all-start = ((bf16[16,4,48,128]{3,2,1,0:T(8,128)(2,1)}), bf16[16,4,48,128]{3,2,1,0:T(8,128)(2,1)S(1)}, u32[]{:S(2)}, u32[]{:S(2)}) async-start(bf16[16,4,48,128]{3,2,1,0:T(8,128)(2,1)} %get-tuple-element.6), calls=%async_computation | async-start | bytes 1572864 | tf_op jit(solution)/shard_map/all_to_all | solution.py:320
  10.5 26.8 %collective-permute-start.1 = (bf16[16,128,128]{2,1,0:T(8,128)(2,1)S(1)}, bf16[16,128,128]{2,1,0:T(8,128)(2,1)}, u32[]{:S(2)}, u32[]{:S(2)}) collective-permute-start(bf16[16,128,128]{2,1,0:T(8,128)(2,1)S(1)} %get-tuple-element.7.own_ref), channel_id=1, source_target_pairs={{1,2},{2,1},{3,4},{4,3},{5,6},{6,5},{7,8},{8,7},{9,10},{10,9},{11,... | collective-permute-start | bytes 1572872 | tf_op jit(solution)/shard_map/ppermute | solution.py:313
  11.9 25.4 %collective-permute-start = (bf16[16,128,128]{2,1,0:T(8,128)(2,1)S(1)}, bf16[16,128,128]{2,1,0:T(8,128)(2,1)}, u32[]{:S(2)}, u32[]{:S(2)}) collective-permute-start(bf16[16,128,128]{2,1,0:T(8,128)(2,1)S(1)} %get-tuple-element.7.own_ref), channel_id=1, source_target_pairs={{0,1},{1,0},{2,3},{3,2},{4,5},{5,4},{6,7},{7,6},{8,9},{9,8},{10,11... | collective-permute-start | bytes 1572872 | tf_op jit(solution)/shard_map/ppermute | solution.py:324
  31.8 13.5 %all-to-all-start.1 = ((bf16[16,64,128]{2,1,0:T(8,128)(2,1)}), bf16[16,64,128]{2,1,0:T(8,128)(2,1)S(1)}, u32[]{:S(2)}, u32[]{:S(2)}) async-start(bf16[16,64,128]{2,1,0:T(8,128)(2,1)} %attend.1), calls=%async_computation.1 | async-start | bytes 524288 | tf_op jit(solution)/shard_map/all_to_all | solution.py:320

commit v25 on v22

--- a/solution.py
+++ b/solution.py
@@ -312,7 +312,7 @@
 
     chip = lax.ppermute(kv, "seq", chip_pairs)
 
-    order = [(devices // 2 + 1 - p) % devices for p in range(devices)]
+    order = [(devices // 4 - 1 - p) % devices for p in range(devices)]
 
     def exchange(value):
         return lax.all_to_all(

time: 46.3 us -> 45.8 us (0.989)
  starting transfers between devices: 17.2 us -> 13.9 us
  waiting for transfers between devices: 16.2 us -> 19.1 us
    all_to_all x2, waiting for transfers between devices: 16.2 us -> 19.1 us  [exchange(): lax.all_to_all(value, 'seq', split_axis=0, concat_axis=0, tiled=True, axi...]
    all_to_all x2, starting transfers between devices: 13.6 us -> 11.4 us  [exchange(): lax.all_to_all(value, 'seq', split_axis=0, concat_axis=0, tiled=True, axi...]
    ppermute x1, starting transfers between devices: 2.11 us -> 1.01 us  [local(): core = lax.ppermute(kv, 'seq', core_pairs)]
where the time goes in v25:
time: 45.8 us; the launch traced here: 45 us
  waiting for transfers between devices  19.1 us (42%)
  starting transfers between devices  13.9 us (30%)
  Pallas kernels  11.2 us (24%)
  between operations  0.7 us (2%)
    all_to_all x2, waiting for transfers between devices, exchange(): lax.all_to_all(value, 'seq', split_axis=0, concat_axis=0, tiled=True, axi...  19.1 us
    all_to_all x2, starting transfers between devices, exchange(): lax.all_to_all(value, 'seq', split_axis=0, concat_axis=0, tiled=True, axi...  11.4 us
    pallas_call x1, Pallas kernels, video(): pl.pallas_call(functools.partial(video_kernel, scale, 4), in_specs=[in_sm...  6.18 us
    pallas_call x1, Pallas kernels, attend(): pl.pallas_call(functools.partial(attend_kernel, scale), in_specs=[pl.Bloc...  2.28 us
    pallas_call x1, Pallas kernels, arrange(): pl.pallas_call(functools.partial(arrange_kernel, pieces), in_specs=[pl.Bl...  2.03 us
    ppermute x1, starting transfers between devices, local(): chip = lax.ppermute(kv, 'seq', chip_pairs)  1.44 us
    ppermute x1, starting transfers between devices, local(): core = lax.ppermute(kv, 'seq', core_pairs)  1.01 us
  transfers between devices with their start and end apart: 4, of which 2 were waited for; matrix products, arithmetic and copies ran while one was open for 0% of the time, Pallas kernels for 19%

profile of v25, /device:TPU:0, one launch (start us, length us, event | category | flops | bytes accessed | tf_op | source)
XLA Modules:
  0.0 45.0 jit_solution(14638042326259976334)
XLA Ops:
  0.6 2.0 %arrange.1 = (bf16[16,4,48,128]{3,2,1,0:T(8,128)(2,1)}, bf16[16,128,128]{2,1,0:T(8,128)(2,1)S(1)}) custom-call(bf16[64,3,16,128]{3,2,1,0:T(8,128)(2,1)} %qkv_ref.1), custom_call_target="tpu_custom_call" | custom-call | tf_op jit(solution)/shard_map/arrange/pallas_call | solution.py:56
  2.7 0.0 copy-start
  2.7 0.0 copy-start.1
  2.7 0.0 copy-start.2
  2.7 7.8 %all-to-all-start = ((bf16[16,4,48,128]{3,2,1,0:T(8,128)(2,1)}), bf16[16,4,48,128]{3,2,1,0:T(8,128)(2,1)S(1)}, u32[]{:S(2)}, u32[]{:S(2)}) async-start(bf16[16,4,48,128]{3,2,1,0:T(8,128)(2,1)} %get-tuple-element.6), calls=%async_computation | async-start | bytes 1572864 | tf_op jit(solution)/shard_map/all_to_all | solution.py:318
  10.5 1.4 %collective-permute-start.1 = (bf16[16,128,128]{2,1,0:T(8,128)(2,1)S(1)}, bf16[16,128,128]{2,1,0:T(8,128)(2,1)}, u32[]{:S(2)}, u32[]{:S(2)}) collective-permute-start(bf16[16,128,128]{2,1,0:T(8,128)(2,1)S(1)} %get-tuple-element.7.own_ref), channel_id=1, source_target_pairs={{1,2},{2,1},{3,4},{4,3},{5,6},{6,5},{7,8},{8,7},{9,10},{10,9},{11,... | collective-permute-start | bytes 1572872 | tf_op jit(solution)/shard_map/ppermute | solution.py:313
  11.9 1.0 %collective-permute-start = (bf16[16,128,128]{2,1,0:T(8,128)(2,1)S(1)}, bf16[16,128,128]{2,1,0:T(8,128)(2,1)}, u32[]{:S(2)}, u32[]{:S(2)}) collective-permute-start(bf16[16,128,128]{2,1,0:T(8,128)(2,1)S(1)} %get-tuple-element.7.own_ref), channel_id=1, source_target_pairs={{0,1},{1,0},{2,3},{3,2},{4,5},{5,4},{6,7},{7,6},{8,9},{9,8},{10,11... | collective-permute-start | bytes 1572872 | tf_op jit(solution)/shard_map/ppermute | solution.py:322
  12.9 17.3 %all-to-all-done.recv_ref = bf16[16,4,48,128]{3,2,1,0:T(8,128)(2,1)S(1)} async-done(((bf16[16,4,48,128]{3,2,1,0:T(8,128)(2,1)}), bf16[16,4,48,128]{3,2,1,0:T(8,128)(2,1)S(1)}, u32[]{:S(2)}, u32[]{:S(2)}) %all-to-all-start) | async-done | bytes 786464 | tf_op jit(solution)/shard_map/all_to_all | solution.py:318
  30.3 2.3 %attend.1 = bf16[16,64,128]{2,1,0:T(8,128)(2,1)} custom-call(bf16[16,4,48,128]{3,2,1,0:T(8,128)(2,1)S(1)} %all-to-all-done.recv_ref), custom_call_target="tpu_custom_call" | custom-call | flops 536870912 | bytes 1048576 | tf_op jit(solution)/shard_map/attend/pallas_call | solution.py:125
  32.5 3.7 %all-to-all-start.1 = ((bf16[16,64,128]{2,1,0:T(8,128)(2,1)}), bf16[16,64,128]{2,1,0:T(8,128)(2,1)S(1)}, u32[]{:S(2)}, u32[]{:S(2)}) async-start(bf16[16,64,128]{2,1,0:T(8,128)(2,1)} %attend.1), calls=%async_computation.1 | async-start | bytes 524288 | tf_op jit(solution)/shard_map/all_to_all | solution.py:318
  36.2 0.1 pad_add_fusion.where_ref
  36.3 0.0 collective-permute-done.1.chip_ref
  36.3 0.0 collective-permute-done.core_ref
  36.3 0.0 copy-done
  36.3 0.0 copy-done.1
  36.3 0.0 copy-done.2
  36.3 6.2 %video.1 = bf16[512,16,128]{2,1,0:T(8,128)(2,1)} custom-call(s32[4,4]{1,0:T(4,128)S(1)} %copy-done.1, s32[4]{0:T(128)S(1)} %copy-done.2, s32[3]{0:T(128)S(1)} %pad_add_fusion.where_ref, bf16[512,16,128]{2,1,0:T(8,128)(2,1)S(1)} %copy-done, bf16[16,128,128]{2,1,0:T(8,128)(2,1)S(1)} %get-tuple-element.7.own_ref, ...), custom_call_target="tpu_custom_call" | custom-call | flops 536870912 | bytes 33554432 | tf_op jit(solution)/shard_map/video/pallas_call | solution.py:280
  42.5 1.8 %all-to-all-done.1.by_head_ref = bf16[16,64,128]{2,1,0:T(8,128)(2,1)S(1)} async-done(((bf16[16,64,128]{2,1,0:T(8,128)(2,1)}), bf16[16,64,128]{2,1,0:T(8,128)(2,1)S(1)}, u32[]{:S(2)}, u32[]{:S(2)}) %all-to-all-start.1) | async-done | bytes 262176 | tf_op jit(solution)/shard_map/all_to_all | solution.py:318
  44.3 0.8 %collect.1 = bf16[64,16,128]{2,1,0:T(8,128)(2,1)} custom-call(bf16[16,64,128]{2,1,0:T(8,128)(2,1)S(1)} %all-to-all-done.1.by_head_ref), custom_call_target="tpu_custom_call" | custom-call | tf_op jit(solution)/shard_map/collect/pallas_call | solution.py:199
Async XLA Ops:
  2.7 33.6 %copy-start = (bf16[512,16,128]{2,1,0:T(8,128)(2,1)S(1)}, bf16[512,16,128]{2,1,0:T(8,128)(2,1)}, u32[]{:S(2)}) copy-start(bf16[512,16,128]{2,1,0:T(8,128)(2,1)} %video_ref.1) | copy-start | bytes 6291460
  2.7 33.6 %copy-start.1 = (s32[4,4]{1,0:T(4,128)S(1)}, s32[4,4]{1,0:T(4,128)}, u32[]{:S(2)}) copy-start(s32[4,4]{1,0:T(4,128)} %pairs_ref.1) | copy-start | bytes 196
  2.7 33.6 %copy-start.2 = (s32[4]{0:T(128)S(1)}, s32[4]{0:T(128)}, u32[]{:S(2)}) copy-start(s32[4]{0:T(128)} %counts_ref.1) | copy-start | bytes 52
  2.7 27.6 %all-to-all-start = ((bf16[16,4,48,128]{3,2,1,0:T(8,128)(2,1)}), bf16[16,4,48,128]{3,2,1,0:T(8,128)(2,1)S(1)}, u32[]{:S(2)}, u32[]{:S(2)}) async-start(bf16[16,4,48,128]{3,2,1,0:T(8,128)(2,1)} %get-tuple-element.6), calls=%async_computation | async-start | bytes 1572864 | tf_op jit(solution)/shard_map/all_to_all | solution.py:318
  10.5 25.8 %collective-permute-start.1 = (bf16[16,128,128]{2,1,0:T(8,128)(2,1)S(1)}, bf16[16,128,128]{2,1,0:T(8,128)(2,1)}, u32[]{:S(2)}, u32[]{:S(2)}) collective-permute-start(bf16[16,128,128]{2,1,0:T(8,128)(2,1)S(1)} %get-tuple-element.7.own_ref), channel_id=1, source_target_pairs={{1,2},{2,1},{3,4},{4,3},{5,6},{6,5},{7,8},{8,7},{9,10},{10,9},{11,... | collective-permute-start | bytes 1572872 | tf_op jit(solution)/shard_map/ppermute | solution.py:313
  11.9 24.4 %collective-permute-start = (bf16[16,128,128]{2,1,0:T(8,128)(2,1)S(1)}, bf16[16,128,128]{2,1,0:T(8,128)(2,1)}, u32[]{:S(2)}, u32[]{:S(2)}) collective-permute-start(bf16[16,128,128]{2,1,0:T(8,128)(2,1)S(1)} %get-tuple-element.7.own_ref), channel_id=1, source_target_pairs={{0,1},{1,0},{2,3},{3,2},{4,5},{5,4},{6,7},{7,6},{8,9},{9,8},{10,11... | collective-permute-start | bytes 1572872 | tf_op jit(solution)/shard_map/ppermute | solution.py:322
  32.5 11.7 %all-to-all-start.1 = ((bf16[16,64,128]{2,1,0:T(8,128)(2,1)}), bf16[16,64,128]{2,1,0:T(8,128)(2,1)S(1)}, u32[]{:S(2)}, u32[]{:S(2)}) async-start(bf16[16,64,128]{2,1,0:T(8,128)(2,1)} %attend.1), calls=%async_computation.1 | async-start | bytes 524288 | tf_op jit(solution)/shard_map/all_to_all | solution.py:318
